TPU v7x, 32 devices: a whole 2x2x4 slice. The times are simulated.
32 devices in a mesh: wide: 8 (over z, y), narrow: 4 (over x, core).
Axes of the slice: x: 2, y: 2, z: 4, core: 2. Of those that a mesh axis runs over, the one named last changes fastest.
Arguments:
- inputs: bfloat16 [4096, 1024], P(('wide', 'narrow')), may hold values from -6 to 6
- memory: bfloat16 [8192, 1024], P(('wide', 'narrow')), may hold values from -6 to 6
- cotangent: bfloat16 [4096, 1024], P(('wide', 'narrow')), may hold values from -6 to 6
- segments: int32 [4096], P(('wide', 'narrow')), may hold values from 0 to 3, as said below
- memory_segments: int32 [8192], P(('wide', 'narrow')), may hold values from 0 to 3, as said below
- query_self: bfloat16 [1024, 1024], P(('wide', 'narrow')), may hold values from -0.1875 to 0.1875
- key_self: bfloat16 [1024, 1024], P(('wide', 'narrow')), may hold values from -0.1875 to 0.1875
- value_self: bfloat16 [1024, 1024], P(('wide', 'narrow')), may hold values from -0.1875 to 0.1875
- output_self: bfloat16 [1024, 1024], P(('wide', 'narrow')), may hold values from -1 to 1
- query_cross: bfloat16 [1024, 1024], P(('wide', 'narrow')), may hold values from -0.1875 to 0.1875
- key_cross: bfloat16 [1024, 1024], P(('wide', 'narrow')), may hold values from -0.1875 to 0.1875
- value_cross: bfloat16 [1024, 1024], P(('wide', 'narrow')), may hold values from -0.1875 to 0.1875
- output_cross: bfloat16 [1024, 1024], P(('wide', 'narrow')), may hold values from -1 to 1
- self_gain: bfloat16 [1024], P(('wide', 'narrow')), may hold values from 0.099609375 to 1.8984375
- self_shift: bfloat16 [1024], P(('wide', 'narrow')), may hold values from -3 to 3
- cross_gain: bfloat16 [1024], P(('wide', 'narrow')), may hold values from 0.099609375 to 1.8984375
- cross_shift: bfloat16 [1024], P(('wide', 'narrow')), may hold values from -3 to 3
- final_gain: bfloat16 [1024], P(('wide', 'narrow')), may hold values from 0.099609375 to 1.8984375
- final_shift: bfloat16 [1024], P(('wide', 'narrow')), may hold values from -3 to 3
- feed_in: bfloat16 [1024, 4096], P(None, 'wide'), may hold values from -0.1875 to 0.1875
- feed_out: bfloat16 [4096, 1024], P('wide'), may hold values from -0.09375 to 0.09375
- adapter_down: bfloat16 [1024, 512], P(None, 'narrow'), may hold values from -0.1875 to 0.1875
- adapter_up: bfloat16 [512, 1024], P('narrow'), may hold values from -0.0625 to 0.0625
- prefix_embed: bfloat16 [30, 1024], P(None, ('wide', 'narrow')), may hold values from -6 to 6
- prefix_inner: bfloat16 [1024, 512], P(('wide', 'narrow')), may hold values from -0.1875 to 0.1875
- prefix_outer: bfloat16 [512, 2048], P(None, ('wide', 'narrow')), may hold values from -0.375 to 0.375
Outputs:
- output: bfloat16 [4096, 1024], P(('wide', 'narrow'))
- inputs_grad: bfloat16 [4096, 1024], P(('wide', 'narrow'))
- memory_grad: bfloat16 [8192, 1024], P(('wide', 'narrow'))
- query_self_grad: float32 [1024, 1024], P(('wide', 'narrow'))
- key_self_grad: float32 [1024, 1024], P(('wide', 'narrow'))
- value_self_grad: float32 [1024, 1024], P(('wide', 'narrow'))
- output_self_grad: float32 [1024, 1024], P(('wide', 'narrow'))
- query_cross_grad: float32 [1024, 1024], P(('wide', 'narrow'))
- key_cross_grad: float32 [1024, 1024], P(('wide', 'narrow'))
- value_cross_grad: float32 [1024, 1024], P(('wide', 'narrow'))
- output_cross_grad: float32 [1024, 1024], P(('wide', 'narrow'))
- self_gain_grad: float32 [1024], P(('wide', 'narrow'))
- self_shift_grad: float32 [1024], P(('wide', 'narrow'))
- cross_gain_grad: float32 [1024], P(('wide', 'narrow'))
- cross_shift_grad: float32 [1024], P(('wide', 'narrow'))
- final_gain_grad: float32 [1024], P(('wide', 'narrow'))
- final_shift_grad: float32 [1024], P(('wide', 'narrow'))
- feed_in_grad: float32 [1024, 4096], P('narrow', 'wide')
- feed_out_grad: float32 [4096, 1024], P('wide', 'narrow')
- adapter_down_grad: float32 [1024, 512], P('wide', 'narrow')
- adapter_up_grad: float32 [512, 1024], P('narrow', 'wide')
- prefix_embed_grad: float32 [30, 1024], P(None, ('wide', 'narrow'))
- prefix_inner_grad: float32 [1024, 512], P(('wide', 'narrow'))
- prefix_outer_grad: float32 [512, 2048], P(None, ('wide', 'narrow'))
Inputs may be any that keep to these rules, and one draw needn't show every extreme that they name: `segments`: within each sequence's 128 target tokens the ids never fall; the first is 0 and the last is 3. `memory_segments`: within each sequence's 256 encoder tokens the ids never fall, and every id of 0 to 3 names at least one of them.
All inputs are finite; a program needn't handle non-finite values.
Results may differ from a plain program's by a relative error of at most 0.024.
Values may be sent and summed in bfloat16 or wider, within the bound.
A program may use at most 256 MiB of HBM per device.

v0:
```python
from functools import reduce

import jax
import jax.numpy as jnp
from jax import lax
from jax.sharding import PartitionSpec as P

HEADS = 16
HEAD = 64
PREFIX = 30


HIGHEST = lax.Precision.HIGHEST
EPSILON = 1e-05
MASKED = -1000000000.0
ADAPT_SCALE = 4.0


def matmul(left, right):
    return jnp.dot(left, right, preferred_element_type=jnp.float32)


def left_product(left, right):
    return lax.dot_general(
        left, right, (((0,), (0,)), ((), ())), preferred_element_type=jnp.float32
    )


def right_product(left, right):
    return lax.dot_general(
        left, right, (((1,), (1,)), ((), ())), preferred_element_type=jnp.float32
    )


def exact_left(left, right):
    return lax.dot_general(
        left, right, (((0,), (0,)), ((), ())), precision=HIGHEST, preferred_element_type=jnp.float32
    )


def exact_right(left, right):
    return lax.dot_general(
        left, right, (((1,), (1,)), ((), ())), precision=HIGHEST, preferred_element_type=jnp.float32
    )


def norm_forward(values, factor, offset):
    average = jnp.mean(values, axis=-1, keepdims=True)
    center = values - average
    inverse = lax.rsqrt(jnp.mean(center * center, axis=-1, keepdims=True) + EPSILON)
    normed = center * inverse
    return (normed * factor + offset, normed, inverse)


def norm_backward(grad_out, normed, inverse, factor):
    scaled = grad_out * factor
    grad_in = inverse * (
        scaled
        - jnp.mean(scaled, axis=-1, keepdims=True)
        - normed * jnp.mean(scaled * normed, axis=-1, keepdims=True)
    )
    return (grad_in, jnp.sum(grad_out * normed, axis=0), jnp.sum(grad_out, axis=0))


def head_view(rows):
    return rows.reshape(rows.shape[0], HEADS, HEAD)


def scored(queries, key_rows, allowed):
    raw = jnp.einsum(
        "shd,khd->hsk", head_view(queries), head_view(key_rows), preferred_element_type=jnp.float32
    )
    return jnp.where(allowed[None], raw * HEAD ** (-0.5), MASKED)


def attend_forward(queries, parts):
    scores = [scored(queries, member[0], member[2]) for member in parts]
    largest = reduce(jnp.maximum, [jnp.max(matrix, axis=-1, keepdims=True) for matrix in scores])
    total = reduce(
        jnp.add, [jnp.sum(jnp.exp(matrix - largest), axis=-1, keepdims=True) for matrix in scores]
    )
    logsum = largest + jnp.log(total)
    mixed = reduce(
        jnp.add,
        [
            jnp.einsum(
                "hsk,khd->shd",
                jnp.exp(matrix - logsum).astype(jnp.bfloat16),
                head_view(member[1]),
                preferred_element_type=jnp.float32,
            )
            for matrix, member in zip(scores, parts)
        ],
    )
    return (mixed.reshape(queries.shape[0], HEADS * HEAD), logsum)


def attend_backward(queries, parts, logsum, grad_low):
    grad_heads = head_view(grad_low)
    chances = [jnp.exp(scored(queries, member[0], member[2]) - logsum) for member in parts]
    slopes = [
        jnp.einsum(
            "shd,khd->hsk", grad_heads, head_view(member[1]), preferred_element_type=jnp.float32
        )
        for member in parts
    ]
    row_dot = reduce(
        jnp.add,
        [jnp.sum(chance * slope, axis=-1, keepdims=True) for chance, slope in zip(chances, slopes)],
    )
    scale = HEAD ** (-0.5)
    grad_query = jnp.zeros((queries.shape[0], HEADS, HEAD), jnp.float32)
    results = []
    for member, chance, slope in zip(parts, chances, slopes):
        dscore = (chance * (slope - row_dot)).astype(jnp.bfloat16)
        grad_query = grad_query + jnp.einsum(
            "hsk,khd->shd", dscore, head_view(member[0]), preferred_element_type=jnp.float32
        )
        grad_key = (
            jnp.einsum(
                "hsk,shd->khd", dscore, head_view(queries), preferred_element_type=jnp.float32
            )
            * scale
        )
        grad_value = jnp.einsum(
            "hsk,shd->khd",
            chance.astype(jnp.bfloat16),
            grad_heads,
            preferred_element_type=jnp.float32,
        )
        results.append(
            (
                grad_key.reshape(grad_key.shape[0], HEADS * HEAD),
                grad_value.reshape(grad_value.shape[0], HEADS * HEAD),
            )
        )
    return ((grad_query * scale).reshape(queries.shape[0], HEADS * HEAD), results)


def gelu_back(pre_values, grad_values):
    return jax.vjp(lambda inner: jax.nn.gelu(inner, approximate=False), pre_values)[1](grad_values)[
        0
    ]


def body(
    inputs,
    memory,
    cotangent,
    segments,
    memory_segments,
    query_self,
    key_self,
    value_self,
    output_self,
    query_cross,
    key_cross,
    value_cross,
    output_cross,
    self_gain,
    self_shift,
    cross_gain,
    cross_shift,
    final_gain,
    final_shift,
    feed_in,
    feed_out,
    adapter_down,
    adapter_up,
    prefix_embed,
    prefix_inner,
    prefix_outer,
):
    (
        query_one,
        key_one,
        value_one,
        output_one,
        query_two,
        key_two,
        value_two,
        output_two,
        gain_one,
        shift_one,
        gain_two,
        shift_two,
        gain_three,
        shift_three,
        embed_full,
        inner_full,
        outer_full,
    ) = (
        lax.all_gather(query_self, ("wide", "narrow"), axis=0, tiled=True),
        lax.all_gather(key_self, ("wide", "narrow"), axis=0, tiled=True),
        lax.all_gather(value_self, ("wide", "narrow"), axis=0, tiled=True),
        lax.all_gather(output_self, ("wide", "narrow"), axis=0, tiled=True),
        lax.all_gather(query_cross, ("wide", "narrow"), axis=0, tiled=True),
        lax.all_gather(key_cross, ("wide", "narrow"), axis=0, tiled=True),
        lax.all_gather(value_cross, ("wide", "narrow"), axis=0, tiled=True),
        lax.all_gather(output_cross, ("wide", "narrow"), axis=0, tiled=True),
        lax.all_gather(self_gain, ("wide", "narrow"), axis=0, tiled=True),
        lax.all_gather(self_shift, ("wide", "narrow"), axis=0, tiled=True),
        lax.all_gather(cross_gain, ("wide", "narrow"), axis=0, tiled=True),
        lax.all_gather(cross_shift, ("wide", "narrow"), axis=0, tiled=True),
        lax.all_gather(final_gain, ("wide", "narrow"), axis=0, tiled=True),
        lax.all_gather(final_shift, ("wide", "narrow"), axis=0, tiled=True),
        lax.all_gather(prefix_embed, ("wide", "narrow"), axis=1, tiled=True),
        lax.all_gather(prefix_inner, ("wide", "narrow"), axis=0, tiled=True),
        lax.all_gather(prefix_outer, ("wide", "narrow"), axis=1, tiled=True),
    )
    factor_one = gain_one.astype(jnp.float32)
    factor_two = gain_two.astype(jnp.float32)
    factor_three = gain_three.astype(jnp.float32)
    length = inputs.shape[0]
    width = inputs.shape[1]
    places = jnp.arange(length)
    causal = places[:, None] >= places[None, :]
    local_mask = (segments[:, None] == segments[None, :]) & causal
    prefix_mask = jnp.ones((length, PREFIX), jnp.bool_)
    cross_mask = segments[:, None] == memory_segments[None, :]
    tangent = jnp.tanh(matmul(embed_full, inner_full))
    tangent_low = tangent.astype(jnp.bfloat16)
    prefix_rows = matmul(tangent_low, outer_full).astype(jnp.bfloat16)
    prefix_keys = prefix_rows[:, :width]
    prefix_values = prefix_rows[:, width:]
    queries = matmul(inputs, query_one).astype(jnp.bfloat16)
    key_rows = matmul(inputs, key_one).astype(jnp.bfloat16)
    value_rows = matmul(inputs, value_one).astype(jnp.bfloat16)
    self_parts = ((prefix_keys, prefix_values, prefix_mask), (key_rows, value_rows, local_mask))
    attended, self_logsum = attend_forward(queries, self_parts)
    attended_low = attended.astype(jnp.bfloat16)
    first, normed_one, inverse_one = norm_forward(
        inputs.astype(jnp.float32) + matmul(attended_low, output_one),
        factor_one,
        shift_one.astype(jnp.float32),
    )
    first_low = first.astype(jnp.bfloat16)
    cross_queries = matmul(first_low, query_two).astype(jnp.bfloat16)
    cross_keys = matmul(memory, key_two).astype(jnp.bfloat16)
    cross_values = matmul(memory, value_two).astype(jnp.bfloat16)
    cross_parts = ((cross_keys, cross_values, cross_mask),)
    crossed, cross_logsum = attend_forward(cross_queries, cross_parts)
    crossed_low = crossed.astype(jnp.bfloat16)
    second, normed_two, inverse_two = norm_forward(
        first + matmul(crossed_low, output_two), factor_two, shift_two.astype(jnp.float32)
    )
    second_low = second.astype(jnp.bfloat16)
    feed_rows = lax.all_gather(second_low, "wide", axis=0, tiled=True)
    hidden_pre = matmul(feed_rows, feed_in)
    hidden_low = jax.nn.gelu(hidden_pre, approximate=False).astype(jnp.bfloat16)
    feed_sum = lax.psum_scatter(
        matmul(hidden_low, feed_out), "wide", scatter_dimension=0, tiled=True
    )
    adapt_rows = lax.all_gather(second_low, "narrow", axis=0, tiled=True)
    bottle_pre = matmul(adapt_rows, adapter_down)
    bottle_low = jax.nn.gelu(bottle_pre, approximate=False).astype(jnp.bfloat16)
    adapt_sum = lax.psum_scatter(
        matmul(bottle_low, adapter_up).astype(jnp.bfloat16),
        "narrow",
        scatter_dimension=0,
        tiled=True,
    ).astype(jnp.float32)
    branch = feed_sum + ADAPT_SCALE * adapt_sum
    result, normed_three, inverse_three = norm_forward(
        second + branch, factor_three, shift_three.astype(jnp.float32)
    )
    grad_branch, gain_three_grad, shift_three_grad = norm_backward(
        cotangent.astype(jnp.float32), normed_three, inverse_three, factor_three
    )
    branch_low = grad_branch.astype(jnp.bfloat16)
    branch_rows = lax.all_gather(branch_low, "wide", axis=0, tiled=True)
    grad_hidden = right_product(branch_rows, feed_out)
    grad_pre = gelu_back(hidden_pre, grad_hidden).astype(jnp.bfloat16)
    grad_out_part = left_product(hidden_low, branch_rows)
    grad_in_part = left_product(feed_rows, grad_pre)
    grad_feed = lax.psum_scatter(
        right_product(grad_pre, feed_in), "wide", scatter_dimension=0, tiled=True
    )
    feed_in_total, feed_out_total = (
        lax.psum_scatter(
            grad_in_part.astype(jnp.bfloat16), "narrow", scatter_dimension=0, tiled=True
        ).astype(jnp.float32),
        lax.psum_scatter(
            grad_out_part.astype(jnp.bfloat16), "narrow", scatter_dimension=1, tiled=True
        ).astype(jnp.float32),
    )
    branch_narrow = lax.all_gather(branch_low, "narrow", axis=0, tiled=True)
    grad_bottle = ADAPT_SCALE * right_product(branch_narrow, adapter_up)
    grad_bottle_pre = gelu_back(bottle_pre, grad_bottle).astype(jnp.bfloat16)
    grad_up_part = ADAPT_SCALE * left_product(bottle_low, branch_narrow)
    grad_down_part = left_product(adapt_rows, grad_bottle_pre)
    grad_adapt = lax.psum_scatter(
        right_product(grad_bottle_pre, adapter_down).astype(jnp.bfloat16),
        "narrow",
        scatter_dimension=0,
        tiled=True,
    ).astype(jnp.float32)
    down_total, up_total = (
        lax.psum_scatter(grad_down_part, "wide", scatter_dimension=0, tiled=True),
        lax.psum_scatter(grad_up_part, "wide", scatter_dimension=1, tiled=True),
    )
    grad_second = grad_branch + grad_feed + grad_adapt
    grad_mid, gain_two_grad, shift_two_grad = norm_backward(
        grad_second, normed_two, inverse_two, factor_two
    )
    mid_low = grad_mid.astype(jnp.bfloat16)
    output_two_grad = left_product(crossed_low, mid_low)
    crossed_grad = right_product(mid_low, output_two).astype(jnp.bfloat16)
    cross_query_grad, cross_results = attend_backward(
        cross_queries, cross_parts, cross_logsum, crossed_grad
    )
    cross_query_low = cross_query_grad.astype(jnp.bfloat16)
    cross_key_low = cross_results[0][0].astype(jnp.bfloat16)
    cross_value_low = cross_results[0][1].astype(jnp.bfloat16)
    query_two_grad = left_product(first_low, cross_query_low)
    key_two_grad = left_product(memory, cross_key_low)
    value_two_grad = left_product(memory, cross_value_low)
    memory_grad = (
        right_product(cross_key_low, key_two) + right_product(cross_value_low, value_two)
    ).astype(jnp.bfloat16)
    grad_first = grad_mid + right_product(cross_query_low, query_two)
    grad_start, gain_one_grad, shift_one_grad = norm_backward(
        grad_first, normed_one, inverse_one, factor_one
    )
    start_low = grad_start.astype(jnp.bfloat16)
    output_one_grad = left_product(attended_low, start_low)
    attended_grad = right_product(start_low, output_one).astype(jnp.bfloat16)
    self_query_grad, self_results = attend_backward(queries, self_parts, self_logsum, attended_grad)
    self_query_low = self_query_grad.astype(jnp.bfloat16)
    self_key_low = self_results[1][0].astype(jnp.bfloat16)
    self_value_low = self_results[1][1].astype(jnp.bfloat16)
    query_one_grad = left_product(inputs, self_query_low)
    key_one_grad = left_product(inputs, self_key_low)
    value_one_grad = left_product(inputs, self_value_low)
    inputs_grad = (
        grad_start
        + right_product(self_query_low, query_one)
        + right_product(self_key_low, key_one)
        + right_product(self_value_low, value_one)
    ).astype(jnp.bfloat16)
    prefix_grad = jnp.concatenate([self_results[0][0], self_results[0][1]], axis=1)
    outer_grad = exact_left(tangent_low.astype(jnp.float32), prefix_grad)
    tangent_grad = exact_right(prefix_grad, outer_full.astype(jnp.float32)) * (
        1.0 - tangent * tangent
    )
    inner_grad = exact_left(embed_full.astype(jnp.float32), tangent_grad)
    embed_grad = exact_right(tangent_grad, inner_full.astype(jnp.float32))
    (
        query_one_sum,
        key_one_sum,
        value_one_sum,
        output_one_sum,
        query_two_sum,
        key_two_sum,
        value_two_sum,
        output_two_sum,
        gain_one_sum,
        shift_one_sum,
        gain_two_sum,
        shift_two_sum,
        gain_three_sum,
        shift_three_sum,
        embed_sum,
        inner_sum,
        outer_sum,
    ) = (
        lax.psum_scatter(query_one_grad, ("wide", "narrow"), scatter_dimension=0, tiled=True),
        lax.psum_scatter(key_one_grad, ("wide", "narrow"), scatter_dimension=0, tiled=True),
        lax.psum_scatter(value_one_grad, ("wide", "narrow"), scatter_dimension=0, tiled=True),
        lax.psum_scatter(output_one_grad, ("wide", "narrow"), scatter_dimension=0, tiled=True),
        lax.psum_scatter(query_two_grad, ("wide", "narrow"), scatter_dimension=0, tiled=True),
        lax.psum_scatter(key_two_grad, ("wide", "narrow"), scatter_dimension=0, tiled=True),
        lax.psum_scatter(value_two_grad, ("wide", "narrow"), scatter_dimension=0, tiled=True),
        lax.psum_scatter(output_two_grad, ("wide", "narrow"), scatter_dimension=0, tiled=True),
        lax.psum_scatter(gain_one_grad, ("wide", "narrow"), scatter_dimension=0, tiled=True),
        lax.psum_scatter(shift_one_grad, ("wide", "narrow"), scatter_dimension=0, tiled=True),
        lax.psum_scatter(gain_two_grad, ("wide", "narrow"), scatter_dimension=0, tiled=True),
        lax.psum_scatter(shift_two_grad, ("wide", "narrow"), scatter_dimension=0, tiled=True),
        lax.psum_scatter(gain_three_grad, ("wide", "narrow"), scatter_dimension=0, tiled=True),
        lax.psum_scatter(shift_three_grad, ("wide", "narrow"), scatter_dimension=0, tiled=True),
        lax.psum_scatter(embed_grad, ("wide", "narrow"), scatter_dimension=1, tiled=True),
        lax.psum_scatter(inner_grad, ("wide", "narrow"), scatter_dimension=0, tiled=True),
        lax.psum_scatter(outer_grad, ("wide", "narrow"), scatter_dimension=1, tiled=True),
    )
    return (
        result.astype(jnp.bfloat16),
        inputs_grad,
        memory_grad,
        query_one_sum,
        key_one_sum,
        value_one_sum,
        output_one_sum,
        query_two_sum,
        key_two_sum,
        value_two_sum,
        output_two_sum,
        gain_one_sum,
        shift_one_sum,
        gain_two_sum,
        shift_two_sum,
        gain_three_sum,
        shift_three_sum,
        feed_in_total,
        feed_out_total,
        down_total,
        up_total,
        embed_sum,
        inner_sum,
        outer_sum,
    )


def solution(mesh):
    return jax.shard_map(
        body,
        mesh=mesh,
        in_specs=(
            P(("wide", "narrow"), None),
            P(("wide", "narrow"), None),
            P(("wide", "narrow"), None),
            P(("wide", "narrow")),
            P(("wide", "narrow")),
            P(("wide", "narrow"), None),
            P(("wide", "narrow"), None),
            P(("wide", "narrow"), None),
            P(("wide", "narrow"), None),
            P(("wide", "narrow"), None),
            P(("wide", "narrow"), None),
            P(("wide", "narrow"), None),
            P(("wide", "narrow"), None),
            P(("wide", "narrow")),
            P(("wide", "narrow")),
            P(("wide", "narrow")),
            P(("wide", "narrow")),
            P(("wide", "narrow")),
            P(("wide", "narrow")),
            P(None, "wide"),
            P("wide", None),
            P(None, "narrow"),
            P("narrow", None),
            P(None, ("wide", "narrow")),
            P(("wide", "narrow"), None),
            P(None, ("wide", "narrow")),
        ),
        out_specs=(
            P(("wide", "narrow"), None),
            P(("wide", "narrow"), None),
            P(("wide", "narrow"), None),
            P(("wide", "narrow"), None),
            P(("wide", "narrow"), None),
            P(("wide", "narrow"), None),
            P(("wide", "narrow"), None),
            P(("wide", "narrow"), None),
            P(("wide", "narrow"), None),
            P(("wide", "narrow"), None),
            P(("wide", "narrow"), None),
            P(("wide", "narrow")),
            P(("wide", "narrow")),
            P(("wide", "narrow")),
            P(("wide", "narrow")),
            P(("wide", "narrow")),
            P(("wide", "narrow")),
            P("narrow", "wide"),
            P("wide", "narrow"),
            P("wide", "narrow"),
            P("narrow", "wide"),
            P(None, ("wide", "narrow")),
            P(("wide", "narrow"), None),
            P(None, ("wide", "narrow")),
        ),
        check_vma=False,
    )
```

profile of v0, /device:TPU:0, one launch (start us, length us, event | category | flops | bytes accessed | tf_op | source)
XLA Modules:
  0.0 2692.6 jit_solution(15564105121936889642)
XLA Ops:
  128.3 55.6 %all-gather.19.cloned.1.call-done = bf16[1024,1024]{1,0:T(8,128)(2,1)} async-done(((bf16[32,1024]{1,0:T(8,128)(2,1)}), bf16[1024,1024]{1,0:T(8,128)(2,1)}) %all-gather.19.cloned.1.call-update) | async-done | bytes 2097168 | tf_op jit(solution)/shard_map/all_gather | solution.py:193
  186.2 55.7 %all-gather.21.cloned.1.call-done = bf16[1024,1024]{1,0:T(8,128)(2,1)} async-done(((bf16[32,1024]{1,0:T(8,128)(2,1)}), bf16[1024,1024]{1,0:T(8,128)(2,1)}) %all-gather.21.cloned.1.call-update) | async-done | bytes 2097168 | tf_op jit(solution)/shard_map/all_gather | solution.py:194
  244.1 55.7 %all-gather.23.cloned.1.call-done = bf16[1024,1024]{1,0:T(8,128)(2,1)} async-done(((bf16[32,1024]{1,0:T(8,128)(2,1)}), bf16[1024,1024]{1,0:T(8,128)(2,1)}) %all-gather.23.cloned.1.call-update) | async-done | bytes 2097168 | tf_op jit(solution)/shard_map/all_gather | solution.py:195
  304.2 53.6 %all-gather.25.cloned.1.call-done = bf16[1024,1024]{1,0:T(8,128)(2,1)} async-done(((bf16[32,1024]{1,0:T(8,128)(2,1)}), bf16[1024,1024]{1,0:T(8,128)(2,1)}) %all-gather.25.cloned.1.call-update) | async-done | bytes 2097168 | tf_op jit(solution)/shard_map/all_gather | solution.py:196
  360.3 55.7 %all-gather.29.cloned.1.call-done = bf16[1024,1024]{1,0:T(8,128)(2,1)} async-done(((bf16[32,1024]{1,0:T(8,128)(2,1)}), bf16[1024,1024]{1,0:T(8,128)(2,1)}) %all-gather.29.cloned.1.call-update) | async-done | bytes 2097168 | tf_op jit(solution)/shard_map/all_gather | solution.py:197
  418.9 55.2 %all-gather.31.cloned.1.call-done = bf16[1024,1024]{1,0:T(8,128)(2,1)} async-done(((bf16[32,1024]{1,0:T(8,128)(2,1)}), bf16[1024,1024]{1,0:T(8,128)(2,1)}) %all-gather.31.cloned.1.call-update) | async-done | bytes 2097168 | tf_op jit(solution)/shard_map/all_gather | solution.py:198
  477.4 54.8 %all-gather.27.cloned.1.call-done = bf16[1024,1024]{1,0:T(8,128)(2,1)} async-done(((bf16[32,1024]{1,0:T(8,128)(2,1)}), bf16[1024,1024]{1,0:T(8,128)(2,1)}) %all-gather.27.cloned.1.call-update) | async-done | bytes 2097168 | tf_op jit(solution)/shard_map/all_gather | solution.py:199
  539.2 50.9 %all-gather.33.cloned.1.call-done = bf16[1024,1024]{1,0:T(8,128)(2,1)} async-done(((bf16[32,1024]{1,0:T(8,128)(2,1)}), bf16[1024,1024]{1,0:T(8,128)(2,1)}) %all-gather.33.cloned.1.call-update) | async-done | bytes 2097168 | tf_op jit(solution)/shard_map/all_gather | solution.py:200
  615.8 46.5 %all-gather.35.cloned.1.call-done = bf16[1024,1024]{1,0:T(8,128)(2,1)} async-done(((bf16[128,1024]{1,0:T(8,128)(2,1)}), bf16[1024,1024]{1,0:T(8,128)(2,1)}) %all-gather.35.cloned.1.call-update) | async-done | bytes 2097168 | tf_op jit(solution)/shard_map/all_gather | solution.py:248
  688.3 92.0 %reduce-scatter.34.cloned.1.call-done = f32[128,1024]{1,0:T(8,128)} async-done(((f32[1024,1024]{1,0:T(8,128)}), f32[128,1024]{1,0:T(8,128)}) %reduce-scatter.34.cloned.1.call-update) | async-done | bytes 524304 | tf_op jit(solution)/shard_map/reduce_scatter | solution.py:251
  805.6 47.4 %all-gather.39.cloned.1.call-done = bf16[1024,1024]{1,0:T(8,128)(2,1)} async-done(((bf16[128,1024]{1,0:T(8,128)(2,1)}), bf16[1024,1024]{1,0:T(8,128)(2,1)}) %all-gather.39.cloned.1.call-update) | async-done | bytes 2097168 | tf_op jit(solution)/shard_map/all_gather | solution.py:271
  878.7 92.0 %reduce-scatter.38.cloned.1.call-done = f32[128,1024]{1,0:T(8,128)} async-done(((f32[1024,1024]{1,0:T(8,128)}), f32[128,1024]{1,0:T(8,128)}) %reduce-scatter.38.cloned.1.call-update) | async-done | bytes 524304 | tf_op jit(solution)/shard_map/reduce_scatter | solution.py:276
  1163.2 61.3 %reduce-scatter.54.cloned.1.call-done = f32[128,128]{1,0:T(8,128)} async-done(((f32[128,1024]{1,0:T(8,128)}), f32[128,128]{1,0:T(8,128)}) %reduce-scatter.54.cloned.1.call-update) | async-done | bytes 65552 | tf_op jit(solution)/shard_map/reduce_scatter | solution.py:300
  1224.6 64.8 %reduce-scatter.52.cloned.1.call-done = f32[128,128]{1,0:T(8,128)} async-done(((f32[1024,128]{1,0:T(8,128)}), f32[128,128]{1,0:T(8,128)}) %reduce-scatter.52.cloned.1.call-update) | async-done | bytes 65552 | tf_op jit(solution)/shard_map/reduce_scatter | solution.py:299
  1289.4 138.6 %reduce-scatter.70.cloned.1.call-done = f32[32,512]{1,0:T(8,128)} async-done(((f32[1024,512]{1,0:T(8,128)}), f32[32,512]{1,0:T(8,128)}) %reduce-scatter.70.cloned.1.call-update) | async-done | bytes 65552
  1428.0 139.7 %reduce-scatter.56.cloned.1.call-done = f32[512,64]{0,1:T(8,128)} async-done(((f32[512,2048]{0,1:T(8,128)}), f32[512,64]{0,1:T(8,128)}) %reduce-scatter.56.cloned.1.call-update) | async-done | bytes 131088 | tf_op jit(solution)/shard_map/reduce_scatter | solution.py:383
  1567.6 139.5 %reduce-scatter.44.cloned.1.call-done = f32[32,1024]{1,0:T(8,128)} async-done(((f32[1024,1024]{1,0:T(8,128)}), f32[32,1024]{1,0:T(8,128)}) %reduce-scatter.44.cloned.1.call-update) | async-done | bytes 131088 | tf_op jit(solution)/shard_map/reduce_scatter | solution.py:371
  1707.2 139.5 %reduce-scatter.66.cloned.1.call-done = f32[32,1024]{1,0:T(8,128)} async-done(((f32[1024,1024]{1,0:T(8,128)}), f32[32,1024]{1,0:T(8,128)}) %reduce-scatter.66.cloned.1.call-update) | async-done | bytes 131088
  1846.6 139.8 %reduce-scatter.64.cloned.1.call-done = f32[32,1024]{1,0:T(8,128)} async-done(((f32[1024,1024]{1,0:T(8,128)}), f32[32,1024]{1,0:T(8,128)}) %reduce-scatter.64.cloned.1.call-update) | async-done | bytes 131088
  1986.4 139.8 %reduce-scatter.62.cloned.1.call-done = f32[32,1024]{1,0:T(8,128)} async-done(((f32[1024,1024]{1,0:T(8,128)}), f32[32,1024]{1,0:T(8,128)}) %reduce-scatter.62.cloned.1.call-update) | async-done | bytes 131088
  2126.2 139.8 %reduce-scatter.58.cloned.1.call-done = f32[32,1024]{1,0:T(8,128)} async-done(((f32[1024,1024]{1,0:T(8,128)}), f32[32,1024]{1,0:T(8,128)}) %reduce-scatter.58.cloned.1.call-update) | async-done | bytes 131088
  2266.0 139.9 %reduce-scatter.60.cloned.1.call-done = f32[32,1024]{1,0:T(8,128)} async-done(((f32[1024,1024]{1,0:T(8,128)}), f32[32,1024]{1,0:T(8,128)}) %reduce-scatter.60.cloned.1.call-update) | async-done | bytes 131088
  2405.8 139.9 %reduce-scatter.42.cloned.1.call-done = f32[32,1024]{1,0:T(8,128)} async-done(((f32[1024,1024]{1,0:T(8,128)}), f32[32,1024]{1,0:T(8,128)}) %reduce-scatter.42.cloned.1.call-update) | async-done | bytes 131088 | tf_op jit(solution)/shard_map/reduce_scatter | solution.py:370
  2545.7 139.6 %reduce-scatter.46.cloned.1.call-done = f32[32,1024]{1,0:T(8,128)} async-done(((f32[1024,1024]{1,0:T(8,128)}), f32[32,1024]{1,0:T(8,128)}) %reduce-scatter.46.cloned.1.call-update) | async-done | bytes 131088 | tf_op jit(solution)/shard_map/reduce_scatter | solution.py:374
  (410 shorter events, 439.1 us)
Async XLA Ops:
  8.7 175.3 %all-gather.19.cloned.1.call-start = ((), (), s32[]{:S(2)}) async-start(), calls=%async_computation.21 | async-start | bytes 2162688 | tf_op jit(solution)/shard_map/all_gather | solution.py:193
  9.4 232.5 %all-gather.21.cloned.1.call-start = ((), (), s32[]{:S(2)}) async-start(), calls=%async_computation.22 | async-start | bytes 2162688 | tf_op jit(solution)/shard_map/all_gather | solution.py:194
  10.0 289.9 %all-gather.23.cloned.1.call-start = ((), (), s32[]{:S(2)}) async-start(), calls=%async_computation.23 | async-start | bytes 2162688 | tf_op jit(solution)/shard_map/all_gather | solution.py:195
  10.6 347.3 %all-gather.25.cloned.1.call-start = ((), (), s32[]{:S(2)}) async-start(), calls=%async_computation.24 | async-start | bytes 2162688 | tf_op jit(solution)/shard_map/all_gather | solution.py:196
  11.2 404.8 %all-gather.29.cloned.1.call-start = ((), (), s32[]{:S(2)}) async-start(), calls=%async_computation.26 | async-start | bytes 2162688 | tf_op jit(solution)/shard_map/all_gather | solution.py:197
  11.9 462.2 %all-gather.31.cloned.1.call-start = ((), (), s32[]{:S(2)}) async-start(), calls=%async_computation.27 | async-start | bytes 2162688 | tf_op jit(solution)/shard_map/all_gather | solution.py:198
  12.7 519.5 %all-gather.27.cloned.1.call-start = ((), (), s32[]{:S(2)}) async-start(), calls=%async_computation.25 | async-start | bytes 2162688 | tf_op jit(solution)/shard_map/all_gather | solution.py:199
  13.4 576.8 %all-gather.33.cloned.1.call-start = ((), (), s32[]{:S(2)}) async-start(), calls=%async_computation.28 | async-start | bytes 2162688 | tf_op jit(solution)/shard_map/all_gather | solution.py:200
  14.0 596.5 %all-gather.37.cloned.1.call-start = ((), (), s32[]{:S(2)}) async-start(), calls=%async_computation.31 | async-start | bytes 1310720 | tf_op jit(solution)/shard_map/all_gather | solution.py:254
  862.3 224.4 %reduce-scatter.50.cloned.1.call-start = ((), (), s32[]{:S(2)}) async-start(), calls=%async_computation.41 | async-start | bytes 1310720 | tf_op jit(solution)/shard_map/reduce_scatter | solution.py:283
  867.4 221.3 %reduce-scatter.48.cloned.1.call-start = ((), (), s32[]{:S(2)}) async-start(), calls=%async_computation.40 | async-start | bytes 1310720 | tf_op jit(solution)/shard_map/reduce_scatter | solution.py:280
  873.1 288.7 %reduce-scatter.68.cloned.1.call-start = ((), (), s32[]{:S(2)}) async-start(), calls=%async_computation.50 | async-start | bytes 540672
  1007.0 217.6 %reduce-scatter.54.cloned.1.call-start = ((), (), s32[]{:S(2)}) async-start(), calls=%async_computation.43 | async-start | bytes 589824 | tf_op jit(solution)/shard_map/reduce_scatter | solution.py:300
  1010.1 279.2 %reduce-scatter.52.cloned.1.call-start = ((), (), s32[]{:S(2)}) async-start(), calls=%async_computation.42 | async-start | bytes 589824 | tf_op jit(solution)/shard_map/reduce_scatter | solution.py:299
  1012.7 415.3 %reduce-scatter.70.cloned.1.call-start = ((), (), s32[]{:S(2)}) async-start(), calls=%async_computation.51 | async-start | bytes 2162688
  1019.1 548.5 %reduce-scatter.56.cloned.1.call-start = ((), (), s32[]{:S(2)}) async-start(), calls=%async_computation.44 | async-start | bytes 4325376 | tf_op jit(solution)/shard_map/reduce_scatter | solution.py:383
  1024.1 683.1 %reduce-scatter.44.cloned.1.call-start = ((), (), s32[]{:S(2)}) async-start(), calls=%async_computation.38 | async-start | bytes 4325376 | tf_op jit(solution)/shard_map/reduce_scatter | solution.py:371
  1028.3 818.3 %reduce-scatter.66.cloned.1.call-start = ((), (), s32[]{:S(2)}) async-start(), calls=%async_computation.49 | async-start | bytes 4325376
  1038.9 947.5 %reduce-scatter.64.cloned.1.call-start = ((), (), s32[]{:S(2)}) async-start(), calls=%async_computation.48 | async-start | bytes 4325376
  1049.8 1076.5 %reduce-scatter.62.cloned.1.call-start = ((), (), s32[]{:S(2)}) async-start(), calls=%async_computation.47 | async-start | bytes 4325376
  1059.3 1206.7 %reduce-scatter.58.cloned.1.call-start = ((), (), s32[]{:S(2)}) async-start(), calls=%async_computation.45 | async-start | bytes 4325376
  1069.5 1336.3 %reduce-scatter.60.cloned.1.call-start = ((), (), s32[]{:S(2)}) async-start(), calls=%async_computation.46 | async-start | bytes 4325376
  1079.0 1466.7 %reduce-scatter.42.cloned.1.call-start = ((), (), s32[]{:S(2)}) async-start(), calls=%async_computation.37 | async-start | bytes 4325376 | tf_op jit(solution)/shard_map/reduce_scatter | solution.py:370
  1082.8 1602.6 %reduce-scatter.46.cloned.1.call-start = ((), (), s32[]{:S(2)}) async-start(), calls=%async_computation.39 | async-start | bytes 4325376 | tf_op jit(solution)/shard_map/reduce_scatter | solution.py:374
  (103 other events, 6059.7 us)
Sparse Core Ops, SparseCore 0:
  10.9 56.4 all-gather.14
  70.2 55.5 all-gather.16
  128.7 55.2 all-gather.18
  186.7 55.2 all-gather.20
  244.6 55.2 all-gather.22
  302.6 55.2 all-gather.24
  360.7 55.2 all-gather.28
  418.8 55.2 all-gather.30
  534.9 55.2 all-gather.32
  692.2 88.0 reduce-scatter.33
  882.7 88.0 reduce-scatter.37
  1027.6 134.1 reduce-scatter.67
  1166.1 58.3 reduce-scatter.53
  1228.5 60.8 reduce-scatter.51
  1292.2 135.7 reduce-scatter.69
  1430.8 136.7 reduce-scatter.55
  1570.3 136.7 reduce-scatter.43
  1709.8 136.7 reduce-scatter.65
  1849.5 136.8 reduce-scatter.63
  1989.2 136.9 reduce-scatter.61
  2128.9 137.0 reduce-scatter.57
  2268.8 136.9 reduce-scatter.59
  2408.7 137.0 reduce-scatter.41
  2548.4 136.8 reduce-scatter.45
  (9 shorter events, 281.5 us)
where the time goes:
time: 2700 us; the launch traced here: 2690 us
  waiting for transfers between devices  2330 us (86%)
  matrix products  125 us (5%)
  blocking collectives  123 us (5%)
  local copies, waits for them, and re-layouts  74.8 us (3%)
    unnamed x40, waiting for transfers between devices  864 us
    reduce_scatter x1, waiting for transfers between devices, body(): lax.psum_scatter(output_one_grad, ('wide', 'narrow'), scatter_dimension=0...  140 us
    reduce_scatter x1, waiting for transfers between devices, body(): lax.psum_scatter(outer_grad, ('wide', 'narrow'), scatter_dimension=1, til...  140 us
    reduce_scatter x1, waiting for transfers between devices, body(): lax.psum_scatter(output_two_grad, ('wide', 'narrow'), scatter_dimension=0...  140 us
    reduce_scatter x1, waiting for transfers between devices, body(): lax.psum_scatter(query_two_grad, ('wide', 'narrow'), scatter_dimension=0,...  140 us
    reduce_scatter x1, waiting for transfers between devices, body(): lax.psum_scatter(matmul(hidden_low, feed_out), 'wide', scatter_dimension=...  92 us
    reduce_scatter x1, waiting for transfers between devices, body(): lax.psum_scatter(right_product(grad_pre, feed_in), 'wide', scatter_dimens...  92 us
    unnamed x2, blocking collectives  78.4 us
  transfers between devices with their start and end apart: 33, of which 30 were waited for; matrix products, arithmetic and copies ran while one was open for 7% of the time, Pallas kernels for 0%

commit v1 on v0

--- a/solution.py
+++ b/solution.py
@@ -1,9 +1,18 @@
+import functools
 from functools import reduce
 
 import jax
 import jax.numpy as jnp
 from jax import lax
+from jax.experimental import pallas as pl
+from jax.experimental.pallas import tpu as pltpu
 from jax.sharding import PartitionSpec as P
+
+MESH = pl.DeviceIdType.MESH
+bf16, f32 = jnp.bfloat16, jnp.float32
+WIDE, NARROW = "wide", "narrow"
+BOTH = (WIDE, NARROW)
+
 
 HEADS = 16
 HEAD = 64
@@ -143,7 +152,7 @@
     ]
 
 
-def body(
+def plain_body(
     inputs,
     memory,
     cotangent,
@@ -190,23 +199,23 @@
         inner_full,
         outer_full,
     ) = (
-        lax.all_gather(query_self, ("wide", "narrow"), axis=0, tiled=True),
-        lax.all_gather(key_self, ("wide", "narrow"), axis=0, tiled=True),
-        lax.all_gather(value_self, ("wide", "narrow"), axis=0, tiled=True),
-        lax.all_gather(output_self, ("wide", "narrow"), axis=0, tiled=True),
-        lax.all_gather(query_cross, ("wide", "narrow"), axis=0, tiled=True),
-        lax.all_gather(key_cross, ("wide", "narrow"), axis=0, tiled=True),
-        lax.all_gather(value_cross, ("wide", "narrow"), axis=0, tiled=True),
-        lax.all_gather(output_cross, ("wide", "narrow"), axis=0, tiled=True),
-        lax.all_gather(self_gain, ("wide", "narrow"), axis=0, tiled=True),
-        lax.all_gather(self_shift, ("wide", "narrow"), axis=0, tiled=True),
-        lax.all_gather(cross_gain, ("wide", "narrow"), axis=0, tiled=True),
-        lax.all_gather(cross_shift, ("wide", "narrow"), axis=0, tiled=True),
-        lax.all_gather(final_gain, ("wide", "narrow"), axis=0, tiled=True),
-        lax.all_gather(final_shift, ("wide", "narrow"), axis=0, tiled=True),
-        lax.all_gather(prefix_embed, ("wide", "narrow"), axis=1, tiled=True),
-        lax.all_gather(prefix_inner, ("wide", "narrow"), axis=0, tiled=True),
-        lax.all_gather(prefix_outer, ("wide", "narrow"), axis=1, tiled=True),
+        lax.all_gather(query_self, BOTH, axis=0, tiled=True),
+        lax.all_gather(key_self, BOTH, axis=0, tiled=True),
+        lax.all_gather(value_self, BOTH, axis=0, tiled=True),
+        lax.all_gather(output_self, BOTH, axis=0, tiled=True),
+        lax.all_gather(query_cross, BOTH, axis=0, tiled=True),
+        lax.all_gather(key_cross, BOTH, axis=0, tiled=True),
+        lax.all_gather(value_cross, BOTH, axis=0, tiled=True),
+        lax.all_gather(output_cross, BOTH, axis=0, tiled=True),
+        lax.all_gather(self_gain, BOTH, axis=0, tiled=True),
+        lax.all_gather(self_shift, BOTH, axis=0, tiled=True),
+        lax.all_gather(cross_gain, BOTH, axis=0, tiled=True),
+        lax.all_gather(cross_shift, BOTH, axis=0, tiled=True),
+        lax.all_gather(final_gain, BOTH, axis=0, tiled=True),
+        lax.all_gather(final_shift, BOTH, axis=0, tiled=True),
+        lax.all_gather(prefix_embed, BOTH, axis=1, tiled=True),
+        lax.all_gather(prefix_inner, BOTH, axis=0, tiled=True),
+        lax.all_gather(prefix_outer, BOTH, axis=1, tiled=True),
     )
     factor_one = gain_one.astype(jnp.float32)
     factor_two = gain_two.astype(jnp.float32)
@@ -245,18 +254,18 @@
         first + matmul(crossed_low, output_two), factor_two, shift_two.astype(jnp.float32)
     )
     second_low = second.astype(jnp.bfloat16)
-    feed_rows = lax.all_gather(second_low, "wide", axis=0, tiled=True)
+    feed_rows = lax.all_gather(second_low, WIDE, axis=0, tiled=True)
     hidden_pre = matmul(feed_rows, feed_in)
     hidden_low = jax.nn.gelu(hidden_pre, approximate=False).astype(jnp.bfloat16)
     feed_sum = lax.psum_scatter(
-        matmul(hidden_low, feed_out), "wide", scatter_dimension=0, tiled=True
-    )
-    adapt_rows = lax.all_gather(second_low, "narrow", axis=0, tiled=True)
+        matmul(hidden_low, feed_out), WIDE, scatter_dimension=0, tiled=True
+    )
+    adapt_rows = lax.all_gather(second_low, NARROW, axis=0, tiled=True)
     bottle_pre = matmul(adapt_rows, adapter_down)
     bottle_low = jax.nn.gelu(bottle_pre, approximate=False).astype(jnp.bfloat16)
     adapt_sum = lax.psum_scatter(
         matmul(bottle_low, adapter_up).astype(jnp.bfloat16),
-        "narrow",
+        NARROW,
         scatter_dimension=0,
         tiled=True,
     ).astype(jnp.float32)
@@ -268,36 +277,36 @@
         cotangent.astype(jnp.float32), normed_three, inverse_three, factor_three
     )
     branch_low = grad_branch.astype(jnp.bfloat16)
-    branch_rows = lax.all_gather(branch_low, "wide", axis=0, tiled=True)
+    branch_rows = lax.all_gather(branch_low, WIDE, axis=0, tiled=True)
     grad_hidden = right_product(branch_rows, feed_out)
     grad_pre = gelu_back(hidden_pre, grad_hidden).astype(jnp.bfloat16)
     grad_out_part = left_product(hidden_low, branch_rows)
     grad_in_part = left_product(feed_rows, grad_pre)
     grad_feed = lax.psum_scatter(
-        right_product(grad_pre, feed_in), "wide", scatter_dimension=0, tiled=True
+        right_product(grad_pre, feed_in), WIDE, scatter_dimension=0, tiled=True
     )
     feed_in_total, feed_out_total = (
         lax.psum_scatter(
-            grad_in_part.astype(jnp.bfloat16), "narrow", scatter_dimension=0, tiled=True
+            grad_in_part.astype(jnp.bfloat16), NARROW, scatter_dimension=0, tiled=True
         ).astype(jnp.float32),
         lax.psum_scatter(
-            grad_out_part.astype(jnp.bfloat16), "narrow", scatter_dimension=1, tiled=True
+            grad_out_part.astype(jnp.bfloat16), NARROW, scatter_dimension=1, tiled=True
         ).astype(jnp.float32),
     )
-    branch_narrow = lax.all_gather(branch_low, "narrow", axis=0, tiled=True)
+    branch_narrow = lax.all_gather(branch_low, NARROW, axis=0, tiled=True)
     grad_bottle = ADAPT_SCALE * right_product(branch_narrow, adapter_up)
     grad_bottle_pre = gelu_back(bottle_pre, grad_bottle).astype(jnp.bfloat16)
     grad_up_part = ADAPT_SCALE * left_product(bottle_low, branch_narrow)
     grad_down_part = left_product(adapt_rows, grad_bottle_pre)
     grad_adapt = lax.psum_scatter(
         right_product(grad_bottle_pre, adapter_down).astype(jnp.bfloat16),
-        "narrow",
+        NARROW,
         scatter_dimension=0,
         tiled=True,
     ).astype(jnp.float32)
     down_total, up_total = (
-        lax.psum_scatter(grad_down_part, "wide", scatter_dimension=0, tiled=True),
-        lax.psum_scatter(grad_up_part, "wide", scatter_dimension=1, tiled=True),
+        lax.psum_scatter(grad_down_part, WIDE, scatter_dimension=0, tiled=True),
+        lax.psum_scatter(grad_up_part, WIDE, scatter_dimension=1, tiled=True),
     )
     grad_second = grad_branch + grad_feed + grad_adapt
     grad_mid, gain_two_grad, shift_two_grad = norm_backward(
@@ -364,23 +373,23 @@
         inner_sum,
         outer_sum,
     ) = (
-        lax.psum_scatter(query_one_grad, ("wide", "narrow"), scatter_dimension=0, tiled=True),
-        lax.psum_scatter(key_one_grad, ("wide", "narrow"), scatter_dimension=0, tiled=True),
-        lax.psum_scatter(value_one_grad, ("wide", "narrow"), scatter_dimension=0, tiled=True),
-        lax.psum_scatter(output_one_grad, ("wide", "narrow"), scatter_dimension=0, tiled=True),
-        lax.psum_scatter(query_two_grad, ("wide", "narrow"), scatter_dimension=0, tiled=True),
-        lax.psum_scatter(key_two_grad, ("wide", "narrow"), scatter_dimension=0, tiled=True),
-        lax.psum_scatter(value_two_grad, ("wide", "narrow"), scatter_dimension=0, tiled=True),
-        lax.psum_scatter(output_two_grad, ("wide", "narrow"), scatter_dimension=0, tiled=True),
-        lax.psum_scatter(gain_one_grad, ("wide", "narrow"), scatter_dimension=0, tiled=True),
-        lax.psum_scatter(shift_one_grad, ("wide", "narrow"), scatter_dimension=0, tiled=True),
-        lax.psum_scatter(gain_two_grad, ("wide", "narrow"), scatter_dimension=0, tiled=True),
-        lax.psum_scatter(shift_two_grad, ("wide", "narrow"), scatter_dimension=0, tiled=True),
-        lax.psum_scatter(gain_three_grad, ("wide", "narrow"), scatter_dimension=0, tiled=True),
-        lax.psum_scatter(shift_three_grad, ("wide", "narrow"), scatter_dimension=0, tiled=True),
-        lax.psum_scatter(embed_grad, ("wide", "narrow"), scatter_dimension=1, tiled=True),
-        lax.psum_scatter(inner_grad, ("wide", "narrow"), scatter_dimension=0, tiled=True),
-        lax.psum_scatter(outer_grad, ("wide", "narrow"), scatter_dimension=1, tiled=True),
+        lax.psum_scatter(query_one_grad, BOTH, scatter_dimension=0, tiled=True),
+        lax.psum_scatter(key_one_grad, BOTH, scatter_dimension=0, tiled=True),
+        lax.psum_scatter(value_one_grad, BOTH, scatter_dimension=0, tiled=True),
+        lax.psum_scatter(output_one_grad, BOTH, scatter_dimension=0, tiled=True),
+        lax.psum_scatter(query_two_grad, BOTH, scatter_dimension=0, tiled=True),
+        lax.psum_scatter(key_two_grad, BOTH, scatter_dimension=0, tiled=True),
+        lax.psum_scatter(value_two_grad, BOTH, scatter_dimension=0, tiled=True),
+        lax.psum_scatter(output_two_grad, BOTH, scatter_dimension=0, tiled=True),
+        lax.psum_scatter(gain_one_grad, BOTH, scatter_dimension=0, tiled=True),
+        lax.psum_scatter(shift_one_grad, BOTH, scatter_dimension=0, tiled=True),
+        lax.psum_scatter(gain_two_grad, BOTH, scatter_dimension=0, tiled=True),
+        lax.psum_scatter(shift_two_grad, BOTH, scatter_dimension=0, tiled=True),
+        lax.psum_scatter(gain_three_grad, BOTH, scatter_dimension=0, tiled=True),
+        lax.psum_scatter(shift_three_grad, BOTH, scatter_dimension=0, tiled=True),
+        lax.psum_scatter(embed_grad, BOTH, scatter_dimension=1, tiled=True),
+        lax.psum_scatter(inner_grad, BOTH, scatter_dimension=0, tiled=True),
+        lax.psum_scatter(outer_grad, BOTH, scatter_dimension=1, tiled=True),
     )
     return (
         result.astype(jnp.bfloat16),
@@ -410,63 +419,952 @@
     )
 
 
+def place():
+    w = lax.axis_index(WIDE); n = lax.axis_index(NARROW)
+    return w // 2, w % 2, n // 2, n % 2
+
+def device(a, b, x, c):
+    return (a * 2 + b, x * 2 + c)
+
+def greet(peers):
+    barrier = pltpu.get_barrier_semaphore()
+    for p in peers:
+        pl.semaphore_signal(barrier, inc=1, device_id=p, device_id_type=MESH)
+    pl.semaphore_wait(barrier, len(peers))
+
+def remote(src, dst, send, recv, dev):
+    return pltpu.make_async_remote_copy(src_ref=src, dst_ref=dst, send_sem=send, recv_sem=recv, device_id=dev, device_id_type=MESH)
+
+def gather_kernel(A, r, s_ref, fin, fout, down, up, g_ref, fin2, fout2, down4, up4, f_s, f_r, own_sem, own_s, own_r, z_s, z_r, m_s, m_r, l_s, l_r, d_s, d_r):
+    a, b, x, c = place()
+    core, xp, yp = device(a, b, x, 1 - c), device(a, b, 1 - x, c), device(a, 1 - b, x, c)
+    zp = [device((a + j) % A, b, x, c) for j in range(A)]
+    greet([core, xp, yp] + zp[1:])
+    width = g_ref.shape[2]
+    half = width // 2
+    def row(a_, b_, x_):
+        return pl.multiple_of(((a_ * 2 + b_) * 2 + x_) * 2 * r, 2 * r)
+    mine = row(a, b, x)
+    pairs = s_ref.shape[0] // 2
+    local, cross = [], []
+    for i in range(pairs):
+        k, o = 2 * i + c, 2 * i + 1 - c
+        at = pl.multiple_of(mine + c * r, r)
+        l = pltpu.make_async_copy(s_ref.at[k], g_ref.at[k, pl.ds(at, r)], own_sem.at[i])
+        q = remote(s_ref.at[o], g_ref.at[o, pl.ds(at, r)], own_s.at[i], own_r.at[i], core)
+        q.start(); l.start()
+        local.append(l); cross.append(q)
+    def block(i, h, a_, b_, x_):
+        return g_ref.at[2 * i + c, pl.ds(row(a_, b_, x_), 2 * r), pl.ds(h * half, half)]
+    sent = []
+    def send(i, h, where, sems, idx, dev):
+        ss, rr = sems
+        cp = remote(block(i, h, *where), block(i, h, *where), ss.at[idx], rr.at[idx], dev)
+        cp.start(); sent.append(cp)
+    arr = {}
+    def wait(i, h, where, rr, idx):
+        pltpu.make_async_copy(block(i, h, *where), block(i, h, *where), rr.at[idx]).wait()
+    def first(i):
+        local[i].wait(); cross[i].wait()
+        for h in range(2):
+            send(i, h, (a, b, x), (m_s, m_r), (i * 2 + h) * A, (yp, xp)[h])
+        for h in range(2):
+            send(i, h, (a, b, x), (l_s, l_r), 2 * (i * 2 + h) * A, (xp, yp)[h])
+        for j in range(1, A):
+            for h in range(2):
+                send(i, h, (a, b, x), (z_s, z_r), (i * 2 + h) * A + j, zp[j])
+    def third(i, j):
+        aj = (a + A - j) % A
+        for h in range(2):
+            idx = (i * 2 + h) * A + j
+            other = (aj, 1 - b, x) if h == 0 else (aj, b, 1 - x)
+            wait(i, h, other, m_r, idx)
+            send(i, h, other, (l_s, l_r), 2 * idx + 1, (xp, yp)[h])
+    def middle(i):
+        third(i, 0)
+        for j in range(1, A):
+            aj = (a + A - j) % A
+            for h in range(2):
+                wait(i, h, (aj, b, x), z_r, (i * 2 + h) * A + j)
+                send(i, h, (aj, b, x), (m_s, m_r), (i * 2 + h) * A + j, (yp, xp)[h])
+            for h in range(2):
+                send(i, h, (aj, b, x), (l_s, l_r), 2 * ((i * 2 + h) * A + j), (xp, yp)[h])
+    def last(i):
+        for j in range(1, A):
+            third(i, j)
+    def finish(i):
+        for j in range(A):
+            aj = (a + A - j) % A
+            for h in range(2):
+                idx = (i * 2 + h) * A + j
+                one = (aj, b, 1 - x) if h == 0 else (aj, 1 - b, x)
+                wait(i, h, one, l_r, 2 * idx)
+                wait(i, h, (aj, 1 - b, 1 - x), l_r, 2 * idx + 1)
+        k = 2 * i + c
+        q = remote(g_ref.at[k], g_ref.at[k], d_s.at[i], d_r.at[i], core)
+        q.start(); cross.append(q)
+    za = a + 1 - 2 * (a % 2)
+    zq = device(za, b, x, c)
+    H, AD = fin.shape[1], down.shape[1]
+    D = fin.shape[0]
+    extra = []
+    def put(src, dst, dev):
+        q = remote(src, dst, f_s.at[len(extra)], f_r.at[len(extra)], dev)
+        q.start(); extra.append(q)
+        return q
+    def keep(src, dst):
+        q = pltpu.make_async_copy(src, dst, f_s.at[len(extra)])
+        q.start(); extra.append(None)
+        return q
+    kept = []
+    def feeds():
+        kept.append(keep(fin, fin2.at[:, pl.ds(0, H)]))
+        kept.append(keep(fout, fout2.at[pl.ds(0, H)]))
+        ri, ro = pl.ds(pl.multiple_of(c * (D // 2), D // 2), D // 2), pl.ds(pl.multiple_of(c * (H // 2), H // 2), H // 2)
+        ro2 = pl.ds(pl.multiple_of(H + c * (H // 2), H // 2), H // 2)
+        return ([put(fin.at[ri], fin2.at[ri, pl.ds(H, H)], zq), put(fout.at[ro], fout2.at[ro2], zq)],
+                [(fin2.at[ri, pl.ds(H, H)],) * 2, (fout2.at[ro2],) * 2])
+    def adapter():
+        n = pl.ds(pl.multiple_of((x * 2 + c) * AD, AD), AD)
+        m = pl.ds(pl.multiple_of((2 - 2 * x + c) * AD, AD), AD)
+        kept.append(keep(down, down4.at[:, n]))
+        kept.append(keep(up, up4.at[n]))
+        q = [put(down, down4.at[:, n], xp), put(up, up4.at[n], xp), put(down, down4.at[:, n], core), put(up, up4.at[n], core)]
+        return q[:2], [(down4.at[:, m],) * 2, (up4.at[m],) * 2]
+    def onward(waits, pairs_):
+        for q, (src, dst) in zip(waits, pairs_):
+            q.wait_recv()
+            put(src, dst, core)
+    first(0)
+    for i in range(pairs):
+        if i + 1 < pairs:
+            first(i + 1)
+        if i == 1:
+            ad = adapter()
+        if i == 2:
+            fe = feeds()
+        middle(i)
+        last(i)
+        if i: finish(i - 1)
+    onward(*ad)
+    onward(*fe)
+    finish(pairs - 1)
+    for i in range(pairs):
+        cross[pairs + i].wait()
+    for cp in sent:
+        cp.wait_send()
+    for cp in kept:
+        cp.wait()
+    for cp in extra:
+        if cp is not None:
+            cp.wait_send()
+            if not any(cp is q for q in ad[0] + fe[0]):
+                cp.wait_recv()
+
+def gather(A, shards, fin, fout, down, up):
+    K, r, width = shards.shape
+    pairs = K // 2
+    sem = pltpu.SemaphoreType.DMA
+    n = pairs * 2 * A
+    sds = jax.ShapeDtypeStruct
+    D, H = fin.shape
+    AD = down.shape[1]
+    any_ = pl.BlockSpec(memory_space=pl.ANY)
+    return pl.pallas_call(
+        functools.partial(gather_kernel, A, r),
+        out_shape=(sds((K, A * 8 * r, width), bf16), sds((D, 2 * H), bf16), sds((2 * H, D), bf16), sds((D, 4 * AD), bf16), sds((4 * AD, D), bf16)),
+        in_specs=[any_] * 5, out_specs=(any_,) * 5,
+        scratch_shapes=[sem((16,)), sem((16,)), sem((pairs,)), sem((pairs,)), sem((pairs,)), sem((n,)), sem((n,)), sem((n,)), sem((n,)), sem((2 * n,)), sem((2 * n,)), sem((pairs,)), sem((pairs,))],
+        compiler_params=pltpu.CompilerParams(collective_id=1, has_side_effects=True),
+        name="weights_in")(shards, fin, fout, down, up)
+
+
+def dot_left(l, r):
+    return lax.dot_general(l, r, (((0,), (0,)), ((), ())), preferred_element_type=f32)
+
+class Copies:
+    def __init__(self, send, recv):
+        self.send, self.recv, self.count, self.all = send, recv, 0, []
+    def __call__(self, src, dst, dev):
+        cp = remote(src, dst, self.send.at[self.count], self.recv.at[self.count], dev)
+        self.count += 1
+        cp.start(); self.all.append(cp)
+        return cp
+    def local(self, src, dst):
+        cp = pltpu.make_async_copy(src, dst, self.send.at[self.count])
+        self.count += 1
+        cp.start()
+        return cp
+    def sent(self, some):
+        for cp in some:
+            cp.wait_send()
+            self.all = [o for o in self.all if o is not cp]
+    def close(self):
+        for cp in self.all: cp.wait_send()
+
+def reduce_kernel(A, r, xs, ys, mem, ym, ax, ay, fi, fo, out, aout, fi_out, fo_out,
+                  xb, yb, mb, mby, axb, ayb, pb, apb, fib, fob, r1, r2, r3, ra1, ra2, ra3, rfi, rfo, rzi, rzo, rxi, rxo, ob, aob, fib2, fob2, ssem, rsem):
+    a, b, x, c = place()
+    core, xp, yp = device(a, b, x, 1 - c), device(a, b, 1 - x, c), device(a, 1 - b, x, c)
+    zp = [device((a + j) % A, b, x, c) for j in range(A)]
+    za = a + 1 - 2 * (a % 2)
+    zq = device(za, b, x, c)
+    greet([core, xp, yp] + zp[1:])
+    cp = Copies(ssem, rsem)
+    o = 1 - c
+    T = 128
+    D = pb.shape[-1]; HID = fi.shape[1] // 2
+    st0 = []
+    fcopies = []
+    Q = fi.shape[0] // 4
+    for xx in range(2):
+        dq = pl.ds(pl.multiple_of((xx * 2 + o) * Q, Q), Q)
+        fcopies.append(cp(fi.at[dq, :], rfi.at[xx], core))
+        fcopies.append(cp(fo.at[:, dq], rfo.at[xx], core))
+    for i in range(3):
+        e = [cp(xs.at[2 * i + o], xb.at[i, pl.ds(T, T)], core), cp(ys.at[2 * i + o], yb.at[i, pl.ds(T, T)], core)]
+        l = [cp.local(xs.at[2 * i + c], xb.at[i, pl.ds(0, T)]), cp.local(ys.at[2 * i + c], yb.at[i, pl.ds(0, T)])]
+        st0.append((e, l))
+    M = mem.shape[0]
+    e = [cp(mem, mb.at[pl.ds(M, M)], core), cp(ym.at[o], mby.at[pl.ds(M, M)], core)]
+    l = [cp.local(mem, mb.at[pl.ds(0, M)]), cp.local(ym.at[c], mby.at[pl.ds(0, M)])]
+    st0.append((e, l))
+    e = [cp(ax.at[o], axb.at[pl.ds(T, T)], core), cp(ay.at[o], ayb.at[pl.ds(T, T)], core)]
+    l = [cp.local(ax.at[c], axb.at[pl.ds(0, T)]), cp.local(ay.at[c], ayb.at[pl.ds(0, T)])]
+    st0.append((e, l))
+    def ready(i):
+        for q in st0[i][0]: q.wait_recv()
+        for q in st0[i][1]: q.wait()
+    for q in fcopies: q.wait_recv()
+    for xx in range(2):
+        dq = pl.ds(pl.multiple_of((xx * 2 + c) * Q, Q), Q)
+        def rows_fi(t, _):
+            fib[xx, pl.ds(t * 32, 32), :] = fi[pl.ds(pl.multiple_of((xx * 2 + c) * Q + t * 32, 32), 32), :] + rfi[xx, pl.ds(t * 32, 32), :]
+            return 0
+        lax.fori_loop(0, Q // 32, rows_fi, 0)
+        def rows_fo(t, _):
+            fob[xx, pl.ds(t * 64, 64), :] = fo[pl.ds(t * 64, 64), dq] + rfo[xx, pl.ds(t * 64, 64), :]
+            return 0
+        lax.fori_loop(0, fo.shape[0] // 64, rows_fo, 0)
+    zf = [cp(fib.at[:, :, pl.ds(HID, HID)], rzi, zq), cp(fob.at[:, pl.ds(HID, HID), :], rzo, zq)]
+
+    half = D // 2
+    first, second, third = {}, {}, {}
+    def compute(i):
+        ready(i)
+        for h in range(2):
+            def tile(t, _):
+                cols = pl.ds(pl.multiple_of(h * half + t * 256, 256), 256)
+                if i < 3:
+                    p = dot_left(xb[i], yb[i, :, cols])
+                else:
+                    p = dot_left(mb[...], mby[:, cols])
+                pb[i, :, :, :, :, cols] = p.astype(bf16).reshape(A, 2, 2, 2 * r, 256)
+                return 0
+            lax.fori_loop(0, half // 256, tile, 0)
+            cols = pl.ds(h * half, half)
+            if h == 0:
+                first[i, h] = cp(pb.at[i, :, :, 1 - x, :, cols], r1.at[i, h], xp)
+            else:
+                first[i, h] = cp(pb.at[i, :, 1 - b, :, :, cols], r1.at[i, h], yp)
+    def one(i, h):
+        cols = pl.ds(h * half, half)
+        first[i, h].wait_recv()
+        def add(side):
+            def row(z, _):
+                if h == 0:
+                    pb[i, z, side, x, :, cols] = pb[i, z, side, x, :, cols] + r1[i, h, z, side]
+                else:
+                    pb[i, z, b, side, :, cols] = pb[i, z, b, side, :, cols] + r1[i, h, z, side]
+                return 0
+            lax.fori_loop(0, A, row, 0)
+        add(1 - b if h == 0 else 1 - x)
+        if h == 0:
+            second[i, h] = cp(pb.at[i, :, 1 - b, x, :, cols], r2.at[i, h], yp)
+        else:
+            second[i, h] = cp(pb.at[i, :, b, 1 - x, :, cols], r2.at[i, h], xp)
+        add(b if h == 0 else x)
+    def two(i, h):
+        cols = pl.ds(h * half, half)
+        second[i, h].wait_recv()
+        for j in range(1, A):
+            aj = (a + j) % A
+            pb[i, aj, b, x, :, cols] = pb[i, aj, b, x, :, cols] + r2[i, h, aj]
+            third[i, h, j] = cp(pb.at[i, aj, b, x, :, cols], r3.at[i, h, j - 1], zp[j])
+        pb[i, a, b, x, :, cols] = pb[i, a, b, x, :, cols] + r2[i, h, a]
+    outs = []
+    def three(i, h):
+        cols = pl.ds(h * half, half)
+        for j in range(1, A): third[i, h, j].wait_recv()
+        t = pb[i, a, b, x, :, cols].astype(f32)
+        for j in range(1, A): t = t + r3[i, h, j - 1].astype(f32)
+        ob[i, :, cols] = t
+        if h == 1:
+            outs.append(cp.local(ob.at[i, pl.ds(pl.multiple_of(c * r, r), r)], out.at[2 * i + c]).wait)
+            q = cp(ob.at[i, pl.ds(pl.multiple_of(o * r, r), r)], out.at[2 * i + c], core)
+            outs.append(q.wait_recv)
+    def adapt0():
+        ready(4)
+        for t in range(2):
+            cols = pl.ds(t * 256, 256)
+            apb[t] = dot_left(axb[...], ayb[:, cols]).astype(bf16).reshape(A, 2, D // (2 * A), 256)
+        first["a"] = cp(apb.at[1 - x], ra1, xp)
+    def adapt1():
+        first["a"].wait_recv()
+        def row(z, _):
+            for s in range(2):
+                apb[x, z, s] = apb[x, z, s] + ra1[z, s]
+            return 0
+        lax.fori_loop(0, A, row, 0)
+        second["a"] = cp(apb.at[x, :, 1 - b], ra2, yp)
+    def adapt2():
+        second["a"].wait_recv()
+        for j in range(1, A):
+            aj = (a + j) % A
+            apb[x, aj, b] = apb[x, aj, b] + ra2[aj]
+            third["a", j] = cp(apb.at[x, aj, b], ra3.at[j - 1], zp[j])
+        apb[x, a, b] = apb[x, a, b] + ra2[a]
+    def adapt3():
+        for j in range(1, A): third["a", j].wait_recv()
+        t = apb[x, a, b].astype(f32)
+        for j in range(1, A): t = t + ra3[j - 1].astype(f32)
+        aob[0] = t[:, :128]
+        aob[1] = t[:, 128:]
+        outs.append(cp.local(aob.at[c], aout.at[c]).wait)
+        outs.append(cp(aob.at[o], aout.at[c], core).wait_recv)
+    xf = []
+    def feed1():
+        for q in zf: q.wait_recv()
+        def rows_fi(t, _):
+            for xx in range(2):
+                rows = pl.ds(t * 32, 32)
+                fib[xx, rows, pl.ds(0, HID)] = fib[xx, rows, pl.ds(0, HID)] + rzi[xx, rows, :]
+            return 0
+        lax.fori_loop(0, Q // 32, rows_fi, 0)
+        def rows_fo(t, _):
+            for xx in range(2):
+                rows = pl.ds(t * 64, 64)
+                fob[xx, rows, :] = fob[xx, rows, :] + rzo[xx, rows, :]
+            return 0
+        lax.fori_loop(0, HID // 64, rows_fo, 0)
+        xf.append(cp(fib.at[1 - x, :, pl.ds(0, HID)], rxi, xp))
+        xf.append(cp(fob.at[1 - x, pl.ds(0, HID), :], rxo, xp))
+    def feed2():
+        for q in xf: q.wait_recv()
+        def rows_fi(t, _):
+            rows = pl.ds(t * 32, 32)
+            fib2[rows, :] = fib[x, rows, pl.ds(0, HID)].astype(f32) + rxi[rows, :].astype(f32)
+            return 0
+        lax.fori_loop(0, Q // 32, rows_fi, 0)
+        def rows_fo(t, _):
+            rows = pl.ds(t * 64, 64)
+            fob2[rows, :] = fob[x, rows, :].astype(f32) + rxo[rows, :].astype(f32)
+            return 0
+        lax.fori_loop(0, HID // 64, rows_fo, 0)
+        outs.append(cp.local(fib2, fi_out).wait)
+        outs.append(cp.local(fob2, fo_out).wait)
+    compute(0)
+    compute(1)
+    compute(2)
+    one(0, 0); one(0, 1)
+    compute(3)
+    one(1, 0); one(1, 1)
+    feed1()
+    adapt0()
+    two(0, 0); two(0, 1)
+    one(2, 0); one(2, 1)
+    two(1, 0); two(1, 1)
+    one(3, 0); one(3, 1)
+    two(2, 0); two(2, 1)
+    three(0, 0); three(0, 1)
+    adapt1()
+    two(3, 0); two(3, 1)
+    adapt2()
+    three(1, 0); three(1, 1)
+    feed2()
+    three(2, 0); three(2, 1)
+    adapt3()
+    three(3, 0); three(3, 1)
+    for q in outs: q()
+    cp.close()
+
+def reduce_grads(A, r, xs, ys, mem, ym, ax, ay, fi, fo):
+    D = xs.shape[2]; T = xs.shape[1]; M = mem.shape[0]; Q = fi.shape[0] // 4; H2 = fi.shape[1]; H = H2 // 2
+    v = lambda *s: pltpu.VMEM(s, bf16)
+    vf = lambda *s: pltpu.VMEM(s, f32)
+    any_ = pl.BlockSpec(memory_space=pl.ANY)
+    vm = pl.BlockSpec(memory_space=pltpu.VMEM)
+    half = D // 2
+    sds = jax.ShapeDtypeStruct
+    return pl.pallas_call(
+        functools.partial(reduce_kernel, A, r),
+        out_shape=(sds((8, r, D), f32), sds((2, D // (2 * A), 128), f32), sds((Q, H), f32), sds((H, Q), f32)),
+        in_specs=[vm] * 8, out_specs=(any_,) * 4,
+        scratch_shapes=[v(3, 2 * T, D), v(3, 2 * T, D), v(2 * M, D), v(2 * M, D), v(2 * T, D), v(2 * T, 512),
+            v(4, A, 2, 2, 2 * r, D), v(2, A, 2, D // (2 * A), 256), v(2, Q, H2), v(2, H2, Q),
+            v(4, 2, A, 2, 2 * r, half), v(4, 2, A, 2 * r, half), v(4, 2, A - 1, 2 * r, half),
+            v(A, 2, D // (2 * A), 256), v(A, D // (2 * A), 256), v(A - 1, D // (2 * A), 256),
+            v(2, Q, H2), v(2, H2, Q), v(2, Q, H), v(2, H, Q), v(Q, H), v(H, Q),
+            vf(4, 2 * r, D), vf(2, D // (2 * A), 128), vf(Q, H), vf(H, Q),
+            pltpu.SemaphoreType.DMA((128,)), pltpu.SemaphoreType.DMA((128,))],
+        compiler_params=pltpu.CompilerParams(collective_id=2, has_side_effects=True, vmem_limit_bytes=60 << 20),
+        name="weight_grads")(xs, ys, mem, ym, ax, ay, fi, fo)
+
+
+EPSILON = 1e-05
+ADAPT_SCALE = 4.0
+
+def dot(l, r):
+    return jnp.dot(l, r, preferred_element_type=f32)
+
+def dot_right(l, r):
+    return lax.dot_general(l, r, (((1,), (1,)), ((), ())), preferred_element_type=f32)
+
+def gelu_both(v):
+    phi = 0.5 + 0.5 * lax.erf(v * 0.7071067811865476)
+    return v * phi, phi + v * (0.3989422804014327 * jnp.exp(-0.5 * v * v))
+
+def norm(v):
+    center = v - jnp.mean(v, axis=-1, keepdims=True)
+    inverse = lax.rsqrt(jnp.mean(center * center, axis=-1, keepdims=True) + EPSILON)
+    return center * inverse, inverse
+
+def norm_back(e, n, inverse, factor):
+    s = e * factor
+    return inverse * (s - jnp.mean(s, axis=-1, keepdims=True) - n * jnp.mean(s * n, axis=-1, keepdims=True))
+
+def feed_kernel(A, second, cot, fin, fout, down, up, gain, shift, result, gsec, fi, fo, ay, blow, ngrad,
+                rows, brow, hid, slope, gpre, part, q1, q2, q3, bslope, acc, ssem, rsem):
+    a, b, x, c = place()
+    yp = device(a, 1 - b, x, c)
+    zp = device((a + A // 2) % A, b, x, c)
+    greet([yp, zp])
+    cp = Copies(ssem, rsem)
+    T, D = second.shape
+    NC = 2
+    R = T // NC
+    HID = fin.shape[1]; TW = 256
+
+    def spread(buf):
+        zs, ys = [], []
+        for q in range(NC):
+            s = pl.ds(q * R, R)
+            zs.append(cp(buf.at[0, s], buf.at[2, s], zp))
+            ys.append(cp(buf.at[0, s], buf.at[1, s], yp))
+        def forward():
+            f = []
+            for q in range(NC):
+                s = pl.ds(q * R, R)
+                zs[q].wait_recv()
+                f.append(cp(buf.at[2, s], buf.at[3, s], yp))
+            return f
+        return zs, ys, forward
+
+    p3_sent = []
+    def collect(level):
+        p3, p1 = [], []
+        for q in range(NC):
+            p3.append(cp(part.at[3, pl.ds(q * R, R)], q3.at[level, pl.ds(q * R, R)], yp))
+        for q in range(NC):
+            p1.append(cp(part.at[1, pl.ds(q * R, R)], q1.at[level, pl.ds(q * R, R)], yp))
+        p2 = []
+        for q in range(NC):
+            s = pl.ds(q * R, R)
+            p3[q].wait_recv()
+            part[2, s] = part[2, s] + q3[level, s]
+            p2.append(cp(part.at[2, s], q2.at[level, s], zp))
+        p3_sent.append(p3)
+        return p1, p2
+
+    def gather_up(level, p1, p2):
+        for q in range(NC):
+            s = pl.ds(q * R, R)
+            p1[q].wait_recv(); p2[q].wait_recv()
+            acc[s] = acc[s] + q1[level, s].astype(f32) + q2[level, s].astype(f32)
+        cp.sent(p1 + p2 + p3_sent.pop())
+
+    rows[0] = second[...].astype(bf16)
+    zs, ys, forward = spread(rows)
+    for t in range(2):
+        cols = pl.ds(t * 256, 256)
+        g, s = gelu_both(dot(rows[0], down[:, cols]))
+        ay[1, :, cols] = (ADAPT_SCALE * g.astype(bf16).astype(f32)).astype(bf16)
+        bslope[:, cols] = s
+    def enter(j):
+        def tile(t, _):
+            cols = pl.ds(pl.multiple_of(t * TW, TW), TW)
+            g, s = gelu_both(dot(rows[j], fin[:, cols]))
+            hid[j, :, cols] = g.astype(bf16)
+            slope[j, :, cols] = s
+            return 0
+        lax.fori_loop(0, HID // TW, tile, 0)
+        def tile2(t, _):
+            cols = pl.ds(pl.multiple_of(t * TW, TW), TW)
+            p = dot(hid[j], fout[:, cols])
+            if j == 0:
+                acc[:, cols] = p + dot(ay[1], up[:, cols])
+            else:
+                part[j, :, cols] = p.astype(bf16)
+            return 0
+        lax.fori_loop(0, D // TW, tile2, 0)
+    enter(0)
+    for q in ys: q.wait_recv()
+    fw = forward()
+    enter(1)
+    enter(2)
+    for q in fw: q.wait_recv()
+    enter(3)
+    p1, p2 = collect(0)
+    gather_up(0, p1, p2)
+    n3, inv3 = norm(second[...] + acc[...])
+    fac = gain[...].astype(f32)
+    result[...] = (n3 * fac + shift[...].astype(f32)).astype(bf16)
+    e = cot[...].astype(f32)
+    gb = norm_back(e, n3, inv3, fac)
+    gbl = gb.astype(bf16)
+    brow[0] = gbl
+    zs, ys, forward = spread(brow)
+    blow[...] = gbl
+    acc[...] = gb
+    ngrad[0:1, :] = jnp.sum(e * n3, axis=0, keepdims=True)
+    ngrad[1:2, :] = jnp.sum(e, axis=0, keepdims=True)
+    def adapt_tile(t, _):
+        cols = pl.ds(pl.multiple_of(t * 256, 256), 256)
+        gbot = bslope[:, cols] * (ADAPT_SCALE * dot_right(brow[0], up[cols, :]))
+        ay[0, :, cols] = gbot.astype(bf16)
+        return 0
+    lax.fori_loop(0, down.shape[1] // 256, adapt_tile, 0)
+    def leave(j):
+        def tile(t, _):
+            cols = pl.ds(pl.multiple_of(t * TW, TW), TW)
+            gh = dot_right(brow[j], fout[cols, :])
+            gpre[j, :, cols] = (slope[j, :, cols] * gh).astype(bf16)
+            return 0
+        lax.fori_loop(0, HID // TW, tile, 0)
+        def tile2(t, _):
+            cols = pl.ds(pl.multiple_of(t * TW, TW), TW)
+            p = dot_right(gpre[j], fin[cols, :])
+            if j == 0:
+                acc[:, cols] = acc[:, cols] + p + dot_right(ay[0], down[cols, :])
+            else:
+                part[j, :, cols] = p.astype(bf16)
+            return 0
+        lax.fori_loop(0, D // TW, tile2, 0)
+    leave(0)
+    for q in ys: q.wait_recv()
+    fw = forward()
+    leave(1)
+    leave(2)
+    for q in fw: q.wait_recv()
+    leave(3)
+    p1, p2 = collect(1)
+    def wtile(t, _):
+        cols = pl.ds(pl.multiple_of(t * TW, TW), TW)
+        fi[:, cols] = dot_left(rows[...].reshape(4 * T, D), gpre[:, :, cols].reshape(4 * T, TW)).astype(bf16)
+        fo[:, cols] = dot_left(hid[...].reshape(4 * T, HID), brow[:, :, cols].reshape(4 * T, TW)).astype(bf16)
+        return 0
+    lax.fori_loop(0, HID // TW, wtile, 0)
+    gather_up(1, p1, p2)
+    gsec[...] = acc[...]
+    cp.close()
+
+def feed(A, second, cot, fin, fout, down, up, gain, shift):
+    T, D = second.shape; HID = fin.shape[1]; AD = down.shape[1]
+    v = lambda *s: pltpu.VMEM(s, bf16)
+    vf = lambda *s: pltpu.VMEM(s, f32)
+    vm = pl.BlockSpec(memory_space=pltpu.VMEM)
+    sds = jax.ShapeDtypeStruct
+    return pl.pallas_call(
+        functools.partial(feed_kernel, A),
+        out_shape=(sds((T, D), bf16), sds((T, D), f32), sds((D, HID), bf16), sds((HID, D), bf16), sds((2, T, AD), bf16), sds((T, D), bf16), sds((2, D), f32)),
+        in_specs=[vm] * 8, out_specs=(vm,) * 7,
+        scratch_shapes=[v(4, T, D), v(4, T, D), v(4, T, HID), vf(4, T, HID), v(4, T, HID), v(4, T, D),
+            v(2, T, D), v(2, T, D), v(2, T, D), vf(T, AD), vf(T, D),
+            pltpu.SemaphoreType.DMA((64,)), pltpu.SemaphoreType.DMA((64,))],
+        compiler_params=pltpu.CompilerParams(collective_id=3, has_side_effects=True, vmem_limit_bytes=60 << 20),
+        name="feed_forward")(second, cot, fin, fout, down, up, gain, shift)
+
+
+def all_add(cp, A, peers, buf, got, zbuf, value):
+    a = place()[0]
+    core, xp, yp, zp = peers
+    for k, p in enumerate((core, xp, yp)):
+        buf[k] = value
+        q = cp(buf.at[k], got.at[k], p)
+        q.wait_recv()
+        value = value + got[k]
+    zbuf[a] = value
+    qs = [cp(zbuf.at[a], zbuf.at[a], zp[j]) for j in range(1, A)]
+    for q in qs: q.wait_recv()
+    value = zbuf[0]
+    for k in range(1, A): value = value + zbuf[k]
+    return value
+
+def neighbours(A):
+    a, b, x, c = place()
+    return device(a, b, x, 1 - c), device(a, b, 1 - x, c), device(a, 1 - b, x, c), [device((a + j) % A, b, x, c) for j in range(A)]
+
+def prefix_kernel(A, part, outer2, norms, tangent, prows, nout, buf, got, zbuf, r0, r1, ssem, rsem):
+    a, b, x, c = place()
+    peers = neighbours(A)
+    core, xp, yp, zp = peers
+    greet([core, xp, yp] + zp[1:])
+    cp = Copies(ssem, rsem)
+    G = norms.shape[0]
+    me = ((a * 2 + b) * 2 + x) * 2 + c
+    def nrows(start, count): return nout.at[pl.ds(pl.multiple_of(start * G, G), count * G)]
+    nout[pl.ds(pl.multiple_of(me * G, G), G), :] = norms[...]
+    n0 = cp(nrows(me, 1), nrows(me, 1), core)
+    t = jnp.tanh(all_add(cp, A, peers, buf, got, zbuf, part[...]))
+    tangent[...] = t
+    n0.wait_recv()
+    n1 = cp(nrows(me - c, 2), nrows(me - c, 2), xp)
+    mine = jnp.dot(t.astype(bf16), outer2[...], preferred_element_type=f32).astype(bf16)
+    r0[...] = mine
+    q = cp(r0, r1, core)
+    q.wait_recv()
+    lane = lax.broadcasted_iota(jnp.int32, mine.shape, 1)
+    chip = (a * 2 + b) * 2 + x
+    def lanes(start, count): return prows.at[:, pl.ds(pl.multiple_of(start * 128, 128), count * 128)]
+    prows[:, pl.ds(pl.multiple_of(chip * 128, 128), 128)] = jnp.where((lane // 64) == c, mine.astype(f32), r1[...].astype(f32)).astype(bf16)
+    q = cp(lanes(chip, 1), lanes(chip, 1), xp)
+    n1.wait_recv()
+    n2 = cp(nrows(me - c - 2 * x, 4), nrows(me - c - 2 * x, 4), yp)
+    q.wait_recv()
+    q = cp(lanes(chip - x, 2), lanes(chip - x, 2), yp)
+    n2.wait_recv(); q.wait_recv()
+    qs = [cp(lanes(a * 4, 4), lanes(a * 4, 4), zp[j]) for j in range(1, A)] + [cp(nrows(a * 8, 8), nrows(a * 8, 8), zp[j]) for j in range(1, A)]
+    for q in qs: q.wait_recv()
+    cp.close()
+
+def prefix(A, part, outer2, norms):
+    v = lambda *s: pltpu.VMEM(s, bf16)
+    vf = lambda *s: pltpu.VMEM(s, f32)
+    vm = pl.BlockSpec(memory_space=pltpu.VMEM)
+    sds = jax.ShapeDtypeStruct
+    S = part.shape; n = A * 4
+    return pl.pallas_call(functools.partial(prefix_kernel, A),
+        out_shape=(sds(S, f32), sds((S[0], n * 128), bf16), sds((2 * n * norms.shape[0], 128), bf16)),
+        in_specs=[vm] * 3, out_specs=(vm,) * 3,
+        scratch_shapes=[vf(3, *S), vf(3, *S), vf(A, *S), v(S[0], 128), v(S[0], 128), pltpu.SemaphoreType.DMA((32,)), pltpu.SemaphoreType.DMA((32,))],
+        compiler_params=pltpu.CompilerParams(collective_id=4, has_side_effects=True), name="prefix_in")(part, outer2, norms)
+
+def tail_kernel(A, pg, outer2, ng, pown, tgrad, nsum, buf, got, zbuf, nbuf, ngot, nz, w0, w1, w2, w3, s0, s1, s2, c0, ssem, rsem):
+    a, b, x, c = place()
+    peers = neighbours(A)
+    core, xp, yp, zp = peers
+    greet([core, xp, yp] + zp[1:])
+    cp = Copies(ssem, rsem)
+    def lanes(start, count): return pl.ds(pl.multiple_of(start * 128, 128), count * 128)
+    qs = [cp(pg.at[:, lanes((a + j) % A * 4, 4)], w0.at[j - 1], zp[j]) for j in range(1, A)]
+    nsum[...] = all_add(cp, A, peers, nbuf, ngot, nz, ng[...])
+    t = pg[:, lanes(a * 4, 4)]
+    for j, q in enumerate(qs):
+        q.wait_recv()
+        t = t + w0[j]
+    s0[...] = t
+    q = cp(s0.at[:, lanes((1 - b) * 2, 2)], w1, yp)
+    q.wait_recv()
+    s1[...] = s0[:, lanes(b * 2, 2)] + w1[...]
+    q = cp(s1.at[:, lanes(1 - x, 1)], w2, xp)
+    q.wait_recv()
+    s2[...] = s1[:, lanes(x, 1)] + w2[...]
+    q = cp(s2, w3, core)
+    q.wait_recv()
+    t = s2[...] + w3[...]
+    pown[...] = t
+    lane = lax.broadcasted_iota(jnp.int32, t.shape, 1)
+    t = jnp.where((lane // 64) == c, t, 0.0)
+    p = lax.dot_general(t, outer2[...].astype(f32), (((1,), (1,)), ((), ())), precision=lax.Precision.HIGHEST, preferred_element_type=f32)
+    tgrad[...] = all_add(cp, A, peers, buf, got, zbuf, p)
+    cp.close()
+
+def tail(A, pg, outer2, ng):
+    vf = lambda *s: pltpu.VMEM(s, f32)
+    vm = pl.BlockSpec(memory_space=pltpu.VMEM)
+    sds = jax.ShapeDtypeStruct
+    K = pg.shape[0]; H = outer2.shape[0]; S = (K, H); N = ng.shape
+    return pl.pallas_call(functools.partial(tail_kernel, A),
+        out_shape=(sds((K, 128), f32), sds(S, f32), sds(N, f32)),
+        in_specs=[vm] * 3, out_specs=(vm,) * 3,
+        scratch_shapes=[vf(3, *S), vf(3, *S), vf(A, *S), vf(3, *N), vf(3, *N), vf(A, *N), vf(A - 1, K, 512), vf(K, 256), vf(K, 128), vf(K, 128), vf(K, 512), vf(K, 256), vf(K, 128), vf(8, 128), pltpu.SemaphoreType.DMA((32,)), pltpu.SemaphoreType.DMA((32,))],
+        compiler_params=pltpu.CompilerParams(collective_id=5, has_side_effects=True), name="prefix_out")(pg, outer2, ng)
+
+
+NEGATIVE = -1000000000.0
+PADDED = 32
+
+def project(x, weight, out, tile=256):
+    def step(t, _):
+        cols = pl.ds(pl.multiple_of(t * tile, tile), tile)
+        out[:, cols] = dot(x[...], weight[:, cols]).astype(out.dtype)
+        return 0
+    lax.fori_loop(0, out.shape[1] // tile, step, 0)
+
+def project_back(x, weight, out, tile=256):
+    def step(t, _):
+        cols = pl.ds(pl.multiple_of(t * tile, tile), tile)
+        out[:, cols] = dot_right(x[...], weight[cols, :]).astype(out.dtype)
+        return 0
+    lax.fori_loop(0, out.shape[1] // tile, step, 0)
+
+def lane_half(rows):
+    return lax.broadcasted_iota(jnp.int32, (rows, 128), 1) < 64
+
+def split_heads(v):
+    low = lane_half(v.shape[0])
+    zero = jnp.zeros_like(v)
+    return jnp.where(low, v, zero), jnp.where(low, zero, v)
+
+def self_mask(seg_col, seg_row):
+    T = seg_col.shape[0]
+    row = lax.broadcasted_iota(jnp.int32, (T, T), 0)
+    col = lax.broadcasted_iota(jnp.int32, (T, T), 1)
+    own = jnp.where((row >= col) & (seg_col[...] == seg_row[...]), 0.0, NEGATIVE)
+    lane = lax.broadcasted_iota(jnp.int32, (T, PADDED), 1)
+    return jnp.concatenate([own, jnp.where(lane < 30, 0.0, NEGATIVE)], axis=1)
+
+def attend(q, keys, values, penalty, probs, out, pairs=8):
+    def step(p, _):
+        cols = pl.ds(pl.multiple_of(p * 128, 128), 128)
+        kk, vv = keys(cols), values(cols)
+        qs = split_heads(q[:, cols])
+        vs = split_heads(vv)
+        total = None
+        for s in range(2):
+            score = jnp.where(penalty[...] < -1.0, NEGATIVE, dot_right(qs[s], kk) * 0.125)
+            e = jnp.exp(score - jnp.max(score, axis=-1, keepdims=True))
+            prob = (e * (1.0 / jnp.sum(e, axis=-1, keepdims=True))).astype(bf16)
+            probs[2 * p + s] = prob
+            mixed = dot(prob, vs[s])
+            total = mixed if total is None else total + mixed
+        out[:, cols] = total.astype(bf16)
+        return 0
+    lax.fori_loop(0, pairs, step, 0)
+
+def attend_back(grad, q, keys, values, probs, emit, pairs=8):
+    def step(p, _):
+        cols = pl.ds(pl.multiple_of(p * 128, 128), 128)
+        kk, vv = keys(cols), values(cols)
+        qs = split_heads(q[:, cols])
+        ks = split_heads(kk)
+        gs = split_heads(grad[:, cols])
+        dq = dk = dv = None
+        for s in range(2):
+            low = probs[2 * p + s]
+            prob = low.astype(f32)
+            t = prob * dot_right(gs[s], vv)
+            ds = (t - prob * jnp.sum(t, axis=-1, keepdims=True)).astype(bf16)
+            a, b, c = dot(ds, ks[s]), dot_left(ds, qs[s]), dot_left(low, gs[s])
+            dq, dk, dv = (a, b, c) if dq is None else (dq + a, dk + b, dv + c)
+        emit(cols, dq * 0.125, dk * 0.125, dv)
+        return 0
+    lax.fori_loop(0, pairs, step, 0)
+
+def both_keys(own, prows, offset):
+    def get(cols):
+        shifted = pl.ds(pl.multiple_of(cols.start + offset, 128), 128)
+        return jnp.concatenate([own[:, cols], prows[:, shifted]], axis=0)
+    return get
+
+def whole(ref):
+    return lambda cols: ref[:, cols]
+
+def add_norm(base, low, weight, gain, shift, out, normed, inverse, tile=256):
+    def step(t, _):
+        cols = pl.ds(pl.multiple_of(t * tile, tile), tile)
+        out[:, cols] = base[:, cols].astype(f32) + dot(low[...], weight[:, cols])
+        return 0
+    lax.fori_loop(0, out.shape[1] // tile, step, 0)
+    n, i = norm(out[...])
+    normed[...] = n
+    inverse[...] = i
+    out[...] = n * gain + shift
+
+def forward_kernel(inputs, memory, seg_col, seg_row, mem_row, weights, prows, vecs,
+                   q, k, v, probs, attended, first, n1, i1, cq, ck, cv, cprobs, crossed, second, n2, i2, pen, cpen):
+    width = inputs.shape[1]
+    pen[...] = self_mask(seg_col, seg_row)
+    cpen[...] = jnp.where(seg_col[...] == mem_row[...], 0.0, NEGATIVE)
+    project(inputs, weights.at[0], q); project(inputs, weights.at[1], k); project(inputs, weights.at[2], v)
+    project(memory, weights.at[6], ck); project(memory, weights.at[7], cv)
+    attend(q, both_keys(k, prows, 0), both_keys(v, prows, width), pen, probs, attended)
+    add_norm(inputs, attended, weights.at[3], vecs[0:1, :], vecs[1:2, :], first, n1, i1)
+    q[...] = q[...]
+    def step(t, _):
+        cols = pl.ds(pl.multiple_of(t * 256, 256), 256)
+        cq[:, cols] = dot(first[...].astype(bf16), weights[4, :, cols]).astype(bf16)
+        return 0
+    lax.fori_loop(0, width // 256, step, 0)
+    attend(cq, whole(ck), whole(cv), cpen, cprobs, crossed)
+    add_norm(first, crossed, weights.at[5], vecs[2:3, :], vecs[3:4, :], second, n2, i2)
+
+def forward(inputs, memory, seg_col, seg_row, mem_row, weights, prows, vecs):
+    T, D = inputs.shape; M = memory.shape[0]
+    vm = pl.BlockSpec(memory_space=pltpu.VMEM)
+    sds = jax.ShapeDtypeStruct
+    row, mrow, full, one = sds((T, D), bf16), sds((M, D), bf16), sds((T, D), f32), sds((T, 1), f32)
+    return pl.pallas_call(forward_kernel,
+        out_shape=(row, row, row, sds((16, T, T + PADDED), bf16), row, full, full, one, row, mrow, mrow, sds((16, T, M), bf16), row, full, full, one),
+        in_specs=[vm] * 8, out_specs=(vm,) * 16,
+        scratch_shapes=[pltpu.VMEM((T, T + PADDED), f32), pltpu.VMEM((T, M), f32)],
+        compiler_params=pltpu.CompilerParams(vmem_limit_bytes=60 << 20), name="attention_forward")(
+            inputs, memory, seg_col, seg_row, mem_row, weights, prows, vecs)
+
+def norm_back_into(e, n, i, gain, out, ngrad, at):
+    ee = e[...]
+    nn = n[...]
+    out[...] = norm_back(ee, nn, i[...], gain)
+    ngrad[at:at + 1, :] = jnp.sum(ee * nn, axis=0, keepdims=True)
+    ngrad[at + 1:at + 2, :] = jnp.sum(ee, axis=0, keepdims=True)
+
+def backward_kernel(gsec, q, k, v, probs, n1, i1, cq, ck, cv, cprobs, n2, i2, weights, prows, vecs,
+                    igrad, mgrad, dq, dk, dv, start_low, dcq, dck, dcv, mid_low, pgrad, ngrad, gmid, gfirst, og):
+    T, D = gsec.shape
+    norm_back_into(gsec, n2, i2, vecs[2:3, :], gmid, ngrad, 2)
+    mid_low[...] = gmid[...].astype(bf16)
+    project_back(mid_low, weights.at[5], og)
+    def emit(cols, a, b, c):
+        dcq[:, cols] = a.astype(bf16)
+        dck[:, cols] = b.astype(bf16)
+        dcv[:, cols] = c.astype(bf16)
+    attend_back(og, cq, whole(ck), whole(cv), cprobs, emit)
+    def step(t, _):
+        cols = pl.ds(pl.multiple_of(t * 256, 256), 256)
+        gfirst[:, cols] = gmid[:, cols] + dot_right(dcq[...], weights[4, cols, :])
+        return 0
+    lax.fori_loop(0, D // 256, step, 0)
+    norm_back_into(gfirst, n1, i1, vecs[0:1, :], gmid, ngrad, 0)
+    start_low[...] = gmid[...].astype(bf16)
+    project_back(start_low, weights.at[3], og)
+    def emit2(cols, a, b, c):
+        dq[:, cols] = a.astype(bf16)
+        dk[:, cols] = b[:T].astype(bf16)
+        dv[:, cols] = c[:T].astype(bf16)
+        pgrad[:, cols] = b[T:]
+        pgrad[:, pl.ds(pl.multiple_of(cols.start + D, 128), 128)] = c[T:]
+    attend_back(og, q, both_keys(k, prows, 0), both_keys(v, prows, D), probs, emit2)
+    def step2(t, _):
+        cols = pl.ds(pl.multiple_of(t * 256, 256), 256)
+        s = gmid[:, cols] + dot_right(dq[...], weights[0, cols, :]) + dot_right(dk[...], weights[1, cols, :]) + dot_right(dv[...], weights[2, cols, :])
+        igrad[:, cols] = s.astype(bf16)
+        mgrad[:, cols] = (dot_right(dck[...], weights[6, cols, :]) + dot_right(dcv[...], weights[7, cols, :])).astype(bf16)
+        return 0
+    lax.fori_loop(0, D // 256, step2, 0)
+
+def backward(gsec, q, k, v, probs, n1, i1, cq, ck, cv, cprobs, n2, i2, weights, prows, vecs):
+    T, D = gsec.shape; M = ck.shape[0]
+    vm = pl.BlockSpec(memory_space=pltpu.VMEM)
+    sds = jax.ShapeDtypeStruct
+    row, mrow = sds((T, D), bf16), sds((M, D), bf16)
+    return pl.pallas_call(backward_kernel,
+        out_shape=(row, mrow, row, row, row, row, row, mrow, mrow, row, sds((PADDED, 2 * D), f32), sds((8, D), f32)),
+        in_specs=[vm] * 16, out_specs=(vm,) * 12,
+        scratch_shapes=[pltpu.VMEM((T, D), f32), pltpu.VMEM((T, D), f32), pltpu.VMEM((T, D), bf16)],
+        compiler_params=pltpu.CompilerParams(vmem_limit_bytes=60 << 20), name="attention_backward")(
+            gsec, q, k, v, probs, n1, i1, cq, ck, cv, cprobs, n2, i2, weights, prows, vecs)
+
+def fast_body(A, inputs, memory, cotangent, segments, memory_segments, query_self, key_self, value_self, output_self,
+              query_cross, key_cross, value_cross, output_cross, self_gain, self_shift, cross_gain, cross_shift,
+              final_gain, final_shift, feed_in, feed_out, adapter_down, adapter_up, prefix_embed, prefix_inner, prefix_outer):
+    r = query_self.shape[0]
+    length, width = inputs.shape
+    w, n = lax.axis_index(WIDE), lax.axis_index(NARROW)
+    part = jnp.pad(matmul(prefix_embed, prefix_inner), ((0, 2), (0, 0)))
+    norms = jnp.pad(jnp.stack([self_gain, self_shift, cross_gain, cross_shift, final_gain, final_shift]), ((0, 10), (0, 128 - r)))
+    outer2 = jnp.concatenate([prefix_outer, prefix_outer], axis=1)
+    tangent, prefix_rows, nblocks = prefix(A, part, outer2, norms)
+    vecs = nblocks.reshape(-1, 16, 128)[:, :8, :r].transpose(1, 0, 2).reshape(8, width).astype(f32)
+    weights, fin2, fout2, down4, up4 = gather(A, jnp.stack([query_self, key_self, value_self, output_self, query_cross, output_cross, key_cross, value_cross]),
+        feed_in, feed_out, adapter_down, adapter_up)
+    q, k, v, probs, attended, first, n1, i1, cq, ck, cv, cprobs, crossed, second, n2, i2 = forward(
+        inputs, memory, segments.reshape(-1, 1), segments.reshape(1, -1), memory_segments.reshape(1, -1), weights, prefix_rows, vecs)
+    result, grad_second, fi, fo, ay, branch_low, ngrad3 = feed(A, second, cotangent, fin2, fout2, down4, up4, vecs[4:5], vecs[5:6])
+    inputs_grad, memory_grad, dq, dk, dv, start_low, dcq, dck, dcv, mid_low, pgrad, ngrad = backward(
+        grad_second, q, k, v, probs, n1, i1, cq, ck, cv, cprobs, n2, i2, weights, prefix_rows, vecs)
+    ng = jnp.concatenate([ngrad[:4], ngrad3, jnp.zeros((2, width), jnp.float32)])
+    pown, tgrad, nsum = tail(A, pgrad, outer2, ng)
+    xs = jnp.stack([inputs, inputs, inputs, attended, first.astype(bf16), crossed])
+    ys = jnp.stack([dq, dk, dv, start_low, dcq, mid_low])
+    sums, adapt, fi_sum, fo_sum = reduce_grads(A, r, xs, ys, memory, jnp.stack([dck, dcv]),
+        jnp.stack([second.astype(jnp.bfloat16), branch_low]), ay, fi, fo)
+    return (result, inputs_grad, memory_grad) + finish_outputs(
+        sums, adapt, fi_sum, fo_sum, pown, tgrad, nsum, tangent, prefix_embed, prefix_inner, r, w, n)
+
+def finish_outputs(sums, adapt, fi_sum, fo_sum, pown, tgrad, nsum, tangent, prefix_embed, prefix_inner, r, w, n):
+    mine = lax.dynamic_slice_in_dim(pown[:PREFIX], (n % 2) * 64, 64, 1)
+    tangent = tangent[:PREFIX]
+    tangent_grad = tgrad[:PREFIX] * (1.0 - tangent * tangent)
+    outer_grad = exact_left(tangent.astype(jnp.bfloat16).astype(jnp.float32), mine)
+    inner_grad = exact_left(prefix_embed.astype(jnp.float32), tangent_grad)
+    embed_grad = exact_right(tangent_grad, prefix_inner.astype(jnp.float32))
+    norm_grads = lax.dynamic_slice_in_dim(nsum, (w * 4 + n) * r, r, 1)
+    return (
+        sums[0], sums[1], sums[2], sums[3], sums[4], sums[6], sums[7], sums[5],
+        norm_grads[0], norm_grads[1], norm_grads[2], norm_grads[3], norm_grads[4], norm_grads[5],
+        fi_sum, fo_sum, adapt[0], adapt[1].T, embed_grad, inner_grad, outer_grad,
+    )
+
 def solution(mesh):
+    wide, narrow = mesh.shape[WIDE], mesh.shape[NARROW]
+    fits = narrow == 4 and wide == 8
+    body = functools.partial(fast_body, wide // 2) if fits else plain_body
     return jax.shard_map(
         body,
         mesh=mesh,
         in_specs=(
-            P(("wide", "narrow"), None),
-            P(("wide", "narrow"), None),
-            P(("wide", "narrow"), None),
-            P(("wide", "narrow")),
-            P(("wide", "narrow")),
-            P(("wide", "narrow"), None),
-            P(("wide", "narrow"), None),
-            P(("wide", "narrow"), None),
-            P(("wide", "narrow"), None),
-            P(("wide", "narrow"), None),
-            P(("wide", "narrow"), None),
-            P(("wide", "narrow"), None),
-            P(("wide", "narrow"), None),
-            P(("wide", "narrow")),
-            P(("wide", "narrow")),
-            P(("wide", "narrow")),
-            P(("wide", "narrow")),
-            P(("wide", "narrow")),
-            P(("wide", "narrow")),
-            P(None, "wide"),
-            P("wide", None),
-            P(None, "narrow"),
-            P("narrow", None),
-            P(None, ("wide", "narrow")),
-            P(("wide", "narrow"), None),
-            P(None, ("wide", "narrow")),
+            P(BOTH, None),
+            P(BOTH, None),
+            P(BOTH, None),
+            P(BOTH),
+            P(BOTH),
+            P(BOTH, None),
+            P(BOTH, None),
+            P(BOTH, None),
+            P(BOTH, None),
+            P(BOTH, None),
+            P(BOTH, None),
+            P(BOTH, None),
+            P(BOTH, None),
+            P(BOTH),
+            P(BOTH),
+            P(BOTH),
+            P(BOTH),
+            P(BOTH),
+            P(BOTH),
+            P(None, WIDE),
+            P(WIDE, None),
+            P(None, NARROW),
+            P(NARROW, None),
+            P(None, BOTH),
+            P(BOTH, None),
+            P(None, BOTH),
         ),
         out_specs=(
-            P(("wide", "narrow"), None),
-            P(("wide", "narrow"), None),
-            P(("wide", "narrow"), None),
-            P(("wide", "narrow"), None),
-            P(("wide", "narrow"), None),
-            P(("wide", "narrow"), None),
-            P(("wide", "narrow"), None),
-            P(("wide", "narrow"), None),
-            P(("wide", "narrow"), None),
-            P(("wide", "narrow"), None),
-            P(("wide", "narrow"), None),
-            P(("wide", "narrow")),
-            P(("wide", "narrow")),
-            P(("wide", "narrow")),
-            P(("wide", "narrow")),
-            P(("wide", "narrow")),
-            P(("wide", "narrow")),
-            P("narrow", "wide"),
-            P("wide", "narrow"),
-            P("wide", "narrow"),
-            P("narrow", "wide"),
-            P(None, ("wide", "narrow")),
-            P(("wide", "narrow"), None),
-            P(None, ("wide", "narrow")),
+            P(BOTH, None),
+            P(BOTH, None),
+            P(BOTH, None),
+            P(BOTH, None),
+            P(BOTH, None),
+            P(BOTH, None),
+            P(BOTH, None),
+            P(BOTH, None),
+            P(BOTH, None),
+            P(BOTH, None),
+            P(BOTH, None),
+            P(BOTH),
+            P(BOTH),
+            P(BOTH),
+            P(BOTH),
+            P(BOTH),
+            P(BOTH),
+            P(NARROW, WIDE),
+            P(WIDE, NARROW),
+            P(WIDE, NARROW),
+            P(NARROW, WIDE),
+            P(None, BOTH),
+            P(BOTH, None),
+            P(None, BOTH),
         ),
         check_vma=False,
     )

time: 2700 us -> 476 us (0.18)
  waiting for transfers between devices: 2330 us -> 0 us
  Pallas kernels: 0 us -> 441 us
  blocking collectives: 123 us -> 0 us
  matrix products: 125 us -> 5.16 us
  local copies, waits for them, and re-layouts: 74.8 us -> 23.6 us
    reduce_scatter x12 -> x0, waiting for transfers between devices: 886 us -> none  [the longest x1 140 us: body(): lax.psum_scatter(output_one_grad, ('wide', 'narrow'), scatter_dimension=0...]
    unnamed x40 -> x0, waiting for transfers between devices: 864 us -> none
    all_gather x14 -> x0, waiting for transfers between devices: 582 us -> none  [the longest x1 55.7 us: body(): lax.all_gather(value_self, ('wide', 'narrow'), axis=0, tiled=True)]
    pallas_call x0 -> x7, Pallas kernels: none -> 441 us  [the longest x1 125 us: gather(): pl.pallas_call(functools.partial(gather_kernel, A, r), out_shape=(sds((K,...]
    unnamed x2 -> x0, blocking collectives: 78.4 us -> none
    dot_general x42 -> x0, matrix products: 75.2 us -> none  [the longest x12 37.9 us: left_product(): lax.dot_general(left, right, (((0,), (0,)), ((), ())), preferred_element_...]
    unnamed x215 -> x87, local copies, waits for them, and re-layouts: 61.4 us -> 12.6 us
    all_gather x1 -> x0, blocking collectives: 44.2 us -> none  [body(): lax.all_gather(prefix_embed, ('wide', 'narrow'), axis=1, tiled=True)]
  transfers between devices with their start and end apart: 33 -> 0, of which waited for: 30 -> 0; matrix products, arithmetic and copies ran while one was open for 7% -> 0% of each run, Pallas kernels for 0% -> 0%
where the time goes in v1:
time: 476 us; the launch traced here: 475 us
  Pallas kernels  441 us (93%)
  local copies, waits for them, and re-layouts  23.6 us (5%)
  matrix products  5.16 us (1%)
    pallas_call x1, Pallas kernels, gather(): pl.pallas_call(functools.partial(gather_kernel, A, r), out_shape=(sds((K,...  125 us
    pallas_call x1, Pallas kernels, reduce_grads(): pl.pallas_call(functools.partial(reduce_kernel, A, r), out_shape=(sds((8,...  124 us
    pallas_call x1, Pallas kernels, feed(): pl.pallas_call(functools.partial(feed_kernel, A), out_shape=(sds((T, D),...  73 us
    pallas_call x1, Pallas kernels, prefix(): pl.pallas_call(functools.partial(prefix_kernel, A), out_shape=(sds(S, f32...  35.4 us
    pallas_call x1, Pallas kernels, tail(): pl.pallas_call(functools.partial(tail_kernel, A), out_shape=(sds((K, 128)...  33.4 us
    pallas_call x1, Pallas kernels, forward(): pl.pallas_call(forward_kernel, out_shape=(row, row, row, sds((16, T, T +...  25.9 us
    pallas_call x1, Pallas kernels, backward(): pl.pallas_call(backward_kernel, out_shape=(row, mrow, row, row, row, row,...  25.3 us
    unnamed x87, local copies, waits for them, and re-layouts  12.6 us

profile of v1, /device:TPU:0, one launch (start us, length us, event | category | flops | bytes accessed | tf_op | source)
XLA Modules:
  0.0 474.8 jit_solution(7073849906786436013)
XLA Ops:
  0.7 0.9 bitcast_dynamic-update-slice_fusion.19
  1.5 0.8 bitcast_dynamic-update-slice_fusion.18
  2.4 0.8 bitcast_dynamic-update-slice_fusion.17
  3.2 0.8 bitcast_dynamic-update-slice_fusion.16
  4.1 0.8 bitcast_dynamic-update-slice_fusion.15
  4.9 0.8 bitcast_dynamic-update-slice_fusion.14
  5.7 0.8 bitcast_dynamic-update-slice_fusion.13
  6.6 0.8 bitcast_dynamic-update-slice_fusion.12.s_ref
  8.3 124.6 %weights_in.1 = (bf16[8,1024,1024]{2,1,0:T(8,128)(2,1)}, bf16[1024,1024]{1,0:T(8,128)(2,1)}, bf16[1024,1024]{1,0:T(8,128)(2,1)}, bf16[1024,512]{1,0:T(8,128)(2,1)}, bf16[512,1024]{1,0:T(8,128)(2,1)}) custom-call(bf16[8,32,1024]{2,1,0:T(8,128)(2,1)} %copy-done.5, bf16[1024,512]{1,0:T(8,128)(2,1)} %fin.1, bf16[512,1024]{1,0:T(8,128)(2,1)} %fout.1, ...), custom_call_target="tpu_custom_call" | custom-call | tf_op jit(solution)/shard_map/weights_in/pallas_call | solution.py:573
  135.2 35.4 %prefix_in.1 = (f32[32,512]{1,0:T(8,128)}, bf16[32,2048]{1,0:T(8,128)(2,1)}, bf16[512,128]{1,0:T(8,128)(2,1)}) custom-call(f32[32,512]{1,0:T(8,128)} %pad.8.part, bf16[512,128]{1,0:T(8,128)(2,1)} %pad_maximum_fusion.2.outer2, bf16[16,128]{1,0:T(8,128)(2,1)} %pad.9.norms), custom_call_target="tpu_custom_call" | custom-call | tf_op jit(solution)/shard_map/prefix_in/pallas_call | solution.py:1046
  170.6 0.8 slice.100
  173.0 25.9 %attention_forward.1 = (bf16[128,1024]{1,0:T(8,128)(2,1)}, bf16[128,1024]{1,0:T(8,128)(2,1)}, bf16[128,1024]{1,0:T(8,128)(2,1)}, bf16[16,128,160]{2,1,0:T(8,128)...) custom-call(bf16[128,1024]{1,0:T(8,128)(2,1)} %inputs.1, ...), custom_call_target="tpu_custom_call" | custom-call | tf_op jit(solution)/shard_map/attention_forward/pallas_call | solution.py:1207
  200.2 73.0 %feed_forward.1 = (bf16[128,1024]{1,0:T(8,128)(2,1)}, f32[128,1024]{1,0:T(8,128)}, bf16[1024,1024]{1,0:T(8,128)(2,1)}, bf16[1024,1024]{1,0:T(8,128)(2,1)}, bf16[...) custom-call(f32[128,1024]{1,0:T(8,128)} %get-tuple-element.77.second, ...), custom_call_target="tpu_custom_call" | custom-call | tf_op jit(solution)/shard_map/feed_forward/pallas_call | solution.py:977
  273.2 25.3 %attention_backward.1 = (bf16[128,1024]{1,0:T(8,128)(2,1)}, bf16[256,1024]{1,0:T(8,128)(2,1)}, bf16[128,1024]{1,0:T(8,128)(2,1)}, bf16[128,1024]{1,0:T(8,128)(2,...) custom-call(f32[128,1024]{1,0:T(8,128)} %get-tuple-element.83.gsec, ...), custom_call_target="tpu_custom_call" | custom-call | tf_op jit(solution)/shard_map/attention_backward/pallas_call | solution.py:1260
  298.6 0.8 slice.88
  300.2 33.4 %prefix_out.1 = (f32[32,128]{1,0:T(8,128)}, f32[32,512]{1,0:T(8,128)}, f32[8,1024]{1,0:T(8,128)}) custom-call(f32[32,2048]{1,0:T(8,128)} %get-tuple-element.114.pg, bf16[512,128]{1,0:T(8,128)(2,1)} %pad_maximum_fusion.2.outer2, f32[8,1024]{1,0:T(8,128)} %maximum_maximum_fusion.ng), custom_call_target="tpu_custom_call" | custom-call | tf_op jit(solution)/shard_map/prefix_out/pallas_call | solution.py:1087
  333.7 1.7 fusion
  335.4 1.7 convolution_bitcast_fusion
  337.1 1.6 fusion.2
  340.0 1.1 pad_maximum_fusion.ym
  343.4 1.0 pad_maximum_fusion.1.ax
  345.0 123.8 %weight_grads.1 = (f32[8,32,1024]{2,1,0:T(8,128)}, f32[2,128,128]{2,1,0:T(8,128)}, f32[256,512]{1,0:T(8,128)}, f32[512,256]{1,0:T(8,128)}) custom-call(bf16[6,128,1024]{2,1,0:T(8,128)(2,1)} %copy-done.3, bf16[6,128,1024]{2,1,0:T(8,128)(2,1)} %copy-done.2, bf16[256,1024]{1,0:T(8,128)(2,1)} %mem.1, bf16[2,256,1024]{2,1,0:T(8,128)(2,1)} %pad_maximum_fusion.ym, ...), custom_call_target="tpu_custom_call" | custom-call | tf_op jit(solution)/shard_map/weight_grads/pallas_call | solution.py:799
  468.8 2.4 slice_bitcast_fusion
  473.3 0.8 copy.78
  (99 shorter events, 13.6 us)
Async XLA Ops:
  0.7 133.1 %copy-start = (bf16[32,512]{1,0:T(8,128)(2,1)S(1)}, bf16[32,512]{1,0:T(8,128)(2,1)}, u32[]{:S(2)}) copy-start(bf16[32,512]{1,0:T(8,128)(2,1)} %param.50) | copy-start | bytes 98308
  8.2 124.7 %copy-start.23 = (bf16[512,64]{0,1:T(8,128)(2,1)S(1)}, bf16[512,64]{0,1:T(8,128)(2,1)}, u32[]{:S(2)}) copy-start(bf16[512,64]{0,1:T(8,128)(2,1)} %param.51) | copy-start | bytes 196612
  8.2 125.6 %copy-start.24 = (bf16[30,32]{1,0:T(8,128)(2,1)S(1)}, bf16[30,32]{1,0:T(8,128)(2,1)}, u32[]{:S(2)}) copy-start(bf16[30,32]{1,0:T(8,128)(2,1)} %param.49) | copy-start | bytes 5764
  8.2 126.3 %copy-start.27 = (bf16[32]{0:T(256)(128)(2,1)S(1)}, bf16[32]{0:T(256)(128)(2,1)}, u32[]{:S(2)}) copy-start(bf16[32]{0:T(256)(128)(2,1)} %param.39) | copy-start | bytes 196
  8.2 126.3 %copy-start.28 = (bf16[32]{0:T(256)(128)(2,1)S(1)}, bf16[32]{0:T(256)(128)(2,1)}, u32[]{:S(2)}) copy-start(bf16[32]{0:T(256)(128)(2,1)} %param.40) | copy-start | bytes 196
  8.2 126.3 %copy-start.29 = (bf16[32]{0:T(256)(128)(2,1)S(1)}, bf16[32]{0:T(256)(128)(2,1)}, u32[]{:S(2)}) copy-start(bf16[32]{0:T(256)(128)(2,1)} %param.41) | copy-start | bytes 196
  8.2 126.3 %copy-start.30 = (bf16[32]{0:T(256)(128)(2,1)S(1)}, bf16[32]{0:T(256)(128)(2,1)}, u32[]{:S(2)}) copy-start(bf16[32]{0:T(256)(128)(2,1)} %param.42) | copy-start | bytes 196
  8.3 126.3 %copy-start.31 = (bf16[32]{0:T(256)(128)(2,1)S(1)}, bf16[32]{0:T(256)(128)(2,1)}, u32[]{:S(2)}) copy-start(bf16[32]{0:T(256)(128)(2,1)} %param.43) | copy-start | bytes 196
  8.3 126.3 %copy-start.32 = (bf16[32]{0:T(256)(128)(2,1)S(1)}, bf16[32]{0:T(256)(128)(2,1)}, u32[]{:S(2)}) copy-start(bf16[32]{0:T(256)(128)(2,1)} %param.44) | copy-start | bytes 196
  8.3 163.9 %copy-start.26 = (s32[128]{0:T(128)S(1)}, s32[128]{0:T(128)}, u32[]{:S(2)}) copy-start(s32[128]{0:T(128)} %param.29) | copy-start | bytes 1540
  273.2 26.3 %copy-start.25 = (f32[2,1024]{1,0:T(2,128)S(1)}, f32[2,1024]{1,0:T(2,128)}, u32[]{:S(2)}) copy-start(f32[2,1024]{1,0:T(2,128)} %get-tuple-element.116) | copy-start | bytes 24580
  273.2 60.4 %copy-start.6 = (f32[32,512]{1,0:T(8,128)S(1)}, f32[32,512]{1,0:T(8,128)}, u32[]{:S(2)}) copy-start(f32[32,512]{1,0:T(8,128)} %get-tuple-element.122) | copy-start | bytes 196612
  298.6 41.4 %copy-start.10 = (bf16[256,1024]{1,0:T(8,128)(2,1)S(1)}, bf16[256,1024]{1,0:T(8,128)(2,1)}, u32[]{:S(2)}) copy-start(bf16[256,1024]{1,0:T(8,128)(2,1)} %get-tuple-element.107) | copy-start | bytes 1572868
  298.6 41.4 %copy-start.11 = (bf16[256,1024]{1,0:T(8,128)(2,1)S(1)}, bf16[256,1024]{1,0:T(8,128)(2,1)}, u32[]{:S(2)}) copy-start(bf16[256,1024]{1,0:T(8,128)(2,1)} %get-tuple-element.108) | copy-start | bytes 1572868
  300.2 40.9 %copy-start.18 = (bf16[128,1024]{1,0:T(8,128)(2,1)S(1)}, bf16[128,1024]{1,0:T(8,128)(2,1)}, u32[]{:S(2)}) copy-start(bf16[128,1024]{1,0:T(8,128)(2,1)} %get-tuple-element.101) | copy-start | bytes 786436
  335.4 5.7 %copy-start.17 = (bf16[128,1024]{1,0:T(8,128)(2,1)S(1)}, bf16[128,1024]{1,0:T(8,128)(2,1)}, u32[]{:S(2)}) copy-start(bf16[128,1024]{1,0:T(8,128)(2,1)} %get-tuple-element.102) | copy-start | bytes 786436
  340.0 1.2 copy-start.15
  341.2 1.2 copy-start.7
  343.2 1.3 copy-start.2
  343.2 1.8 copy-start.3
  468.8 2.4 copy-start.22
  468.8 3.8 copy-start.12
  468.8 4.5 copy-start.9
  468.8 5.2 %copy-start.8 = (f32[512,256]{1,0:T(8,128)S(1)}, f32[512,256]{1,0:T(8,128)}, u32[]{:S(2)}) copy-start(f32[512,256]{1,0:T(8,128)} %get-tuple-element.210) | copy-start | bytes 1572868
  (9 other events, 9.4 us)

commit v2 on v0

--- a/solution.py
+++ b/solution.py
@@ -1,9 +1,18 @@
+import functools
 from functools import reduce
 
 import jax
 import jax.numpy as jnp
 from jax import lax
+from jax.experimental import pallas as pl
+from jax.experimental.pallas import tpu as pltpu
 from jax.sharding import PartitionSpec as P
+
+MESH = pl.DeviceIdType.MESH
+bf16, f32 = jnp.bfloat16, jnp.float32
+WIDE, NARROW = "wide", "narrow"
+BOTH = (WIDE, NARROW)
+
 
 HEADS = 16
 HEAD = 64
@@ -143,7 +152,7 @@
     ]
 
 
-def body(
+def plain_body(
     inputs,
     memory,
     cotangent,
@@ -190,23 +199,23 @@
         inner_full,
         outer_full,
     ) = (
-        lax.all_gather(query_self, ("wide", "narrow"), axis=0, tiled=True),
-        lax.all_gather(key_self, ("wide", "narrow"), axis=0, tiled=True),
-        lax.all_gather(value_self, ("wide", "narrow"), axis=0, tiled=True),
-        lax.all_gather(output_self, ("wide", "narrow"), axis=0, tiled=True),
-        lax.all_gather(query_cross, ("wide", "narrow"), axis=0, tiled=True),
-        lax.all_gather(key_cross, ("wide", "narrow"), axis=0, tiled=True),
-        lax.all_gather(value_cross, ("wide", "narrow"), axis=0, tiled=True),
-        lax.all_gather(output_cross, ("wide", "narrow"), axis=0, tiled=True),
-        lax.all_gather(self_gain, ("wide", "narrow"), axis=0, tiled=True),
-        lax.all_gather(self_shift, ("wide", "narrow"), axis=0, tiled=True),
-        lax.all_gather(cross_gain, ("wide", "narrow"), axis=0, tiled=True),
-        lax.all_gather(cross_shift, ("wide", "narrow"), axis=0, tiled=True),
-        lax.all_gather(final_gain, ("wide", "narrow"), axis=0, tiled=True),
-        lax.all_gather(final_shift, ("wide", "narrow"), axis=0, tiled=True),
-        lax.all_gather(prefix_embed, ("wide", "narrow"), axis=1, tiled=True),
-        lax.all_gather(prefix_inner, ("wide", "narrow"), axis=0, tiled=True),
-        lax.all_gather(prefix_outer, ("wide", "narrow"), axis=1, tiled=True),
+        lax.all_gather(query_self, BOTH, axis=0, tiled=True),
+        lax.all_gather(key_self, BOTH, axis=0, tiled=True),
+        lax.all_gather(value_self, BOTH, axis=0, tiled=True),
+        lax.all_gather(output_self, BOTH, axis=0, tiled=True),
+        lax.all_gather(query_cross, BOTH, axis=0, tiled=True),
+        lax.all_gather(key_cross, BOTH, axis=0, tiled=True),
+        lax.all_gather(value_cross, BOTH, axis=0, tiled=True),
+        lax.all_gather(output_cross, BOTH, axis=0, tiled=True),
+        lax.all_gather(self_gain, BOTH, axis=0, tiled=True),
+        lax.all_gather(self_shift, BOTH, axis=0, tiled=True),
+        lax.all_gather(cross_gain, BOTH, axis=0, tiled=True),
+        lax.all_gather(cross_shift, BOTH, axis=0, tiled=True),
+        lax.all_gather(final_gain, BOTH, axis=0, tiled=True),
+        lax.all_gather(final_shift, BOTH, axis=0, tiled=True),
+        lax.all_gather(prefix_embed, BOTH, axis=1, tiled=True),
+        lax.all_gather(prefix_inner, BOTH, axis=0, tiled=True),
+        lax.all_gather(prefix_outer, BOTH, axis=1, tiled=True),
     )
     factor_one = gain_one.astype(jnp.float32)
     factor_two = gain_two.astype(jnp.float32)
@@ -245,18 +254,18 @@
         first + matmul(crossed_low, output_two), factor_two, shift_two.astype(jnp.float32)
     )
     second_low = second.astype(jnp.bfloat16)
-    feed_rows = lax.all_gather(second_low, "wide", axis=0, tiled=True)
+    feed_rows = lax.all_gather(second_low, WIDE, axis=0, tiled=True)
     hidden_pre = matmul(feed_rows, feed_in)
     hidden_low = jax.nn.gelu(hidden_pre, approximate=False).astype(jnp.bfloat16)
     feed_sum = lax.psum_scatter(
-        matmul(hidden_low, feed_out), "wide", scatter_dimension=0, tiled=True
-    )
-    adapt_rows = lax.all_gather(second_low, "narrow", axis=0, tiled=True)
+        matmul(hidden_low, feed_out), WIDE, scatter_dimension=0, tiled=True
+    )
+    adapt_rows = lax.all_gather(second_low, NARROW, axis=0, tiled=True)
     bottle_pre = matmul(adapt_rows, adapter_down)
     bottle_low = jax.nn.gelu(bottle_pre, approximate=False).astype(jnp.bfloat16)
     adapt_sum = lax.psum_scatter(
         matmul(bottle_low, adapter_up).astype(jnp.bfloat16),
-        "narrow",
+        NARROW,
         scatter_dimension=0,
         tiled=True,
     ).astype(jnp.float32)
@@ -268,36 +277,36 @@
         cotangent.astype(jnp.float32), normed_three, inverse_three, factor_three
     )
     branch_low = grad_branch.astype(jnp.bfloat16)
-    branch_rows = lax.all_gather(branch_low, "wide", axis=0, tiled=True)
+    branch_rows = lax.all_gather(branch_low, WIDE, axis=0, tiled=True)
     grad_hidden = right_product(branch_rows, feed_out)
     grad_pre = gelu_back(hidden_pre, grad_hidden).astype(jnp.bfloat16)
     grad_out_part = left_product(hidden_low, branch_rows)
     grad_in_part = left_product(feed_rows, grad_pre)
     grad_feed = lax.psum_scatter(
-        right_product(grad_pre, feed_in), "wide", scatter_dimension=0, tiled=True
+        right_product(grad_pre, feed_in), WIDE, scatter_dimension=0, tiled=True
     )
     feed_in_total, feed_out_total = (
         lax.psum_scatter(
-            grad_in_part.astype(jnp.bfloat16), "narrow", scatter_dimension=0, tiled=True
+            grad_in_part.astype(jnp.bfloat16), NARROW, scatter_dimension=0, tiled=True
         ).astype(jnp.float32),
         lax.psum_scatter(
-            grad_out_part.astype(jnp.bfloat16), "narrow", scatter_dimension=1, tiled=True
+            grad_out_part.astype(jnp.bfloat16), NARROW, scatter_dimension=1, tiled=True
         ).astype(jnp.float32),
     )
-    branch_narrow = lax.all_gather(branch_low, "narrow", axis=0, tiled=True)
+    branch_narrow = lax.all_gather(branch_low, NARROW, axis=0, tiled=True)
     grad_bottle = ADAPT_SCALE * right_product(branch_narrow, adapter_up)
     grad_bottle_pre = gelu_back(bottle_pre, grad_bottle).astype(jnp.bfloat16)
     grad_up_part = ADAPT_SCALE * left_product(bottle_low, branch_narrow)
     grad_down_part = left_product(adapt_rows, grad_bottle_pre)
     grad_adapt = lax.psum_scatter(
         right_product(grad_bottle_pre, adapter_down).astype(jnp.bfloat16),
-        "narrow",
+        NARROW,
         scatter_dimension=0,
         tiled=True,
     ).astype(jnp.float32)
     down_total, up_total = (
-        lax.psum_scatter(grad_down_part, "wide", scatter_dimension=0, tiled=True),
-        lax.psum_scatter(grad_up_part, "wide", scatter_dimension=1, tiled=True),
+        lax.psum_scatter(grad_down_part, WIDE, scatter_dimension=0, tiled=True),
+        lax.psum_scatter(grad_up_part, WIDE, scatter_dimension=1, tiled=True),
     )
     grad_second = grad_branch + grad_feed + grad_adapt
     grad_mid, gain_two_grad, shift_two_grad = norm_backward(
@@ -364,23 +373,23 @@
         inner_sum,
         outer_sum,
     ) = (
-        lax.psum_scatter(query_one_grad, ("wide", "narrow"), scatter_dimension=0, tiled=True),
-        lax.psum_scatter(key_one_grad, ("wide", "narrow"), scatter_dimension=0, tiled=True),
-        lax.psum_scatter(value_one_grad, ("wide", "narrow"), scatter_dimension=0, tiled=True),
-        lax.psum_scatter(output_one_grad, ("wide", "narrow"), scatter_dimension=0, tiled=True),
-        lax.psum_scatter(query_two_grad, ("wide", "narrow"), scatter_dimension=0, tiled=True),
-        lax.psum_scatter(key_two_grad, ("wide", "narrow"), scatter_dimension=0, tiled=True),
-        lax.psum_scatter(value_two_grad, ("wide", "narrow"), scatter_dimension=0, tiled=True),
-        lax.psum_scatter(output_two_grad, ("wide", "narrow"), scatter_dimension=0, tiled=True),
-        lax.psum_scatter(gain_one_grad, ("wide", "narrow"), scatter_dimension=0, tiled=True),
-        lax.psum_scatter(shift_one_grad, ("wide", "narrow"), scatter_dimension=0, tiled=True),
-        lax.psum_scatter(gain_two_grad, ("wide", "narrow"), scatter_dimension=0, tiled=True),
-        lax.psum_scatter(shift_two_grad, ("wide", "narrow"), scatter_dimension=0, tiled=True),
-        lax.psum_scatter(gain_three_grad, ("wide", "narrow"), scatter_dimension=0, tiled=True),
-        lax.psum_scatter(shift_three_grad, ("wide", "narrow"), scatter_dimension=0, tiled=True),
-        lax.psum_scatter(embed_grad, ("wide", "narrow"), scatter_dimension=1, tiled=True),
-        lax.psum_scatter(inner_grad, ("wide", "narrow"), scatter_dimension=0, tiled=True),
-        lax.psum_scatter(outer_grad, ("wide", "narrow"), scatter_dimension=1, tiled=True),
+        lax.psum_scatter(query_one_grad, BOTH, scatter_dimension=0, tiled=True),
+        lax.psum_scatter(key_one_grad, BOTH, scatter_dimension=0, tiled=True),
+        lax.psum_scatter(value_one_grad, BOTH, scatter_dimension=0, tiled=True),
+        lax.psum_scatter(output_one_grad, BOTH, scatter_dimension=0, tiled=True),
+        lax.psum_scatter(query_two_grad, BOTH, scatter_dimension=0, tiled=True),
+        lax.psum_scatter(key_two_grad, BOTH, scatter_dimension=0, tiled=True),
+        lax.psum_scatter(value_two_grad, BOTH, scatter_dimension=0, tiled=True),
+        lax.psum_scatter(output_two_grad, BOTH, scatter_dimension=0, tiled=True),
+        lax.psum_scatter(gain_one_grad, BOTH, scatter_dimension=0, tiled=True),
+        lax.psum_scatter(shift_one_grad, BOTH, scatter_dimension=0, tiled=True),
+        lax.psum_scatter(gain_two_grad, BOTH, scatter_dimension=0, tiled=True),
+        lax.psum_scatter(shift_two_grad, BOTH, scatter_dimension=0, tiled=True),
+        lax.psum_scatter(gain_three_grad, BOTH, scatter_dimension=0, tiled=True),
+        lax.psum_scatter(shift_three_grad, BOTH, scatter_dimension=0, tiled=True),
+        lax.psum_scatter(embed_grad, BOTH, scatter_dimension=1, tiled=True),
+        lax.psum_scatter(inner_grad, BOTH, scatter_dimension=0, tiled=True),
+        lax.psum_scatter(outer_grad, BOTH, scatter_dimension=1, tiled=True),
     )
     return (
         result.astype(jnp.bfloat16),
@@ -410,63 +419,1117 @@
     )
 
 
+def place():
+    w = lax.axis_index(WIDE); n = lax.axis_index(NARROW)
+    return w // 2, w % 2, n // 2, n % 2
+
+def device(a, b, x, c):
+    return (a * 2 + b, x * 2 + c)
+
+def greet(peers):
+    barrier = pltpu.get_barrier_semaphore()
+    for p in peers:
+        pl.semaphore_signal(barrier, inc=1, device_id=p, device_id_type=MESH)
+    pl.semaphore_wait(barrier, len(peers))
+
+def remote(src, dst, send, recv, dev):
+    return pltpu.make_async_remote_copy(src_ref=src, dst_ref=dst, send_sem=send, recv_sem=recv, device_id=dev, device_id_type=MESH)
+
+
+def dot_left(l, r):
+    return lax.dot_general(l, r, (((0,), (0,)), ((), ())), preferred_element_type=f32)
+
+class Copies:
+    def __init__(self, send, recv):
+        self.send, self.recv, self.count, self.all = send, recv, 0, []
+    def __call__(self, src, dst, dev):
+        cp = remote(src, dst, self.send.at[self.count], self.recv.at[self.count], dev)
+        self.count += 1
+        cp.start(); self.all.append(cp)
+        return cp
+    def local(self, src, dst):
+        cp = pltpu.make_async_copy(src, dst, self.send.at[self.count])
+        self.count += 1
+        cp.start()
+        return cp
+    def sent(self, some):
+        for cp in some:
+            cp.wait_send()
+            self.all = [o for o in self.all if o is not cp]
+    def close(self):
+        for cp in self.all: cp.wait_send()
+
+
+EPSILON = 1e-05
+ADAPT_SCALE = 4.0
+
+def dot(l, r):
+    return jnp.dot(l, r, preferred_element_type=f32)
+
+def dot_right(l, r):
+    return lax.dot_general(l, r, (((1,), (1,)), ((), ())), preferred_element_type=f32)
+
+def gelu_both(v):
+    phi = 0.5 + 0.5 * lax.erf(v * 0.7071067811865476)
+    return v * phi, phi + v * (0.3989422804014327 * jnp.exp(-0.5 * v * v))
+
+def norm(v):
+    center = v - jnp.mean(v, axis=-1, keepdims=True)
+    inverse = lax.rsqrt(jnp.mean(center * center, axis=-1, keepdims=True) + EPSILON)
+    return center * inverse, inverse
+
+def norm_back(e, n, inverse, factor):
+    s = e * factor
+    return inverse * (s - jnp.mean(s, axis=-1, keepdims=True) - n * jnp.mean(s * n, axis=-1, keepdims=True))
+
+def feed_kernel(A, second, cot, fin, fout, down, up, gain, shift, result, gsec, fi, fo, ay, blow, ngrad,
+                rows, brow, hid, slope, gpre, part, q1, q2, q3, bslope, acc, ssem, rsem):
+    a, b, x, c = place()
+    yp = device(a, 1 - b, x, c)
+    zp = device((a + A // 2) % A, b, x, c)
+    greet([yp, zp])
+    cp = Copies(ssem, rsem)
+    T, D = second.shape
+    NC = 2
+    R = T // NC
+    HID = fin.shape[1]; TW = 256
+
+    def spread(buf):
+        zs, ys = [], []
+        for q in range(NC):
+            s = pl.ds(q * R, R)
+            zs.append(cp(buf.at[0, s], buf.at[2, s], zp))
+            ys.append(cp(buf.at[0, s], buf.at[1, s], yp))
+        def forward():
+            f = []
+            for q in range(NC):
+                s = pl.ds(q * R, R)
+                zs[q].wait_recv()
+                f.append(cp(buf.at[2, s], buf.at[3, s], yp))
+            return f
+        return zs, ys, forward
+
+    p3_sent = []
+    def collect(level):
+        p3, p1 = [], []
+        for q in range(NC):
+            p3.append(cp(part.at[3, pl.ds(q * R, R)], q3.at[level, pl.ds(q * R, R)], yp))
+        for q in range(NC):
+            p1.append(cp(part.at[1, pl.ds(q * R, R)], q1.at[level, pl.ds(q * R, R)], yp))
+        p2 = []
+        for q in range(NC):
+            s = pl.ds(q * R, R)
+            p3[q].wait_recv()
+            part[2, s] = part[2, s] + q3[level, s]
+            p2.append(cp(part.at[2, s], q2.at[level, s], zp))
+        p3_sent.append(p3)
+        return p1, p2
+
+    def gather_up(level, p1, p2):
+        for q in range(NC):
+            s = pl.ds(q * R, R)
+            p1[q].wait_recv(); p2[q].wait_recv()
+            acc[s] = acc[s] + q1[level, s].astype(f32) + q2[level, s].astype(f32)
+        cp.sent(p1 + p2 + p3_sent.pop())
+
+    rows[0] = second[...].astype(bf16)
+    zs, ys, forward = spread(rows)
+    for t in range(2):
+        cols = pl.ds(t * 256, 256)
+        g, s = gelu_both(dot(rows[0], down[:, cols]))
+        ay[1, :, cols] = (ADAPT_SCALE * g.astype(bf16).astype(f32)).astype(bf16)
+        bslope[:, cols] = s
+    def enter(j):
+        def tile(t, _):
+            cols = pl.ds(pl.multiple_of(t * TW, TW), TW)
+            g, s = gelu_both(dot(rows[j], fin[:, cols]))
+            hid[j, :, cols] = g.astype(bf16)
+            slope[j, :, cols] = s
+            return 0
+        lax.fori_loop(0, HID // TW, tile, 0)
+        def tile2(t, _):
+            cols = pl.ds(pl.multiple_of(t * TW, TW), TW)
+            p = dot(hid[j], fout[:, cols])
+            if j == 0:
+                acc[:, cols] = p + dot(ay[1], up[:, cols])
+            else:
+                part[j, :, cols] = p.astype(bf16)
+            return 0
+        lax.fori_loop(0, D // TW, tile2, 0)
+    enter(0)
+    for q in ys: q.wait_recv()
+    fw = forward()
+    enter(1)
+    enter(2)
+    for q in fw: q.wait_recv()
+    enter(3)
+    p1, p2 = collect(0)
+    gather_up(0, p1, p2)
+    n3, inv3 = norm(second[...] + acc[...])
+    fac = gain[...].astype(f32)
+    result[...] = (n3 * fac + shift[...].astype(f32)).astype(bf16)
+    e = cot[...].astype(f32)
+    gb = norm_back(e, n3, inv3, fac)
+    gbl = gb.astype(bf16)
+    brow[0] = gbl
+    zs, ys, forward = spread(brow)
+    blow[...] = gbl
+    acc[...] = gb
+    ngrad[0:1, :] = jnp.sum(e * n3, axis=0, keepdims=True)
+    ngrad[1:2, :] = jnp.sum(e, axis=0, keepdims=True)
+    def adapt_tile(t, _):
+        cols = pl.ds(pl.multiple_of(t * 256, 256), 256)
+        gbot = bslope[:, cols] * (ADAPT_SCALE * dot_right(brow[0], up[cols, :]))
+        ay[0, :, cols] = gbot.astype(bf16)
+        return 0
+    lax.fori_loop(0, down.shape[1] // 256, adapt_tile, 0)
+    def leave(j):
+        def tile(t, _):
+            cols = pl.ds(pl.multiple_of(t * TW, TW), TW)
+            gh = dot_right(brow[j], fout[cols, :])
+            gpre[j, :, cols] = (slope[j, :, cols] * gh).astype(bf16)
+            return 0
+        lax.fori_loop(0, HID // TW, tile, 0)
+        def tile2(t, _):
+            cols = pl.ds(pl.multiple_of(t * TW, TW), TW)
+            p = dot_right(gpre[j], fin[cols, :])
+            if j == 0:
+                acc[:, cols] = acc[:, cols] + p + dot_right(ay[0], down[cols, :])
+            else:
+                part[j, :, cols] = p.astype(bf16)
+            return 0
+        lax.fori_loop(0, D // TW, tile2, 0)
+    leave(0)
+    for q in ys: q.wait_recv()
+    fw = forward()
+    leave(1)
+    leave(2)
+    for q in fw: q.wait_recv()
+    leave(3)
+    p1, p2 = collect(1)
+    def wtile(t, _):
+        cols = pl.ds(pl.multiple_of(t * TW, TW), TW)
+        fi[:, cols] = dot_left(rows[...].reshape(4 * T, D), gpre[:, :, cols].reshape(4 * T, TW)).astype(bf16)
+        fo[:, cols] = dot_left(hid[...].reshape(4 * T, HID), brow[:, :, cols].reshape(4 * T, TW)).astype(bf16)
+        return 0
+    lax.fori_loop(0, HID // TW, wtile, 0)
+    gather_up(1, p1, p2)
+    gsec[...] = acc[...]
+    cp.close()
+
+def feed(A, second, cot, fin, fout, down, up, gain, shift):
+    T, D = second.shape; HID = fin.shape[1]; AD = down.shape[1]
+    v = lambda *s: pltpu.VMEM(s, bf16)
+    vf = lambda *s: pltpu.VMEM(s, f32)
+    vm = pl.BlockSpec(memory_space=pltpu.VMEM)
+    sds = jax.ShapeDtypeStruct
+    return pl.pallas_call(
+        functools.partial(feed_kernel, A),
+        out_shape=(sds((T, D), bf16), sds((T, D), f32), sds((D, HID), bf16), sds((HID, D), bf16), sds((2, T, AD), bf16), sds((T, D), bf16), sds((2, D), f32)),
+        in_specs=[vm] * 8, out_specs=(vm,) * 7,
+        scratch_shapes=[v(4, T, D), v(4, T, D), v(4, T, HID), vf(4, T, HID), v(4, T, HID), v(4, T, D),
+            v(2, T, D), v(2, T, D), v(2, T, D), vf(T, AD), vf(T, D),
+            pltpu.SemaphoreType.DMA((64,)), pltpu.SemaphoreType.DMA((64,))],
+        compiler_params=pltpu.CompilerParams(collective_id=3, has_side_effects=True, vmem_limit_bytes=60 << 20),
+        name="feed_forward")(second, cot, fin, fout, down, up, gain, shift)
+
+
+NEGATIVE = -1000000000.0
+PADDED = 32
+
+def project(x, weight, out, tile=256):
+    def step(t, _):
+        cols = pl.ds(pl.multiple_of(t * tile, tile), tile)
+        out[:, cols] = dot(x[...], weight[:, cols]).astype(out.dtype)
+        return 0
+    lax.fori_loop(0, out.shape[1] // tile, step, 0)
+
+
+def lane_half(rows):
+    return lax.broadcasted_iota(jnp.int32, (rows, 128), 1) < 64
+
+def split_heads(v):
+    low = lane_half(v.shape[0])
+    zero = jnp.zeros_like(v)
+    return jnp.where(low, v, zero), jnp.where(low, zero, v)
+
+def self_mask(seg_col, seg_row):
+    T = seg_col.shape[0]
+    row = lax.broadcasted_iota(jnp.int32, (T, T), 0)
+    col = lax.broadcasted_iota(jnp.int32, (T, T), 1)
+    own = jnp.where((row >= col) & (seg_col[...] == seg_row[...]), 0.0, NEGATIVE)
+    lane = lax.broadcasted_iota(jnp.int32, (T, PADDED), 1)
+    return jnp.concatenate([own, jnp.where(lane < 30, 0.0, NEGATIVE)], axis=1)
+
+def attend(q, keys, values, penalty, probs, out, pairs=8):
+    def step(p, _):
+        cols = pl.ds(pl.multiple_of(p * 128, 128), 128)
+        kk, vv = keys(cols), values(cols)
+        qs = split_heads(q[:, cols])
+        vs = split_heads(vv)
+        total = None
+        for s in range(2):
+            score = jnp.where(penalty[...] < -1.0, NEGATIVE, dot_right(qs[s], kk) * 0.125)
+            e = jnp.exp(score - jnp.max(score, axis=-1, keepdims=True))
+            prob = (e * (1.0 / jnp.sum(e, axis=-1, keepdims=True))).astype(bf16)
+            probs[2 * p + s] = prob
+            mixed = dot(prob, vs[s])
+            total = mixed if total is None else total + mixed
+        out[:, cols] = total.astype(bf16)
+        return 0
+    lax.fori_loop(0, pairs, step, 0)
+
+
+def both_keys(own, prows, offset):
+    def get(cols):
+        shifted = pl.ds(pl.multiple_of(cols.start + offset, 128), 128)
+        return jnp.concatenate([own[:, cols], prows[:, shifted]], axis=0)
+    return get
+
+def whole(ref):
+    return lambda cols: ref[:, cols]
+
+def add_norm(base, low, weight, gain, shift, out, normed, inverse, tile=256):
+    def step(t, _):
+        cols = pl.ds(pl.multiple_of(t * tile, tile), tile)
+        out[:, cols] = base[:, cols].astype(f32) + dot(low[...], weight[:, cols])
+        return 0
+    lax.fori_loop(0, out.shape[1] // tile, step, 0)
+    n, i = norm(out[...])
+    normed[...] = n
+    inverse[...] = i
+    out[...] = n * gain + shift
+
+def forward_kernel(inputs, memory, seg_col, seg_row, mem_row, weights, prows, vecs,
+                   q, k, v, probs, attended, first, n1, i1, cq, ck, cv, cprobs, crossed, second, n2, i2, pen, cpen):
+    width = inputs.shape[1]
+    pen[...] = self_mask(seg_col, seg_row)
+    cpen[...] = jnp.where(seg_col[...] == mem_row[...], 0.0, NEGATIVE)
+    project(inputs, weights.at[0], q); project(inputs, weights.at[1], k); project(inputs, weights.at[2], v)
+    project(memory, weights.at[6], ck); project(memory, weights.at[7], cv)
+    attend(q, both_keys(k, prows, 0), both_keys(v, prows, width), pen, probs, attended)
+    add_norm(inputs, attended, weights.at[3], vecs[0:1, :], vecs[1:2, :], first, n1, i1)
+    q[...] = q[...]
+    def step(t, _):
+        cols = pl.ds(pl.multiple_of(t * 256, 256), 256)
+        cq[:, cols] = dot(first[...].astype(bf16), weights[4, :, cols]).astype(bf16)
+        return 0
+    lax.fori_loop(0, width // 256, step, 0)
+    attend(cq, whole(ck), whole(cv), cpen, cprobs, crossed)
+    add_norm(first, crossed, weights.at[5], vecs[2:3, :], vecs[3:4, :], second, n2, i2)
+
+def forward(inputs, memory, seg_col, seg_row, mem_row, weights, prows, vecs):
+    T, D = inputs.shape; M = memory.shape[0]
+    vm = pl.BlockSpec(memory_space=pltpu.VMEM)
+    sds = jax.ShapeDtypeStruct
+    row, mrow, full, one = sds((T, D), bf16), sds((M, D), bf16), sds((T, D), f32), sds((T, 1), f32)
+    return pl.pallas_call(forward_kernel,
+        out_shape=(row, row, row, sds((16, T, T + PADDED), bf16), row, full, full, one, row, mrow, mrow, sds((16, T, M), bf16), row, full, full, one),
+        in_specs=[vm] * 8, out_specs=(vm,) * 16,
+        scratch_shapes=[pltpu.VMEM((T, T + PADDED), f32), pltpu.VMEM((T, M), f32)],
+        compiler_params=pltpu.CompilerParams(vmem_limit_bytes=60 << 20), name="attention_forward")(
+            inputs, memory, seg_col, seg_row, mem_row, weights, prows, vecs)
+
+def norm_back_into(e, n, i, gain, out, ngrad, at):
+    ee = e[...]
+    nn = n[...]
+    out[...] = norm_back(ee, nn, i[...], gain)
+    ngrad[at:at + 1, :] = jnp.sum(ee * nn, axis=0, keepdims=True)
+    ngrad[at + 1:at + 2, :] = jnp.sum(ee, axis=0, keepdims=True)
+
+
+def columns(t, tile=256):
+    return pl.ds(pl.multiple_of(t * tile, tile), tile)
+
+def loop(start, stop, step):
+    lax.fori_loop(start, stop, lambda t, z: (step(t), z)[1], 0)
+
+def front_kernel(A, r, inputs, memory, seg_col, seg_row, mem_row, embed, inner, outer2, norms, *refs):
+    ws, (fin, fout, down, up) = refs[:8], refs[8:12]
+    (wout, fin2, fout2, down4, up4, tangent, prows_o, vecs_o, q_o, k_o, v_o, probs_o, att_o, first_o, n1_o, i1_o, cq_o, ck_o, cv_o, cprobs_o, crossed_o,
+     second_o, slow_o, n2_o, i2_o) = refs[12:37]
+    (g, q, k, v, probs, att, first, flow, n1, i1, cq, ck, cv, cprobs, crossed, second, slow, n2, i2, pen, cpen,
+     buf, got, zbuf, r0, r1, prows, nout, vecs, tan, ssem, rsem) = refs[37:]
+    a, b, x, c = place()
+    core, xp, yp = device(a, b, x, 1 - c), device(a, b, 1 - x, c), device(a, 1 - b, x, c)
+    zp = [device((a + j) % A, b, x, c) for j in range(A)]
+    za = a + 1 - 2 * (a % 2)
+    zq = device(za, b, x, c)
+    greet([core, xp, yp] + zp[1:])
+    cp = Copies(ssem, rsem)
+    T, D = inputs.shape
+    pairs = 4
+    def row(a_, b_, x_):
+        return pl.multiple_of(((a_ * 2 + b_) * 2 + x_) * 2 * r, 2 * r)
+    at = pl.ds(pl.multiple_of(row(a, b, x) + c * r, r), r)
+    cut = (pl.ds(0, 3 * D // 8), pl.ds(3 * D // 8, 5 * D // 8))
+    def block(i, h, a_, b_, x_):
+        return g.at[2 * i + c, pl.ds(row(a_, b_, x_), 2 * r), cut[h]]
+    kept = []
+    own, cross = [], []
+    base = cp.count
+    for i in range(pairs):
+        s1, s2, rr = ssem.at[cp.count], ssem.at[cp.count + 1], rsem.at[cp.count]
+        cp.count += 2
+        def start(keep, give):
+            pltpu.make_async_copy(ws[2 * i + keep], g.at[2 * i + keep, at], s2).start()
+            remote(ws[2 * i + give], g.at[2 * i + give, at], s1, rr, core).start()
+        pl.when(c == 0)(functools.partial(start, 0, 1))
+        pl.when(c == 1)(functools.partial(start, 1, 0))
+        own.append(pltpu.make_async_copy(ws[2 * i], g.at[2 * i, at], s2))
+        cross.append(remote(ws[2 * i], g.at[2 * i, at], s1, rr, core))
+    G = norms.shape[0]
+    me = ((a * 2 + b) * 2 + x) * 2 + c
+    chip = (a * 2 + b) * 2 + x
+    def nrows(start, count): return nout.at[pl.ds(pl.multiple_of(start * G, G), count * G)]
+    def lanes(start, count): return prows.at[:, pl.ds(pl.multiple_of(start * 128, 128), count * 128)]
+    nout[pl.ds(pl.multiple_of(me * G, G), G), :] = norms[...]
+    small = {}
+    peers = (core, xp, yp)
+    def pre0():
+        small["t"] = dot(embed[...], inner[...])
+        buf[0] = small["t"]
+        small["s"] = [cp(buf.at[0], got.at[0], core), cp(nrows(me, 1), nrows(me, 1), core)]
+    def pre(n):
+        def go():
+            for e in small["s"]: e.wait_recv()
+            buf[n] = buf[n - 1] + got[n - 1]
+            start, count = (me - c, 2) if n == 1 else (me - c - 2 * x, 4)
+            small["s"] = [cp(buf.at[n], got.at[n], peers[n]), cp(nrows(start, count), nrows(start, count), peers[n])]
+        return go
+    def pre3():
+        for e in small["s"]: e.wait_recv()
+        zbuf[a] = buf[2] + got[2]
+        small["s"] = [cp(zbuf.at[a], zbuf.at[a], zp[j]) for j in range(1, A)] + [cp(nrows(a * 8, 8), nrows(a * 8, 8), zp[j]) for j in range(1, A)]
+    def pre4():
+        for e in small["s"]: e.wait_recv()
+        t = zbuf[0]
+        for n in range(1, A): t = t + zbuf[n]
+        t = jnp.tanh(t)
+        tan[...] = t
+        r0[...] = dot(t.astype(bf16), outer2[...]).astype(bf16)
+        small["s"] = [cp(r0, r1, core)]
+        lane = lax.broadcasted_iota(jnp.int32, (G, 128), 1) // 32
+        for w in range(2 * A):
+            s = nout[pl.ds(w * 4 * G, G), :].astype(f32)
+            for n in range(1, 4):
+                s = jnp.where(lane == n, nout[pl.ds((w * 4 + n) * G, G), :].astype(f32), s)
+            vecs[:, pl.ds(w * 128, 128)] = s[:8]
+        kept.append(cp.local(tan, tangent))
+        kept.append(cp.local(vecs, vecs_o))
+    def pre5():
+        small["s"][0].wait_recv()
+        lane = lax.broadcasted_iota(jnp.int32, (PADDED, 128), 1)
+        prows[:, pl.ds(pl.multiple_of(chip * 128, 128), 128)] = jnp.where((lane // 64) == c, r0[...].astype(f32), r1[...].astype(f32)).astype(bf16)
+        small["s"] = [cp(lanes(chip, 1), lanes(chip, 1), xp)]
+    def pre6():
+        small["s"][0].wait_recv()
+        small["s"] = [cp(lanes(chip - x, 2), lanes(chip - x, 2), yp)]
+    def pre7():
+        small["s"][0].wait_recv()
+        small["s"] = [cp(lanes(a * 4, 4), lanes(a * 4, 4), zp[j]) for j in range(1, A)]
+    def pre8():
+        for e in small["s"]: e.wait_recv()
+        kept.append(cp.local(prows, prows_o))
+    H, AD = fin.shape[1], down.shape[1]
+    kept += [cp.local(fin, fin2.at[:, pl.ds(0, H)]), cp.local(fout, fout2.at[pl.ds(0, H)])]
+    nd = pl.ds(pl.multiple_of((x * 2 + c) * AD, AD), AD)
+    md = pl.ds(pl.multiple_of((2 - 2 * x + c) * AD, AD), AD)
+    kept += [cp.local(down, down4.at[:, nd]), cp.local(up, up4.at[nd])]
+    feeds, passed = {}, []
+    def feed_send(i):
+        n = D // 8
+        ri = pl.ds(pl.multiple_of(c * (D // 2) + i * n, n), n)
+        m = H // 8
+        ro = pl.ds(pl.multiple_of(c * (H // 2) + i * m, m), m)
+        ro2 = pl.ds(pl.multiple_of(H + c * (H // 2) + i * m, m), m)
+        feeds[i] = [(cp(fin.at[ri], fin2.at[ri, pl.ds(H, H)], zq), fin2.at[ri, pl.ds(H, H)]),
+                    (cp(fout.at[ro], fout2.at[ro2], zq), fout2.at[ro2])]
+    def adapter_send():
+        feeds["a"] = [(cp(down, down4.at[:, nd], xp), down4.at[:, md]), (cp(up, up4.at[nd], xp), up4.at[md])]
+        passed.extend([cp(down, down4.at[:, nd], core), cp(up, up4.at[nd], core)])
+    def feed_pass(i):
+        for e, ref in feeds[i]:
+            e.wait_recv()
+            passed.append(cp(ref, ref, core))
+    zc, mc, lc, dc = {}, {}, {}, {}
+    two, three = (yp, xp), (xp, yp)
+    def first_send(i):
+        own[i].wait(); cross[i].wait()
+        for h in range(2):
+            mc[i, h, 0] = cp(block(i, h, a, b, x), block(i, h, a, b, x), two[h])
+        for h in range(2):
+            lc[i, h, 0, 0] = cp(block(i, h, a, b, x), block(i, h, a, b, x), three[h])
+        for j in range(1, A):
+            for h in range(2):
+                zc[i, h, j] = cp(block(i, h, a, b, x), block(i, h, a, b, x), zp[j])
+    def mid(i, j):
+        aj = (a + A - j) % A
+        for h in range(2):
+            zc[i, h, j].wait_recv()
+            mc[i, h, j] = cp(block(i, h, aj, b, x), block(i, h, aj, b, x), two[h])
+        for h in range(2):
+            lc[i, h, j, 0] = cp(block(i, h, aj, b, x), block(i, h, aj, b, x), three[h])
+    def third(i, j):
+        aj = (a + A - j) % A
+        for h in range(2):
+            w = (aj, 1 - b, x) if h == 0 else (aj, b, 1 - x)
+            mc[i, h, j].wait_recv()
+            lc[i, h, j, 1] = cp(block(i, h, *w), block(i, h, *w), three[h])
+    def fin_wait(i):
+        for j in range(A):
+            for h in range(2):
+                lc[i, h, j, 0].wait_recv(); lc[i, h, j, 1].wait_recv()
+        dc[i] = cp(g.at[2 * i + c], g.at[2 * i + c], core)
+        kept.append(cp.local(g.at[2 * i + c], wout.at[2 * i + c]))
+    def arrive(i):
+        dc[i].wait_recv()
+        kept.append(cp.local(g.at[2 * i + 1 - c], wout.at[2 * i + 1 - c]))
+    def halves(src, w, out):
+        def part(n):
+            def go():
+                xv = src[...]
+                def step(t):
+                    out[:, columns(t)] = dot(xv, g[w, :, columns(t)]).astype(bf16)
+                loop(2 * n, 2 * n + 2, step)
+            return go
+        return [part(0), part(1)]
+    def keep(src, dst):
+        def go(): kept.append(cp.local(src, dst))
+        return go
+    def masks():
+        pen[...] = self_mask(seg_col, seg_row)
+        cpen[...] = jnp.where(seg_col[...] == mem_row[...], 0.0, NEGATIVE)
+    def softmax(qv, kk, penalty):
+        score = jnp.where(penalty[...] < -1.0, NEGATIVE, dot_right(qv, kk) * 0.125)
+        e = jnp.exp(score - jnp.max(score, axis=-1, keepdims=True))
+        return (e * (1.0 / jnp.sum(e, axis=-1, keepdims=True))).astype(bf16)
+    def own_attend(n):
+        def go():
+            def step(p):
+                cols = columns(p, 128)
+                kk = jnp.concatenate([k[:, cols], prows[:, cols]], axis=0)
+                vv = jnp.concatenate([v[:, cols], prows[:, pl.ds(pl.multiple_of(D + p * 128, 128), 128)]], axis=0)
+                qs, vs = split_heads(q[:, cols]), split_heads(vv)
+                total = None
+                for s in range(2):
+                    prob = softmax(qs[s], kk, pen)
+                    probs[2 * p + s] = prob
+                    m = dot(prob, vs[s])
+                    total = m if total is None else total + m
+                att[:, cols] = total.astype(bf16)
+            loop(2 * n, 2 * n + 2, step)
+        return go
+    def cross_scores(n):
+        def go():
+            def step(p):
+                cols = columns(p, 128)
+                qs = split_heads(cq[:, cols])
+                for s in range(2):
+                    cprobs[2 * p + s] = softmax(qs[s], ck[:, cols], cpen)
+            loop(2 * n, 2 * n + 2, step)
+        return go
+    def cross_mix(n):
+        def go():
+            def step(p):
+                cols = columns(p, 128)
+                vs = split_heads(cv[:, cols])
+                crossed[:, cols] = (dot(cprobs[2 * p], vs[0]) + dot(cprobs[2 * p + 1], vs[1])).astype(bf16)
+            loop(4 * n, 4 * n + 4, step)
+        return go
+    def normed(base, low, w, at, out, nn, ii, olow):
+        def part(n):
+            def go():
+                lv = low[...]
+                def step(t):
+                    out[:, columns(t)] = base[:, columns(t)].astype(f32) + dot(lv, g[w, :, columns(t)])
+                loop(2 * n, 2 * n + 2, step)
+            return go
+        def last():
+            m, inv = norm(out[...])
+            nn[...] = m
+            ii[...] = inv
+            s = m * vecs[at:at + 1, :] + vecs[at + 1:at + 2, :]
+            out[...] = s
+            olow[...] = s.astype(bf16)
+        return [part(0), part(1), last]
+    comp = {
+        0: halves(inputs, 0, q) + halves(inputs, 1, k) + [keep(q, q_o), keep(k, k_o), masks],
+        1: halves(inputs, 2, v) + [keep(v, v_o)] + [own_attend(n) for n in range(4)] + [keep(probs, probs_o), keep(att, att_o)]
+           + normed(inputs, att, 3, 0, first, n1, i1, flow) + [keep(flow, first_o), keep(n1, n1_o), keep(i1, i1_o)],
+        2: halves(memory, 4, ck) + [keep(ck, ck_o)] + halves(flow, 5, cq) + [keep(cq, cq_o)] + [cross_scores(n) for n in range(4)] + [keep(cprobs, cprobs_o)],
+        3: halves(memory, 6, cv) + [keep(cv, cv_o)] + [cross_mix(n) for n in range(2)] + [keep(crossed, crossed_o)]
+           + normed(first, crossed, 7, 2, second, n2, i2, slow) + [keep(second, second_o), keep(slow, slow_o), keep(n2, n2_o), keep(i2, i2_o)],
+    }
+    queue = [pre0, pre(1), pre(2), pre3, pre4, pre5, pre6, pre7, pre8]
+    def turn(count=1):
+        for _ in range(count):
+            if queue: queue.pop(0)()
+    first_send(0)
+    turn()
+    for i in range(pairs):
+        if i + 1 < pairs:
+            first_send(i + 1)
+        feed_send(i)
+        if i == 1:
+            adapter_send()
+        turn()
+        third(i, 0)
+        turn()
+        for j in range(1, A):
+            mid(i, j)
+            turn(1)
+        if i:
+            fin_wait(i - 1)
+            feed_pass(i - 1)
+            turn()
+        for j in range(1, A):
+            third(i, j)
+            turn(1)
+        if i:
+            arrive(i - 1)
+            queue += comp[i - 1]
+        turn(3)
+    feed_pass(3); feed_pass("a")
+    turn(6)
+    fin_wait(3)
+    turn(100)
+    arrive(3)
+    queue += comp[3]
+    turn(100)
+    for e in kept: e.wait()
+    for e in passed: e.wait_recv()
+    own_ids = None
+    cp.close()
+
+def front(A, r, inputs, memory, seg_col, seg_row, mem_row, embed, inner, outer2, norms, ws, fin, fout, down, up):
+    T, D = inputs.shape; M = memory.shape[0]; H = fin.shape[1]; AD = down.shape[1]
+    vm = pl.BlockSpec(memory_space=pltpu.VMEM)
+    any_ = pl.BlockSpec(memory_space=pl.ANY)
+    sds = jax.ShapeDtypeStruct
+    v = lambda *s: pltpu.VMEM(s, bf16)
+    vf = lambda *s: pltpu.VMEM(s, f32)
+    row, mrow, full, one = sds((T, D), bf16), sds((M, D), bf16), sds((T, D), f32), sds((T, 1), f32)
+    S = (PADDED, inner.shape[1])
+    probs, cprobs = (16, T, T + PADDED), (16, T, M)
+    return pl.pallas_call(functools.partial(front_kernel, A, r),
+        out_shape=(sds((8, D, D), bf16), sds((D, 2 * H), bf16), sds((2 * H, D), bf16), sds((D, 4 * AD), bf16), sds((4 * AD, D), bf16),
+            sds(S, f32), sds((PADDED, 2 * D), bf16), sds((8, D), f32), row, row, row, sds(probs, bf16), row, row, full, one, row, mrow, mrow, sds(cprobs, bf16), row,
+            full, row, full, one),
+        in_specs=[vm] * 9 + [any_] * 12, out_specs=(any_,) * 25,
+        scratch_shapes=[v(8, D, D), v(T, D), v(T, D), v(T, D), v(*probs), v(T, D), vf(T, D), v(T, D), vf(T, D), vf(T, 1), v(T, D), v(M, D), v(M, D), v(*cprobs), v(T, D),
+            vf(T, D), v(T, D), vf(T, D), vf(T, 1), vf(T, T + PADDED), vf(T, M),
+            vf(3, *S), vf(3, *S), vf(A, *S), v(PADDED, 128), v(PADDED, 128), v(PADDED, 2 * D), v(8 * A * norms.shape[0], 128), vf(8, D), vf(*S),
+            pltpu.SemaphoreType.DMA((320,)), pltpu.SemaphoreType.DMA((320,))],
+        compiler_params=pltpu.CompilerParams(collective_id=1, has_side_effects=True, vmem_limit_bytes=60 << 20), name="front")(
+            inputs, memory, seg_col, seg_row, mem_row, embed, inner, outer2, norms, *ws, fin, fout, down, up)
+
+
+def exact(l, r, dims):
+    return lax.dot_general(l, r, (dims, ((), ())), precision=lax.Precision.HIGHEST, preferred_element_type=f32)
+
+def back_kernel(A, r, gsec, n1, i1, n2, i2, vecs, ngrad3, q, k, v, probs, cq, ck, cv, cprobs, prows, inputs, memory, att, flow, crossed, slow, blow, ay,
+                tangent, embed, inner, outer2, weights, fi, fo,
+                igrad, mgrad, out, aout, fi_out, fo_out, outer_o, inner_o, embed_o, nsum,
+                ws, gmid, gfirst, og, mid, dcq, dck, dcv, startl, dq, dk, dv, pg,
+                xb, yb, mb, mby, axb, ayb, pb, apb, fib, fob, r1, r2, r3, ra1, ra2, ra3, rfi, rfo, rzi, rzo, rxi, rxo, ob, aob, fib2, fob2,
+                buf, got, zbuf, nbuf, ngot, nz, w0, w1, w2, w3, s0, s1, s2, ssem, rsem):
+    a, b, x, c = place()
+    o = 1 - c
+    core, xp, yp = device(a, b, x, o), device(a, b, 1 - x, c), device(a, 1 - b, x, c)
+    zp = [device((a + j) % A, b, x, c) for j in range(A)]
+    za = a + 1 - 2 * (a % 2)
+    zq = device(za, b, x, c)
+    peers = (core, xp, yp)
+    T, D = gsec.shape
+    M = memory.shape[0]
+    HID = fi.shape[1] // 2
+    Q = fi.shape[0] // 4
+    half = D // 2
+    cp = Copies(ssem, rsem)
+    loads = {}
+    def fetch(slot, w):
+        loads[slot] = cp.local(weights.at[w], ws.at[slot])
+    fetch(0, 7); fetch(1, 5); fetch(2, 3); fetch(3, 4)
+    fown = []
+    for xx in range(2):
+        dq_ = pl.ds(pl.multiple_of((xx * 2 + c) * Q, Q), Q)
+        fown += [cp.local(fi.at[dq_, :], fib.at[xx]), cp.local(fo.at[:, dq_], fob.at[xx])]
+    greet([core, xp, yp] + zp[1:])
+    def offer(srcs, mine, theirs):
+        n = cp.count
+        cp.count += 2
+        def start(keep, give):
+            pltpu.make_async_copy(srcs[keep], mine, ssem.at[n]).start()
+            remote(srcs[give], theirs, ssem.at[n + 1], rsem.at[n], core).start()
+        pl.when(c == 0)(functools.partial(start, 0, 1))
+        pl.when(c == 1)(functools.partial(start, 1, 0))
+        e = remote(srcs[0], theirs, ssem.at[n + 1], rsem.at[n], core)
+        cp.all.append(e)
+        return pltpu.make_async_copy(srcs[0], mine, ssem.at[n]).wait, e.wait_recv
+    lowT, highT = pl.ds(0, T), pl.ds(T, T)
+    waits = {}
+    aw = offer((slow, blow), axb.at[lowT], axb.at[highT]) + offer((ay.at[0], ay.at[1]), ayb.at[lowT], ayb.at[highT])
+    waits[0] = offer((crossed, flow), xb.at[0, lowT], xb.at[0, highT])
+    fcopies = []
+    for xx in range(2):
+        dq_ = pl.ds(pl.multiple_of((xx * 2 + o) * Q, Q), Q)
+        fcopies += [cp(fi.at[dq_, :], rfi.at[xx], core), cp(fo.at[:, dq_], rfo.at[xx], core)]
+    waits[1] = offer((memory, memory), mb.at[pl.ds(0, M)], mb.at[pl.ds(M, M)])
+    waits[2] = offer((att, inputs), xb.at[1, lowT], xb.at[1, highT])
+    waits[3] = offer((inputs, inputs), xb.at[2, lowT], xb.at[2, highT])
+
+    zf, xf, outs = [], [], []
+    def feed0():
+        for e in fown: e.wait()
+        for e in fcopies: e.wait_recv()
+        for xx in range(2):
+            def rows_fi(t):
+                s = pl.ds(t * 32, 32)
+                fib[xx, s, :] = fib[xx, s, :] + rfi[xx, s, :]
+            loop(0, Q // 32, rows_fi)
+            def rows_fo(t):
+                s = pl.ds(t * 64, 64)
+                fob[xx, s, :] = fob[xx, s, :] + rfo[xx, s, :]
+            loop(0, 2 * HID // 64, rows_fo)
+        zf.extend([cp(fib.at[:, :, pl.ds(HID, HID)], rzi, zq), cp(fob.at[:, pl.ds(HID, HID), :], rzo, zq)])
+    def feed1():
+        for e in zf: e.wait_recv()
+        for xx in range(2):
+            def rows_fi(t):
+                s = pl.ds(t * 32, 32)
+                fib[xx, s, pl.ds(0, HID)] = fib[xx, s, pl.ds(0, HID)] + rzi[xx, s, :]
+            loop(0, Q // 32, rows_fi)
+            def rows_fo(t):
+                s = pl.ds(t * 64, 64)
+                fob[xx, s, :] = fob[xx, s, :] + rzo[xx, s, :]
+            loop(0, HID // 64, rows_fo)
+        xf.extend([cp(fib.at[1 - x, :, pl.ds(0, HID)], rxi, xp), cp(fob.at[1 - x, pl.ds(0, HID), :], rxo, xp)])
+    def feed2():
+        for e in xf: e.wait_recv()
+        def rows_fi(t):
+            s = pl.ds(t * 32, 32)
+            fib2[s, :] = fib[x, s, pl.ds(0, HID)].astype(f32) + rxi[s, :].astype(f32)
+        loop(0, Q // 32, rows_fi)
+        def rows_fo(t):
+            s = pl.ds(t * 64, 64)
+            fob2[s, :] = fob[x, s, :].astype(f32) + rxo[s, :].astype(f32)
+        loop(0, HID // 64, rows_fo)
+        outs.extend([cp.local(fib2, fi_out).wait, cp.local(fob2, fo_out).wait])
+
+    first, second, third = {}, {}, {}
+    numbers = {}
+    for i in range(4):
+        for h in range(2):
+            numbers[i, h] = cp.count
+            cp.count += 1
+    def level1(i, h):
+        cols = pl.ds(h * half, half)
+        n = numbers[i, h]
+        if h == 0:
+            return remote(pb.at[i, :, :, 1 - x, :, cols], r1.at[i, h], ssem.at[n], rsem.at[n], xp)
+        return remote(pb.at[i, :, 1 - b, :, :, cols], r1.at[i, h], ssem.at[n], rsem.at[n], yp)
+    def product(i):
+        for h in range(2):
+            def tile(t):
+                cols = pl.ds(pl.multiple_of(h * half + t * 256, 256), 256)
+                if i == 1:
+                    p = dot_left(mb[...], mby[:, cols])
+                else:
+                    n = (0, None, 1, 2)[i]
+                    p = dot_left(xb[n], yb[n, :, cols])
+                pb[i, :, :, :, :, cols] = p.astype(bf16).reshape(A, 2, 2, 2 * r, 256)
+            loop(0, half // 256, tile)
+            level1(i, h).start()
+    for i in range(4):
+        for h in range(2):
+            first[i, h] = level1(i, h)
+            cp.all.append(first[i, h])
+    def compute(i):
+        for e in waits[i]: e()
+        product(i)
+    def one(i, h):
+        def go():
+            cols = pl.ds(h * half, half)
+            first[i, h].wait_recv()
+            def add(side):
+                def row(z):
+                    if h == 0:
+                        pb[i, z, side, x, :, cols] = pb[i, z, side, x, :, cols] + r1[i, h, z, side]
+                    else:
+                        pb[i, z, b, side, :, cols] = pb[i, z, b, side, :, cols] + r1[i, h, z, side]
+                loop(0, A, row)
+            add(1 - b if h == 0 else 1 - x)
+            if h == 0:
+                second[i, h] = cp(pb.at[i, :, 1 - b, x, :, cols], r2.at[i, h], yp)
+            else:
+                second[i, h] = cp(pb.at[i, :, b, 1 - x, :, cols], r2.at[i, h], xp)
+            add(b if h == 0 else x)
+        return go
+    def two(i, h):
+        def go():
+            cols = pl.ds(h * half, half)
+            second[i, h].wait_recv()
+            for j in range(1, A):
+                aj = (a + j) % A
+                pb[i, aj, b, x, :, cols] = pb[i, aj, b, x, :, cols] + r2[i, h, aj]
+                third[i, h, j] = cp(pb.at[i, aj, b, x, :, cols], r3.at[i, h, j - 1], zp[j])
+            pb[i, a, b, x, :, cols] = pb[i, a, b, x, :, cols] + r2[i, h, a]
+        return go
+    def three(i, h):
+        def go():
+            cols = pl.ds(h * half, half)
+            for j in range(1, A): third[i, h, j].wait_recv()
+            t = pb[i, a, b, x, :, cols].astype(f32)
+            for j in range(1, A): t = t + r3[i, h, j - 1].astype(f32)
+            ob[i, :, cols] = t
+            if h == 1:
+                outs.append(cp.local(ob.at[i, pl.ds(pl.multiple_of(c * r, r), r)], out.at[2 * i + c]).wait)
+                outs.append(cp(ob.at[i, pl.ds(pl.multiple_of(o * r, r), r)], out.at[2 * i + c], core).wait_recv)
+        return go
+    def adapt0():
+        for e in aw: e()
+        for t in range(2):
+            apb[t] = dot_left(axb[...], ayb[:, pl.ds(t * 256, 256)]).astype(bf16).reshape(A, 2, D // (2 * A), 256)
+        first["a"] = cp(apb.at[1 - x], ra1, xp)
+    def adapt1():
+        first["a"].wait_recv()
+        def row(z):
+            for s in range(2):
+                apb[x, z, s] = apb[x, z, s] + ra1[z, s]
+        loop(0, A, row)
+        second["a"] = cp(apb.at[x, :, 1 - b], ra2, yp)
+    def adapt2():
+        second["a"].wait_recv()
+        for j in range(1, A):
+            aj = (a + j) % A
+            apb[x, aj, b] = apb[x, aj, b] + ra2[aj]
+            third["a", j] = cp(apb.at[x, aj, b], ra3.at[j - 1], zp[j])
+        apb[x, a, b] = apb[x, a, b] + ra2[a]
+    def adapt3():
+        for j in range(1, A): third["a", j].wait_recv()
+        t = apb[x, a, b].astype(f32)
+        for j in range(1, A): t = t + ra3[j - 1].astype(f32)
+        aob[0] = t[:, :128]
+        aob[1] = t[:, 128:]
+        outs.append(cp.local(aob.at[c], aout.at[c]).wait)
+        outs.append(cp(aob.at[o], aout.at[c], core).wait_recv)
+    small = {}
+    def lanes(start, count): return pl.ds(pl.multiple_of(start * 128, 128), count * 128)
+    def tail0():
+        small["w"] = [cp(pg.at[:, lanes((a + j) % A * 4, 4)], w0.at[j - 1], zp[j]) for j in range(1, A)]
+        small["n"] = [cp(nbuf.at[0], ngot.at[0], core)]
+    def tail_norm(n):
+        def go():
+            for e in small["n"]: e.wait_recv()
+            nbuf[n] = nbuf[n - 1] + ngot[n - 1]
+            small["n"] = [cp(nbuf.at[n], ngot.at[n], peers[n])]
+        return go
+    def tail_norm3():
+        for e in small["n"]: e.wait_recv()
+        nz[a] = nbuf[2] + ngot[2]
+        small["n"] = [cp(nz.at[a], nz.at[a], zp[j]) for j in range(1, A)]
+    def tail_norm4():
+        for e in small["n"]: e.wait_recv()
+        t = nz[0]
+        for n in range(1, A): t = t + nz[n]
+        nsum[...] = t
+    def tail1():
+        t = pg[:, lanes(a * 4, 4)]
+        for j, e in enumerate(small["w"]):
+            e.wait_recv()
+            t = t + w0[j]
+        s0[...] = t
+        small["w"] = [cp(s0.at[:, lanes((1 - b) * 2, 2)], w1, yp)]
+    def tail2():
+        small["w"][0].wait_recv()
+        s1[...] = s0[:, lanes(b * 2, 2)] + w1[...]
+        small["w"] = [cp(s1.at[:, lanes(1 - x, 1)], w2, xp)]
+    def tail3():
+        small["w"][0].wait_recv()
+        s2[...] = s1[:, lanes(x, 1)] + w2[...]
+        small["w"] = [cp(s2, w3, core)]
+    def tail4():
+        small["w"][0].wait_recv()
+        t = s2[...] + w3[...]
+        lane = lax.broadcasted_iota(jnp.int32, t.shape, 1)
+        mine = jnp.where((lane // 64) == c, t, 0.0)
+        buf[0] = exact(mine, outer2[...].astype(f32), ((1,), (1,)))
+        small["w"] = [cp(buf.at[0], got.at[0], core)]
+        grad = exact(tangent[...].astype(bf16).astype(f32), t, ((0,), (0,)))
+        outer_o[...] = jnp.where(c == 0, grad[:, :64], grad[:, 64:])
+    def tail5(n):
+        def go():
+            small["w"][0].wait_recv()
+            buf[n] = buf[n - 1] + got[n - 1]
+            small["w"] = [cp(buf.at[n], got.at[n], peers[n])]
+        return go
+    def tail6():
+        small["w"][0].wait_recv()
+        zbuf[a] = buf[2] + got[2]
+        small["w"] = [cp(zbuf.at[a], zbuf.at[a], zp[j]) for j in range(1, A)]
+    def tail7():
+        for e in small["w"]: e.wait_recv()
+        t = zbuf[0]
+        for n in range(1, A): t = t + zbuf[n]
+        tan = tangent[...]
+        t = t * (1.0 - tan * tan)
+        inner_o[...] = exact(embed[...].astype(f32), t, ((0,), (0,)))
+        embed_o[...] = exact(t, inner[...].astype(f32), ((1,), (1,)))
+    def norm_two():
+        norm_back_into(gsec, n2, i2, vecs[2:3, :], gmid, nbuf.at[0], 2)
+        mid[...] = gmid[...].astype(bf16)
+    def back_project(src, slot, n):
+        def go():
+            s = src[...]
+            loop(2 * n, 2 * n + 2, lambda t: og.__setitem__((slice(None), columns(t)), dot_right(s, ws[slot, columns(t), :]).astype(bf16)))
+        return go
+    def wait_slot(slot):
+        def go(): loads[slot].wait()
+        return go
+    def pair_back(p, grad, qr, kk, vv, pr):
+        cols = columns(p, 128)
+        qs, ks, gs = split_heads(qr[:, cols]), split_heads(kk), split_heads(grad[:, cols])
+        res = None
+        for s in range(2):
+            low = pr[2 * p + s]
+            prob = low.astype(f32)
+            t = prob * dot_right(gs[s], vv)
+            ds = (t - prob * jnp.sum(t, axis=-1, keepdims=True)).astype(bf16)
+            m = (dot(ds, ks[s]), dot_left(ds, qs[s]), dot_left(low, gs[s]))
+            res = m if res is None else tuple(e + f for e, f in zip(res, m))
+        return cols, res[0] * 0.125, res[1] * 0.125, res[2]
+    def cross_back(n):
+        def go():
+            def step(p):
+                cs = columns(p, 128)
+                cols, m1, m2, m3 = pair_back(p, og, cq, ck[:, cs], cv[:, cs], cprobs)
+                dcq[:, cols] = m1.astype(bf16)
+                dck[:, cols] = m2.astype(bf16)
+                dcv[:, cols] = m3.astype(bf16)
+            loop(2 * n, 2 * n + 2, step)
+        return go
+    def self_back(n):
+        def go():
+            def step(p):
+                cs = columns(p, 128)
+                cv_ = pl.ds(pl.multiple_of(D + p * 128, 128), 128)
+                kk = jnp.concatenate([k[:, cs], prows[:, cs]], axis=0)
+                vv = jnp.concatenate([v[:, cs], prows[:, cv_]], axis=0)
+                cols, m1, m2, m3 = pair_back(p, og, q, kk, vv, probs)
+                dq[:, cols] = m1.astype(bf16)
+                dk[:, cols] = m2[:T].astype(bf16)
+                dv[:, cols] = m3[:T].astype(bf16)
+                pg[:, cols] = m2[T:]
+                pg[:, cv_] = m3[T:]
+            loop(2 * n, 2 * n + 2, step)
+        return go
+    def first_grad():
+        s = dcq[...]
+        def step(t):
+            gfirst[:, columns(t)] = gmid[:, columns(t)] + dot_right(s, ws[1, columns(t), :])
+        loop(0, D // 256, step)
+    def norm_one():
+        norm_back_into(gfirst, n1, i1, vecs[0:1, :], gmid, nbuf.at[0], 0)
+        nbuf[0, 4:6, :] = ngrad3[...]
+        nbuf[0, 6:8, :] = jnp.zeros((2, D), f32)
+        startl[...] = gmid[...].astype(bf16)
+    def memory_part(n):
+        def go():
+            def step(t):
+                mgrad[:, columns(t)] = (dot_right(dck[...], ws[3, columns(t), :]) + dot_right(dcv[...], ws[0, columns(t), :])).astype(bf16)
+            loop(2 * n, 2 * n + 2, step)
+        return go
+    def input_part(n):
+        def go():
+            def step(t):
+                s = gmid[:, columns(t)] + dot_right(dq[...], ws[1, columns(t), :]) + dot_right(dk[...], ws[2, columns(t), :]) + dot_right(dv[...], ws[3, columns(t), :])
+                igrad[:, columns(t)] = s.astype(bf16)
+            loop(2 * n, 2 * n + 2, step)
+        return go
+    norm_two()
+    wait_slot(0)()
+    back_project(mid, 0, 0)(); back_project(mid, 0, 1)()
+    fetch(0, 6)
+    adapt0()
+    feed0()
+    cross_back(0)(); cross_back(1)()
+    adapt1()
+    cross_back(2)(); cross_back(3)()
+    waits[0] += offer((mid, dcq), yb.at[0, lowT], yb.at[0, highT])
+    waits[1] += offer((dck, dcv), mby.at[pl.ds(0, M)], mby.at[pl.ds(M, M)])
+    wait_slot(1)()
+    first_grad()
+    compute(0)
+    fetch(1, 0)
+    norm_one()
+    adapt2()
+    compute(1)
+    wait_slot(2)()
+    back_project(startl, 2, 0)(); back_project(startl, 2, 1)()
+    fetch(2, 1)
+    feed1()
+    self_back(0)()
+    one(0, 0)(); one(0, 1)()
+    self_back(1)()
+    one(1, 0)()
+    self_back(2)()
+    one(1, 1)()
+    self_back(3)()
+    waits[2] += offer((startl, dq), yb.at[1, lowT], yb.at[1, highT])
+    waits[3] += offer((dk, dv), yb.at[2, lowT], yb.at[2, highT])
+    tail0()
+    compute(2)
+    two(0, 0)(); two(0, 1)()
+    tail_norm(1)()
+    compute(3)
+    tail1()
+    two(1, 0)(); two(1, 1)()
+    tail_norm(2)()
+    feed2()
+    wait_slot(3)(); wait_slot(0)()
+    tail2()
+    memory_part(0)()
+    one(2, 0)()
+    tail_norm3()
+    one(2, 1)()
+    tail3()
+    memory_part(1)()
+    fetch(3, 2)
+    three(0, 0)(); three(0, 1)()
+    tail_norm4()
+    tail4()
+    one(3, 0)()
+    adapt3()
+    one(3, 1)()
+    tail5(1)()
+    wait_slot(1)(); wait_slot(2)(); wait_slot(3)()
+    two(2, 0)()
+    input_part(0)()
+    tail5(2)()
+    two(2, 1)()
+    input_part(1)()
+    tail6()
+    three(1, 0)(); three(1, 1)()
+    tail7()
+    two(3, 0)(); two(3, 1)()
+    three(2, 0)(); three(2, 1)()
+    three(3, 0)(); three(3, 1)()
+    for e in outs: e()
+    cp.close()
+
+def back(A, r, small, fi_fo):
+    gsec, memory = small[0], small[17]
+    T, D = gsec.shape; M = memory.shape[0]
+    fi, fo = fi_fo[1:]
+    Q, H2 = fi.shape[0] // 4, fi.shape[1]
+    H = H2 // 2
+    half = D // 2
+    v = lambda *s: pltpu.VMEM(s, bf16)
+    vf = lambda *s: pltpu.VMEM(s, f32)
+    any_ = pl.BlockSpec(memory_space=pl.ANY)
+    vm = pl.BlockSpec(memory_space=pltpu.VMEM)
+    sds = jax.ShapeDtypeStruct
+    P_, N = PADDED, (8, D)
+    hid = small[-2].shape[1]
+    S = (P_, hid)
+    return pl.pallas_call(functools.partial(back_kernel, A, r),
+        out_shape=(sds((T, D), bf16), sds((M, D), bf16), sds((8, r, D), f32), sds((2, D // (2 * A), 128), f32), sds((Q, H), f32), sds((H, Q), f32),
+            sds((hid, 64), f32), sds((r, hid), f32), sds((P_, r), f32), sds(N, f32)),
+        in_specs=[vm] * len(small) + [any_] * 3, out_specs=(vm, vm) + (any_,) * 4 + (vm,) * 4,
+        scratch_shapes=[v(4, D, D), vf(T, D), vf(T, D), v(T, D), v(T, D), v(T, D), v(M, D), v(M, D), v(T, D), v(T, D), v(T, D), v(T, D), vf(P_, 2 * D),
+            v(3, 2 * T, D), v(3, 2 * T, D), v(2 * M, D), v(2 * M, D), v(2 * T, D), v(2 * T, 512),
+            v(4, A, 2, 2, 2 * r, D), v(2, A, 2, D // (2 * A), 256), v(2, Q, H2), v(2, H2, Q),
+            v(4, 2, A, 2, 2 * r, half), v(4, 2, A, 2 * r, half), v(4, 2, A - 1, 2 * r, half),
+            v(A, 2, D // (2 * A), 256), v(A, D // (2 * A), 256), v(A - 1, D // (2 * A), 256),
+            v(2, Q, H2), v(2, H2, Q), v(2, Q, H), v(2, H, Q), v(Q, H), v(H, Q),
+            vf(4, 2 * r, D), vf(2, D // (2 * A), 128), vf(Q, H), vf(H, Q),
+            vf(3, *S), vf(3, *S), vf(A, *S), vf(3, *N), vf(3, *N), vf(A, *N), vf(A - 1, P_, 512), vf(P_, 256), vf(P_, 128), vf(P_, 128), vf(P_, 512), vf(P_, 256), vf(P_, 128),
+            pltpu.SemaphoreType.DMA((224,)), pltpu.SemaphoreType.DMA((224,))],
+        compiler_params=pltpu.CompilerParams(collective_id=2, has_side_effects=True, vmem_limit_bytes=63 << 20),
+        name="back")(*small, *fi_fo)
+
+def fast_body(A, inputs, memory, cotangent, segments, memory_segments, query_self, key_self, value_self, output_self,
+              query_cross, key_cross, value_cross, output_cross, self_gain, self_shift, cross_gain, cross_shift,
+              final_gain, final_shift, feed_in, feed_out, adapter_down, adapter_up, prefix_embed, prefix_inner, prefix_outer):
+    r = query_self.shape[0]
+    w, n = lax.axis_index(WIDE), lax.axis_index(NARROW)
+    norms = jnp.pad(jnp.stack([self_gain, self_shift, cross_gain, cross_shift, final_gain, final_shift]), ((0, 10), (0, 0)))
+    norms = jnp.concatenate([norms] * 4, axis=1)
+    outer2 = jnp.concatenate([prefix_outer, prefix_outer], axis=1)
+    embed = jnp.pad(prefix_embed, ((0, PADDED - PREFIX), (0, 0)))
+    (weights, fin2, fout2, down4, up4, tangent, prows, vecs, q, k, v, probs, attended, first_low, n1, i1, cq, ck, cv, cprobs, crossed, second, second_low, n2, i2) = front(
+        A, r, inputs, memory, segments.reshape(-1, 1), segments.reshape(1, -1), memory_segments.reshape(1, -1), embed, prefix_inner, outer2, norms,
+        [query_self, key_self, value_self, output_self, key_cross, query_cross, value_cross, output_cross], feed_in, feed_out, adapter_down, adapter_up)
+    result, grad_second, fi, fo, ay, branch_low, ngrad3 = feed(A, second, cotangent, fin2, fout2, down4, up4, vecs[4:5], vecs[5:6])
+    inputs_grad, memory_grad, sums, adapt, fi_sum, fo_sum, outer_grad, inner_grad, embed_grad, nsum = back(A, r,
+        (grad_second, n1, i1, n2, i2, vecs, ngrad3, q, k, v, probs, cq, ck, cv, cprobs, prows, inputs, memory, attended, first_low, crossed, second_low, branch_low, ay,
+         tangent, embed, prefix_inner, outer2), (weights, fi, fo))
+    ng = lax.dynamic_slice_in_dim(nsum, (w * 4 + n) * r, r, 1)
+    return (result, inputs_grad, memory_grad, sums[5], sums[6], sums[7], sums[4], sums[1], sums[2], sums[3], sums[0],
+            ng[0], ng[1], ng[2], ng[3], ng[4], ng[5], fi_sum, fo_sum, adapt[0], adapt[1].T, embed_grad[:PREFIX], inner_grad, outer_grad)
+
+
 def solution(mesh):
+    wide, narrow = mesh.shape[WIDE], mesh.shape[NARROW]
+    fits = narrow == 4 and wide == 8
+    body = functools.partial(fast_body, wide // 2) if fits else plain_body
     return jax.shard_map(
         body,
         mesh=mesh,
         in_specs=(
-            P(("wide", "narrow"), None),
-            P(("wide", "narrow"), None),
-            P(("wide", "narrow"), None),
-            P(("wide", "narrow")),
-            P(("wide", "narrow")),
-            P(("wide", "narrow"), None),
-            P(("wide", "narrow"), None),
-            P(("wide", "narrow"), None),
-            P(("wide", "narrow"), None),
-            P(("wide", "narrow"), None),
-            P(("wide", "narrow"), None),
-            P(("wide", "narrow"), None),
-            P(("wide", "narrow"), None),
-            P(("wide", "narrow")),
-            P(("wide", "narrow")),
-            P(("wide", "narrow")),
-            P(("wide", "narrow")),
-            P(("wide", "narrow")),
-            P(("wide", "narrow")),
-            P(None, "wide"),
-            P("wide", None),
-            P(None, "narrow"),
-            P("narrow", None),
-            P(None, ("wide", "narrow")),
-            P(("wide", "narrow"), None),
-            P(None, ("wide", "narrow")),
+            P(BOTH, None),
+            P(BOTH, None),
+            P(BOTH, None),
+            P(BOTH),
+            P(BOTH),
+            P(BOTH, None),
+            P(BOTH, None),
+            P(BOTH, None),
+            P(BOTH, None),
+            P(BOTH, None),
+            P(BOTH, None),
+            P(BOTH, None),
+            P(BOTH, None),
+            P(BOTH),
+            P(BOTH),
+            P(BOTH),
+            P(BOTH),
+            P(BOTH),
+            P(BOTH),
+            P(None, WIDE),
+            P(WIDE, None),
+            P(None, NARROW),
+            P(NARROW, None),
+            P(None, BOTH),
+            P(BOTH, None),
+            P(None, BOTH),
         ),
         out_specs=(
-            P(("wide", "narrow"), None),
-            P(("wide", "narrow"), None),
-            P(("wide", "narrow"), None),
-            P(("wide", "narrow"), None),
-            P(("wide", "narrow"), None),
-            P(("wide", "narrow"), None),
-            P(("wide", "narrow"), None),
-            P(("wide", "narrow"), None),
-            P(("wide", "narrow"), None),
-            P(("wide", "narrow"), None),
-            P(("wide", "narrow"), None),
-            P(("wide", "narrow")),
-            P(("wide", "narrow")),
-            P(("wide", "narrow")),
-            P(("wide", "narrow")),
-            P(("wide", "narrow")),
-            P(("wide", "narrow")),
-            P("narrow", "wide"),
-            P("wide", "narrow"),
-            P("wide", "narrow"),
-            P("narrow", "wide"),
-            P(None, ("wide", "narrow")),
-            P(("wide", "narrow"), None),
-            P(None, ("wide", "narrow")),
+            P(BOTH, None),
+            P(BOTH, None),
+            P(BOTH, None),
+            P(BOTH, None),
+            P(BOTH, None),
+            P(BOTH, None),
+            P(BOTH, None),
+            P(BOTH, None),
+            P(BOTH, None),
+            P(BOTH, None),
+            P(BOTH, None),
+            P(BOTH),
+            P(BOTH),
+            P(BOTH),
+            P(BOTH),
+            P(BOTH),
+            P(BOTH),
+            P(NARROW, WIDE),
+            P(WIDE, NARROW),
+            P(WIDE, NARROW),
+            P(NARROW, WIDE),
+            P(None, BOTH),
+            P(BOTH, None),
+            P(None, BOTH),
         ),
         check_vma=False,
     )

time: 2700 us -> 358 us (0.13)
  waiting for transfers between devices: 2330 us -> 0 us
  Pallas kernels: 0 us -> 338 us
  matrix products: 125 us -> 0 us
  blocking collectives: 123 us -> 0 us
  local copies, waits for them, and re-layouts: 74.8 us -> 16.7 us
    reduce_scatter x12 -> x0, waiting for transfers between devices: 886 us -> none  [the longest x1 140 us: body(): lax.psum_scatter(output_one_grad, ('wide', 'narrow'), scatter_dimension=0...]
    unnamed x40 -> x0, waiting for transfers between devices: 864 us -> none
    all_gather x14 -> x0, waiting for transfers between devices: 582 us -> none  [the longest x1 55.7 us: body(): lax.all_gather(value_self, ('wide', 'narrow'), axis=0, tiled=True)]
    pallas_call x0 -> x3, Pallas kernels: none -> 338 us  [the longest x1 139 us: back(): pl.pallas_call(functools.partial(back_kernel, A, r), out_shape=(sds((T, D...]
    dot_general x59 -> x0, matrix products: 123 us -> none  [the longest x12 37.9 us: left_product(): lax.dot_general(left, right, (((0,), (0,)), ((), ())), preferred_element_...]
    unnamed x2 -> x0, blocking collectives: 78.4 us -> none
    unnamed x215 -> x28, local copies, waits for them, and re-layouts: 61.4 us -> 7.51 us
    all_gather x1 -> x0, blocking collectives: 44.2 us -> none  [body(): lax.all_gather(prefix_embed, ('wide', 'narrow'), axis=1, tiled=True)]
  transfers between devices with their start and end apart: 33 -> 0, of which waited for: 30 -> 0; matrix products, arithmetic and copies ran while one was open for 7% -> 0% of each run, Pallas kernels for 0% -> 0%
where the time goes in v2:
time: 358 us; the launch traced here: 357 us
  Pallas kernels  338 us (94%)
  local copies, waits for them, and re-layouts  16.7 us (5%)
    pallas_call x1, Pallas kernels, back(): pl.pallas_call(functools.partial(back_kernel, A, r), out_shape=(sds((T, D...  139 us
    pallas_call x1, Pallas kernels, front(): pl.pallas_call(functools.partial(front_kernel, A, r), out_shape=(sds((8,...  125 us
    pallas_call x1, Pallas kernels, feed(): pl.pallas_call(functools.partial(feed_kernel, A), out_shape=(sds((T, D),...  74.3 us
    unnamed x28, local copies, waits for them, and re-layouts  7.51 us

profile of v2, /device:TPU:0, one launch (start us, length us, event | category | flops | bytes accessed | tf_op | source)
XLA Modules:
  0.0 357.2 jit_solution(4050449276276179061)
XLA Ops:
  0.7 1.0 copy.50
  1.6 0.8 pad_maximum_fusion.outer2
  2.4 1.3 pad.8.embed
  3.7 1.4 copy.52.seg_col
  5.1 0.8 stack.27
  5.9 0.7 pad_maximum_fusion.1.norms
  6.5 124.9 %front.1 = (bf16[8,1024,1024]{2,1,0:T(8,128)(2,1)}, bf16[1024,1024]{1,0:T(8,128)(2,1)}, bf16[1024,1024]{1,0:T(8,128)(2,1)}, bf16[1024,512]{1,0:T(8,128)(2,1)}, b...) custom-call(bf16[128,1024]{1,0:T(8,128)(2,1)} %inputs.3, ...), custom_call_target="tpu_custom_call" | custom-call | tf_op jit(solution)/shard_map/front/pallas_call | solution.py:1015
  131.4 1.4 fusion
  132.8 74.3 %feed_forward.1 = (bf16[128,1024]{1,0:T(8,128)(2,1)}, f32[128,1024]{1,0:T(8,128)}, bf16[1024,1024]{1,0:T(8,128)(2,1)}, bf16[1024,1024]{1,0:T(8,128)(2,1)}, bf16[...) custom-call(f32[128,1024]{1,0:T(8,128)} %get-tuple-element.66.second, ...), custom_call_target="tpu_custom_call" | custom-call | tf_op jit(solution)/shard_map/feed_forward/pallas_call | solution.py:626
  207.1 139.2 %back.1 = (bf16[128,1024]{1,0:T(8,128)(2,1)}, bf16[256,1024]{1,0:T(8,128)(2,1)}, f32[8,32,1024]{2,1,0:T(8,128)}, f32[2,128,128]{2,1,0:T(8,128)}, f32[256,512]{1,...) custom-call(f32[128,1024]{1,0:T(8,128)} %get-tuple-element.73.gsec, ...), custom_call_target="tpu_custom_call" | custom-call | tf_op jit(solution)/shard_map/back/pallas_call | solution.py:1436
  346.4 2.4 slice_bitcast_fusion
  348.8 0.6 slice_bitcast_fusion.8
  349.4 0.7 copy.53
  350.1 0.0 copy-done.3
  350.1 0.8 copy.54
  350.9 0.8 constant_dynamic-slice_fusion
  351.7 0.5 slice_bitcast_fusion.10
  352.2 0.7 copy.62
  352.9 0.7 copy.63
  353.6 0.8 copy.64
  354.4 0.8 copy.65
  355.2 0.8 copy.66
  356.0 0.6 copy.67
  356.6 0.6 copy.68
  (18 shorter events, 0.0 us)
Async XLA Ops:
  346.3 2.4 copy-start.6
  346.3 3.8 %copy-start.3 = (f32[512,64]{1,0:T(8,128)S(1)}, f32[512,64]{1,0:T(8,128)}, u32[]{:S(2)}) copy-start(f32[512,64]{1,0:T(8,128)} %get-tuple-element.131) | copy-start | bytes 393220
  346.3 5.9 %copy-start.4 = (bf16[128,1024]{1,0:T(8,128)(2,1)S(1)}, bf16[128,1024]{1,0:T(8,128)(2,1)}, u32[]{:S(2)}) copy-start(bf16[128,1024]{1,0:T(8,128)(2,1)} %get-tuple-element.174) | copy-start | bytes 786436
  346.3 6.6 %copy-start.5 = (bf16[128,1024]{1,0:T(8,128)(2,1)S(1)}, bf16[128,1024]{1,0:T(8,128)(2,1)}, u32[]{:S(2)}) copy-start(bf16[128,1024]{1,0:T(8,128)(2,1)} %get-tuple-element.175) | copy-start | bytes 786436
  346.3 7.3 %copy-start.2 = (bf16[256,1024]{1,0:T(8,128)(2,1)S(1)}, bf16[256,1024]{1,0:T(8,128)(2,1)}, u32[]{:S(2)}) copy-start(bf16[256,1024]{1,0:T(8,128)(2,1)} %get-tuple-element.176) | copy-start | bytes 1572868
  346.4 8.1 %copy-start.1 = (f32[256,512]{1,0:T(8,128)S(1)}, f32[256,512]{1,0:T(8,128)}, u32[]{:S(2)}) copy-start(f32[256,512]{1,0:T(8,128)} %get-tuple-element.191) | copy-start | bytes 1572868
  348.7 6.5 %copy-start = (f32[512,256]{1,0:T(8,128)S(1)}, f32[512,256]{1,0:T(8,128)}, u32[]{:S(2)}) copy-start(f32[512,256]{1,0:T(8,128)} %get-tuple-element.192) | copy-start | bytes 1572868
  352.2 3.8 %copy-start.8 = (f32[32,32]{1,0:T(8,128)S(1)}, f32[32,32]{1,0:T(8,128)}, u32[]{:S(2)}) copy-start(f32[32,32]{1,0:T(8,128)} %get-tuple-element.105) | copy-start | bytes 12292
  352.2 4.4 %copy-start.7 = (f32[32,512]{1,0:T(8,128)S(1)}, f32[32,512]{1,0:T(8,128)}, u32[]{:S(2)}) copy-start(f32[32,512]{1,0:T(8,128)} %get-tuple-element.196) | copy-start | bytes 196612

commit v3 on v2

--- a/solution.py
+++ b/solution.py
@@ -482,17 +482,24 @@
     s = e * factor
     return inverse * (s - jnp.mean(s, axis=-1, keepdims=True) - n * jnp.mean(s * n, axis=-1, keepdims=True))
 
-def feed_kernel(A, second, cot, fin, fout, down, up, gain, shift, result, gsec, fi, fo, ay, blow, ngrad,
-                rows, brow, hid, slope, gpre, part, q1, q2, q3, bslope, acc, ssem, rsem):
+def feed_kernel(A, second, cot, fin_own, fout_own, fin_two, fout_two, down_ref, up_ref, gain, shift, inputs_h, memory_h, att_h, flow_h, crossed_h,
+                result, gsec, fi_out, fo_out, ay, blow, ngrad, xp0, xatt, xin, xmem, inputs, memory, att, flow, crossed, fin, fout, fi, fo, down, up, rows, brow, hid, slope, gpre, part, q1, q2, q3, bslope, acc, ssem, rsem):
     a, b, x, c = place()
+    o = 1 - c
     yp = device(a, 1 - b, x, c)
     zp = device((a + A // 2) % A, b, x, c)
-    greet([yp, zp])
+    core, xp, dp = device(a, b, x, o), device(a, b, 1 - x, c), device(a, b, 1 - x, o)
     cp = Copies(ssem, rsem)
+    half = fin_own.shape[1]
+    lo, hi = pl.ds(0, half), pl.ds(half, half)
+    loads = [cp.local(fin_own, fin.at[:, lo]), cp.local(fin_two, fin.at[:, hi]), cp.local(fout_own, fout.at[lo]), cp.local(fout_two, fout.at[hi])]
+    staged = [cp.local(src, dst) for src, dst in ((inputs_h, inputs), (memory_h, memory), (att_h, att), (flow_h, flow), (crossed_h, crossed))]
+    greet([yp, zp, core, xp, dp])
     T, D = second.shape
-    NC = 2
+    NC = 4
     R = T // NC
     HID = fin.shape[1]; TW = 256
+    NT = D // TW
 
     def spread(buf):
         zs, ys = [], []
@@ -500,45 +507,112 @@
             s = pl.ds(q * R, R)
             zs.append(cp(buf.at[0, s], buf.at[2, s], zp))
             ys.append(cp(buf.at[0, s], buf.at[1, s], yp))
-        def forward():
-            f = []
-            for q in range(NC):
-                s = pl.ds(q * R, R)
-                zs[q].wait_recv()
-                f.append(cp(buf.at[2, s], buf.at[3, s], yp))
-            return f
-        return zs, ys, forward
-
-    p3_sent = []
-    def collect(level):
-        p3, p1 = [], []
-        for q in range(NC):
-            p3.append(cp(part.at[3, pl.ds(q * R, R)], q3.at[level, pl.ds(q * R, R)], yp))
-        for q in range(NC):
-            p1.append(cp(part.at[1, pl.ds(q * R, R)], q1.at[level, pl.ds(q * R, R)], yp))
+        passed = []
+        def forward(q):
+            s = pl.ds(q * R, R)
+            zs[q].wait_recv()
+            passed.append(cp(buf.at[2, s], buf.at[3, s], yp))
+        return ys, forward, passed
+
+    sums = {}
+    def collect(level, between):
+        between()
         p2 = []
-        for q in range(NC):
-            s = pl.ds(q * R, R)
-            p3[q].wait_recv()
-            part[2, s] = part[2, s] + q3[level, s]
-            p2.append(cp(part.at[2, s], q2.at[level, s], zp))
-        p3_sent.append(p3)
-        return p1, p2
-
-    def gather_up(level, p1, p2):
-        for q in range(NC):
-            s = pl.ds(q * R, R)
-            p1[q].wait_recv(); p2[q].wait_recv()
-            acc[s] = acc[s] + q1[level, s].astype(f32) + q2[level, s].astype(f32)
-        cp.sent(p1 + p2 + p3_sent.pop())
+        for t in range(NT):
+            sums[level, 3, t].wait_recv()
+            part[2, t] = part[2, t] + q3[level, t]
+            p2.append(cp(part.at[2, t], q2.at[level, t], zp))
+        return p2
+
+    def send_part(level, j, t):
+        sums[level, j, t] = cp(part.at[j, t], (q3 if j == 3 else q1).at[level, t], yp)
+
+    def gather_up(level, p2):
+        for t in range(NT):
+            cols = pl.ds(t * TW, TW)
+            sums[level, 1, t].wait_recv(); p2[t].wait_recv()
+            acc[:, cols] = acc[:, cols] + q1[level, t].astype(f32) + q2[level, t].astype(f32)
+        cp.sent(p2 + [sums[level, j, t] for j in (1, 3) for t in range(NT)])
 
     rows[0] = second[...].astype(bf16)
-    zs, ys, forward = spread(rows)
-    for t in range(2):
-        cols = pl.ds(t * 256, 256)
-        g, s = gelu_both(dot(rows[0], down[:, cols]))
-        ay[1, :, cols] = (ADAPT_SCALE * g.astype(bf16).astype(f32)).astype(bf16)
-        bslope[:, cols] = s
+    ys, forward, fw = spread(rows)
+    AD = down_ref.shape[1]
+    n = x * 2 + c
+    nd = pl.ds(pl.multiple_of(n * AD, AD), AD)
+    md = pl.ds(pl.multiple_of((2 - 2 * x + c) * AD, AD), AD)
+    kept, late = [cp.local(down_ref, down.at[:, nd]), cp.local(up_ref, up.at[nd])], []
+    over = [cp(down_ref, down.at[:, nd], xp), cp(up_ref, up.at[nd], xp)]
+    near = [cp(down_ref, down.at[:, nd], core), cp(up_ref, up.at[nd], core)]
+    def rowsn(ref, m, place): return ref.at[pl.ds(pl.multiple_of(place * m, m), m)]
+    def fan(srcs, dst, only=False):
+        k = cp.count
+        cp.count += 4
+        def start(me):
+            own, other = srcs[me], srcs[1 - me]
+            if own is not None:
+                pltpu.make_async_copy(own, rowsn(dst, T, n), ssem.at[k]).start()
+                remote(own, rowsn(dst, T, n), ssem.at[k + 1], rsem.at[k + 1], xp).start()
+            if other is not None:
+                remote(other, rowsn(dst, T, n), ssem.at[k + 2], rsem.at[k + 2], core).start()
+                remote(other, rowsn(dst, T, n), ssem.at[k + 3], rsem.at[k + 3], dp).start()
+        def finish(me):
+            own, other = srcs[me], srcs[1 - me]
+            src = own if own is not None else other
+            ways = [remote(src, rowsn(dst, T, n), ssem.at[k + i], rsem.at[k + i], d) for i, d in ((1, xp), (2, core), (3, dp))]
+            if own is not None:
+                pltpu.make_async_copy(own, rowsn(dst, T, n), ssem.at[k]).wait()
+                ways[0].wait_send()
+                for e in ways: e.wait_recv()
+            if other is not None:
+                ways[1].wait_send(); ways[2].wait_send()
+        pl.when(c == 0)(functools.partial(start, 0))
+        pl.when(c == 1)(functools.partial(start, 1))
+        def done():
+            pl.when(c == 0)(functools.partial(finish, 0))
+            pl.when(c == 1)(functools.partial(finish, 1))
+        return done
+    for e in staged: e.wait()
+    fans = [fan((crossed, flow), xp0), fan((att, None), xatt)]
+    M = memory.shape[0]
+    share = []
+    for src, dst, m in ((inputs, xin, T), (memory, xmem, M)):
+        kept.append(cp.local(src, rowsn(dst, m, n)))
+        near.append(cp(src, rowsn(dst, m, n), core))
+        share.append((cp(src, rowsn(dst, m, n), xp), rowsn(dst, m, 2 - 2 * x + c)))
+    def adapter_weights():
+        kept[0].wait(); kept[1].wait()
+        for e, ref in zip(over, (down.at[:, md], up.at[md])):
+            e.wait_recv()
+            late.append(cp(ref, ref, core))
+        near[0].wait_recv(); near[1].wait_recv()
+        for e in late[:2]: e.wait_recv()
+    def share_on():
+        for e, ref in share:
+            e.wait_recv()
+            late.append(cp(ref, ref, core))
+    def adapter_forward():
+        for t in range(2):
+            cols = pl.ds(t * 256, 256)
+            g, s = gelu_both(dot(rows[0], down[:, cols]))
+            ay[1, :, cols] = (ADAPT_SCALE * g.astype(bf16).astype(f32)).astype(bf16)
+            bslope[:, cols] = s
+        def tile(t, _):
+            cols = pl.ds(pl.multiple_of(t * 256, 256), 256)
+            acc[:, cols] = acc[:, cols] + dot(ay[1], up[:, cols])
+            return 0
+        lax.fori_loop(0, D // 256, tile, 0)
+    def adapter_back():
+        def tile(t, _):
+            cols = pl.ds(pl.multiple_of(t * 256, 256), 256)
+            gbot = bslope[:, cols] * (ADAPT_SCALE * dot_right(brow[0], up[cols, :]))
+            ay[0, :, cols] = gbot.astype(bf16)
+            return 0
+        lax.fori_loop(0, down.shape[1] // 256, tile, 0)
+        def tile2(t, _):
+            cols = pl.ds(pl.multiple_of(t * 256, 256), 256)
+            acc[:, cols] = acc[:, cols] + dot_right(ay[0], down[cols, :])
+            return 0
+        lax.fori_loop(0, D // 256, tile2, 0)
     def enter(j):
         def tile(t, _):
             cols = pl.ds(pl.multiple_of(t * TW, TW), TW)
@@ -547,24 +621,28 @@
             slope[j, :, cols] = s
             return 0
         lax.fori_loop(0, HID // TW, tile, 0)
-        def tile2(t, _):
-            cols = pl.ds(pl.multiple_of(t * TW, TW), TW)
+        for t in range(NT):
+            cols = pl.ds(t * TW, TW)
             p = dot(hid[j], fout[:, cols])
             if j == 0:
-                acc[:, cols] = p + dot(ay[1], up[:, cols])
+                acc[:, cols] = p
             else:
-                part[j, :, cols] = p.astype(bf16)
-            return 0
-        lax.fori_loop(0, D // TW, tile2, 0)
+                part[j, t] = p.astype(bf16)
+                if j != 2: send_part(0, j, t)
+    for e in loads: e.wait()
     enter(0)
     for q in ys: q.wait_recv()
-    fw = forward()
+    forward(0); forward(1)
     enter(1)
+    forward(2); forward(3)
     enter(2)
     for q in fw: q.wait_recv()
     enter(3)
-    p1, p2 = collect(0)
-    gather_up(0, p1, p2)
+    def between():
+        adapter_weights()
+        adapter_forward()
+    p2 = collect(0, between)
+    gather_up(0, p2)
     n3, inv3 = norm(second[...] + acc[...])
     fac = gain[...].astype(f32)
     result[...] = (n3 * fac + shift[...].astype(f32)).astype(bf16)
@@ -572,17 +650,11 @@
     gb = norm_back(e, n3, inv3, fac)
     gbl = gb.astype(bf16)
     brow[0] = gbl
-    zs, ys, forward = spread(brow)
+    ys, forward, fw = spread(brow)
     blow[...] = gbl
     acc[...] = gb
     ngrad[0:1, :] = jnp.sum(e * n3, axis=0, keepdims=True)
     ngrad[1:2, :] = jnp.sum(e, axis=0, keepdims=True)
-    def adapt_tile(t, _):
-        cols = pl.ds(pl.multiple_of(t * 256, 256), 256)
-        gbot = bslope[:, cols] * (ADAPT_SCALE * dot_right(brow[0], up[cols, :]))
-        ay[0, :, cols] = gbot.astype(bf16)
-        return 0
-    lax.fori_loop(0, down.shape[1] // 256, adapt_tile, 0)
     def leave(j):
         def tile(t, _):
             cols = pl.ds(pl.multiple_of(t * TW, TW), TW)
@@ -590,48 +662,56 @@
             gpre[j, :, cols] = (slope[j, :, cols] * gh).astype(bf16)
             return 0
         lax.fori_loop(0, HID // TW, tile, 0)
-        def tile2(t, _):
-            cols = pl.ds(pl.multiple_of(t * TW, TW), TW)
+        for t in range(NT):
+            cols = pl.ds(t * TW, TW)
             p = dot_right(gpre[j], fin[cols, :])
             if j == 0:
-                acc[:, cols] = acc[:, cols] + p + dot_right(ay[0], down[cols, :])
+                acc[:, cols] = acc[:, cols] + p
             else:
-                part[j, :, cols] = p.astype(bf16)
-            return 0
-        lax.fori_loop(0, D // TW, tile2, 0)
+                part[j, t] = p.astype(bf16)
+                if j != 2: send_part(1, j, t)
     leave(0)
     for q in ys: q.wait_recv()
-    fw = forward()
+    forward(0); forward(1)
     leave(1)
+    forward(2); forward(3)
     leave(2)
     for q in fw: q.wait_recv()
     leave(3)
-    p1, p2 = collect(1)
+    p2 = collect(1, adapter_back)
     def wtile(t, _):
         cols = pl.ds(pl.multiple_of(t * TW, TW), TW)
         fi[:, cols] = dot_left(rows[...].reshape(4 * T, D), gpre[:, :, cols].reshape(4 * T, TW)).astype(bf16)
         fo[:, cols] = dot_left(hid[...].reshape(4 * T, HID), brow[:, :, cols].reshape(4 * T, TW)).astype(bf16)
         return 0
     lax.fori_loop(0, HID // TW, wtile, 0)
-    gather_up(1, p1, p2)
+    kept += [cp.local(fi, fi_out), cp.local(fo, fo_out)]
+    share_on()
+    gather_up(1, p2)
     gsec[...] = acc[...]
+    for e in kept[2:]: e.wait()
+    for e in near[2:] + late[2:]: e.wait_recv()
+    for e in fans: e()
     cp.close()
 
-def feed(A, second, cot, fin, fout, down, up, gain, shift):
-    T, D = second.shape; HID = fin.shape[1]; AD = down.shape[1]
+def feed(A, second, cot, fin, fout, fin2, fout2, down, up, gain, shift, inputs, memory, att, flow, crossed):
+    T, D = second.shape; HID = 2 * fin.shape[1]; AD = down.shape[1] * 4; M = memory.shape[0]
     v = lambda *s: pltpu.VMEM(s, bf16)
     vf = lambda *s: pltpu.VMEM(s, f32)
     vm = pl.BlockSpec(memory_space=pltpu.VMEM)
+    any_ = pl.BlockSpec(memory_space=pl.ANY)
     sds = jax.ShapeDtypeStruct
+    four = sds((4 * T, D), bf16)
     return pl.pallas_call(
         functools.partial(feed_kernel, A),
-        out_shape=(sds((T, D), bf16), sds((T, D), f32), sds((D, HID), bf16), sds((HID, D), bf16), sds((2, T, AD), bf16), sds((T, D), bf16), sds((2, D), f32)),
-        in_specs=[vm] * 8, out_specs=(vm,) * 7,
-        scratch_shapes=[v(4, T, D), v(4, T, D), v(4, T, HID), vf(4, T, HID), v(4, T, HID), v(4, T, D),
-            v(2, T, D), v(2, T, D), v(2, T, D), vf(T, AD), vf(T, D),
-            pltpu.SemaphoreType.DMA((64,)), pltpu.SemaphoreType.DMA((64,))],
+        out_shape=(sds((T, D), bf16), sds((T, D), f32), sds((D, HID), bf16), sds((HID, D), bf16), sds((2, T, AD), bf16), sds((T, D), bf16), sds((2, D), f32),
+            four, four, four, sds((4 * M, D), bf16)),
+        in_specs=[vm] * 2 + [any_] * 6 + [vm] * 2 + [any_] * 5, out_specs=(vm,) * 2 + (any_,) * 2 + (vm,) * 3 + (any_,) * 4,
+        scratch_shapes=[v(T, D), v(M, D), v(T, D), v(T, D), v(T, D), v(D, HID), v(HID, D), v(D, HID), v(HID, D), v(D, AD), v(AD, D), v(4, T, D), v(4, T, D), v(4, T, HID), vf(4, T, HID), v(4, T, HID), v(4, D // 256, T, 256),
+            v(2, D // 256, T, 256), v(2, D // 256, T, 256), v(2, D // 256, T, 256), vf(T, AD), vf(T, D),
+            pltpu.SemaphoreType.DMA((128,)), pltpu.SemaphoreType.DMA((128,))],
         compiler_params=pltpu.CompilerParams(collective_id=3, has_side_effects=True, vmem_limit_bytes=60 << 20),
-        name="feed_forward")(second, cot, fin, fout, down, up, gain, shift)
+        name="feed_forward")(second, cot, fin, fout, fin2, fout2, down, up, gain, shift, inputs, memory, att, flow, crossed)
 
 
 NEGATIVE = -1000000000.0
@@ -738,18 +818,23 @@
     ngrad[at + 1:at + 2, :] = jnp.sum(ee, axis=0, keepdims=True)
 
 
+def repeat(n):
+    row = lax.broadcasted_iota(jnp.int32, (n, 128), 0)
+    col = lax.broadcasted_iota(jnp.int32, (n, 128), 1)
+    return jnp.where(row == lax.rem(col, n), 1.0, 0.0).astype(bf16)
+
 def columns(t, tile=256):
     return pl.ds(pl.multiple_of(t * tile, tile), tile)
 
 def loop(start, stop, step):
     lax.fori_loop(start, stop, lambda t, z: (step(t), z)[1], 0)
 
-def front_kernel(A, r, inputs, memory, seg_col, seg_row, mem_row, embed, inner, outer2, norms, *refs):
-    ws, (fin, fout, down, up) = refs[:8], refs[8:12]
-    (wout, fin2, fout2, down4, up4, tangent, prows_o, vecs_o, q_o, k_o, v_o, probs_o, att_o, first_o, n1_o, i1_o, cq_o, ck_o, cv_o, cprobs_o, crossed_o,
-     second_o, slow_o, n2_o, i2_o) = refs[12:37]
+def front_kernel(A, r, inputs, memory, seg_row, mem_row, embed, inner, outer, norms, *refs):
+    ws, (fin, fout) = refs[:8], refs[8:10]
+    (wout, fin2, fout2, tangent, prows_o, vecs_o, q_o, k_o, v_o, probs_o, att_o, first_o, n1_o, i1_o, cq_o, ck_o, cv_o, cprobs_o, crossed_o,
+     second_o, slow_o, n2_o, i2_o) = refs[10:33]
     (g, q, k, v, probs, att, first, flow, n1, i1, cq, ck, cv, cprobs, crossed, second, slow, n2, i2, pen, cpen,
-     buf, got, zbuf, r0, r1, prows, nout, vecs, tan, ssem, rsem) = refs[37:]
+     buf, got, zbuf, r0, r1, prows, nout, vecs, tan, ssem, rsem) = refs[33:]
     a, b, x, c = place()
     core, xp, yp = device(a, b, x, 1 - c), device(a, b, 1 - x, c), device(a, 1 - b, x, c)
     zp = [device((a + j) % A, b, x, c) for j in range(A)]
@@ -759,10 +844,16 @@
     cp = Copies(ssem, rsem)
     T, D = inputs.shape
     pairs = 4
+    small = {}
+    def pre0():
+        zbuf[a] = jnp.zeros(zbuf.shape[1:], f32)
+        zbuf[a, :PREFIX, :] = dot(embed[...], inner[...])
+        small["s"] = [cp(zbuf.at[a], zbuf.at[a], zp[j]) for j in range(1, A)]
+    pre0()
     def row(a_, b_, x_):
         return pl.multiple_of(((a_ * 2 + b_) * 2 + x_) * 2 * r, 2 * r)
     at = pl.ds(pl.multiple_of(row(a, b, x) + c * r, r), r)
-    cut = (pl.ds(0, 3 * D // 8), pl.ds(3 * D // 8, 5 * D // 8))
+    cut = (pl.ds(0, D // 2), pl.ds(D // 2, D // 2))
     def block(i, h, a_, b_, x_):
         return g.at[2 * i + c, pl.ds(row(a_, b_, x_), 2 * r), cut[h]]
     kept = []
@@ -783,71 +874,59 @@
     chip = (a * 2 + b) * 2 + x
     def nrows(start, count): return nout.at[pl.ds(pl.multiple_of(start * G, G), count * G)]
     def lanes(start, count): return prows.at[:, pl.ds(pl.multiple_of(start * 128, 128), count * 128)]
-    nout[pl.ds(pl.multiple_of(me * G, G), G), :] = norms[...]
-    small = {}
+    nout[pl.ds(pl.multiple_of(me * G, G), G), :] = dot(norms[...], repeat(norms.shape[1])).astype(bf16)
     peers = (core, xp, yp)
-    def pre0():
-        small["t"] = dot(embed[...], inner[...])
-        buf[0] = small["t"]
-        small["s"] = [cp(buf.at[0], got.at[0], core), cp(nrows(me, 1), nrows(me, 1), core)]
-    def pre(n):
-        def go():
-            for e in small["s"]: e.wait_recv()
-            buf[n] = buf[n - 1] + got[n - 1]
-            start, count = (me - c, 2) if n == 1 else (me - c - 2 * x, 4)
-            small["s"] = [cp(buf.at[n], got.at[n], peers[n]), cp(nrows(start, count), nrows(start, count), peers[n])]
-        return go
-    def pre3():
+    def settle():
         for e in small["s"]: e.wait_recv()
-        zbuf[a] = buf[2] + got[2]
-        small["s"] = [cp(zbuf.at[a], zbuf.at[a], zp[j]) for j in range(1, A)] + [cp(nrows(a * 8, 8), nrows(a * 8, 8), zp[j]) for j in range(1, A)]
-    def pre4():
-        for e in small["s"]: e.wait_recv()
+    def pre1():
+        settle()
         t = zbuf[0]
         for n in range(1, A): t = t + zbuf[n]
-        t = jnp.tanh(t)
+        buf[0] = t
+        small["s"] = [cp(buf.at[0], got.at[0], core)]
+    def pre2(n):
+        def go():
+            settle()
+            buf[n] = buf[n - 1] + got[n - 1]
+            small["s"] = [cp(buf.at[n], got.at[n], peers[n])]
+        return go
+    def pre4():
+        settle()
+        t = jnp.tanh(buf[2] + got[2])
         tan[...] = t
-        r0[...] = dot(t.astype(bf16), outer2[...]).astype(bf16)
-        small["s"] = [cp(r0, r1, core)]
+        r0[...] = dot(dot_right(t.astype(bf16), outer[...]).astype(bf16), repeat(outer.shape[0])).astype(bf16)
+        small["s"] = [cp(r0, r1, core), cp(nrows(me, 1), nrows(me, 1), core)]
+        kept.append(cp.local(tan, tangent))
+    def pre5():
+        settle()
+        lane = lax.broadcasted_iota(jnp.int32, (PADDED, 128), 1)
+        prows[:, pl.ds(pl.multiple_of(chip * 128, 128), 128)] = jnp.where((lane // 64) == c, r0[...].astype(f32), r1[...].astype(f32)).astype(bf16)
+        small["s"] = [cp(lanes(chip, 1), lanes(chip, 1), xp), cp(nrows(me - c, 2), nrows(me - c, 2), xp)]
+    def pre6():
+        settle()
+        small["s"] = [cp(lanes(chip - x, 2), lanes(chip - x, 2), yp), cp(nrows(me - c - 2 * x, 4), nrows(me - c - 2 * x, 4), yp)]
+    def pre7():
+        settle()
+        small["s"] = [cp(lanes(a * 4, 4), lanes(a * 4, 4), zp[j]) for j in range(1, A)] + [cp(nrows(a * 8, 8), nrows(a * 8, 8), zp[j]) for j in range(1, A)]
+    def pre8():
+        settle()
         lane = lax.broadcasted_iota(jnp.int32, (G, 128), 1) // 32
         for w in range(2 * A):
             s = nout[pl.ds(w * 4 * G, G), :].astype(f32)
             for n in range(1, 4):
                 s = jnp.where(lane == n, nout[pl.ds((w * 4 + n) * G, G), :].astype(f32), s)
             vecs[:, pl.ds(w * 128, 128)] = s[:8]
-        kept.append(cp.local(tan, tangent))
         kept.append(cp.local(vecs, vecs_o))
-    def pre5():
-        small["s"][0].wait_recv()
-        lane = lax.broadcasted_iota(jnp.int32, (PADDED, 128), 1)
-        prows[:, pl.ds(pl.multiple_of(chip * 128, 128), 128)] = jnp.where((lane // 64) == c, r0[...].astype(f32), r1[...].astype(f32)).astype(bf16)
-        small["s"] = [cp(lanes(chip, 1), lanes(chip, 1), xp)]
-    def pre6():
-        small["s"][0].wait_recv()
-        small["s"] = [cp(lanes(chip - x, 2), lanes(chip - x, 2), yp)]
-    def pre7():
-        small["s"][0].wait_recv()
-        small["s"] = [cp(lanes(a * 4, 4), lanes(a * 4, 4), zp[j]) for j in range(1, A)]
-    def pre8():
-        for e in small["s"]: e.wait_recv()
         kept.append(cp.local(prows, prows_o))
-    H, AD = fin.shape[1], down.shape[1]
-    kept += [cp.local(fin, fin2.at[:, pl.ds(0, H)]), cp.local(fout, fout2.at[pl.ds(0, H)])]
-    nd = pl.ds(pl.multiple_of((x * 2 + c) * AD, AD), AD)
-    md = pl.ds(pl.multiple_of((2 - 2 * x + c) * AD, AD), AD)
-    kept += [cp.local(down, down4.at[:, nd]), cp.local(up, up4.at[nd])]
+    H = fin.shape[1]
     feeds, passed = {}, []
     def feed_send(i):
         n = D // 8
         ri = pl.ds(pl.multiple_of(c * (D // 2) + i * n, n), n)
         m = H // 8
         ro = pl.ds(pl.multiple_of(c * (H // 2) + i * m, m), m)
-        ro2 = pl.ds(pl.multiple_of(H + c * (H // 2) + i * m, m), m)
-        feeds[i] = [(cp(fin.at[ri], fin2.at[ri, pl.ds(H, H)], zq), fin2.at[ri, pl.ds(H, H)]),
-                    (cp(fout.at[ro], fout2.at[ro2], zq), fout2.at[ro2])]
-    def adapter_send():
-        feeds["a"] = [(cp(down, down4.at[:, nd], xp), down4.at[:, md]), (cp(up, up4.at[nd], xp), up4.at[md])]
-        passed.extend([cp(down, down4.at[:, nd], core), cp(up, up4.at[nd], core)])
+        feeds[i] = [(cp(fin.at[ri], fin2.at[ri], zq), fin2.at[ri]),
+                    (cp(fout.at[ro], fout2.at[ro], zq), fout2.at[ro])]
     def feed_pass(i):
         for e, ref in feeds[i]:
             e.wait_recv()
@@ -876,15 +955,17 @@
             w = (aj, 1 - b, x) if h == 0 else (aj, b, 1 - x)
             mc[i, h, j].wait_recv()
             lc[i, h, j, 1] = cp(block(i, h, *w), block(i, h, *w), three[h])
-    def fin_wait(i):
-        for j in range(A):
-            for h in range(2):
-                lc[i, h, j, 0].wait_recv(); lc[i, h, j, 1].wait_recv()
-        dc[i] = cp(g.at[2 * i + c], g.at[2 * i + c], core)
-        kept.append(cp.local(g.at[2 * i + c], wout.at[2 * i + c]))
+    per = D // A
+    def finish(i, j):
+        aj = (a + A - j) % A
+        for h in range(2):
+            lc[i, h, j, 0].wait_recv(); lc[i, h, j, 1].wait_recv()
+        ref = g.at[2 * i + c, pl.ds(pl.multiple_of(aj * per, per), per)]
+        dc[i, j] = cp(ref, ref, core)
     def arrive(i):
-        dc[i].wait_recv()
-        kept.append(cp.local(g.at[2 * i + 1 - c], wout.at[2 * i + 1 - c]))
+        for j in range(A): dc[i, j].wait_recv()
+        kept.append(cp.local(g.at[2 * i], wout.at[2 * i]))
+        kept.append(cp.local(g.at[2 * i + 1], wout.at[2 * i + 1]))
     def halves(src, w, out):
         def part(n):
             def go():
@@ -898,8 +979,16 @@
         def go(): kept.append(cp.local(src, dst))
         return go
     def masks():
-        pen[...] = self_mask(seg_col, seg_row)
-        cpen[...] = jnp.where(seg_col[...] == mem_row[...], 0.0, NEGATIVE)
+        row = lax.broadcasted_iota(jnp.int32, (T, T), 0)
+        col = lax.broadcasted_iota(jnp.int32, (T, T), 1)
+        across = jnp.broadcast_to(seg_row[...].astype(f32), (T, T))
+        down = across.T
+        pen[:, :T] = jnp.where((row >= col) & (down == across), 0.0, NEGATIVE)
+        lane = lax.broadcasted_iota(jnp.int32, (T, PADDED), 1)
+        pen[:, T:] = jnp.where(lane < PREFIX, 0.0, NEGATIVE)
+        for n in range(memory.shape[0] // T):
+            span = slice(n * T, (n + 1) * T)
+            cpen[:, span] = jnp.where(down == mem_row[:, span].astype(f32), 0.0, NEGATIVE)
     def softmax(qv, kk, penalty):
         score = jnp.where(penalty[...] < -1.0, NEGATIVE, dot_right(qv, kk) * 0.125)
         e = jnp.exp(score - jnp.max(score, axis=-1, keepdims=True))
@@ -961,38 +1050,56 @@
         3: halves(memory, 6, cv) + [keep(cv, cv_o)] + [cross_mix(n) for n in range(2)] + [keep(crossed, crossed_o)]
            + normed(first, crossed, 7, 2, second, n2, i2, slow) + [keep(second, second_o), keep(slow, slow_o), keep(n2, n2_o), keep(i2, i2_o)],
     }
-    queue = [pre0, pre(1), pre(2), pre3, pre4, pre5, pre6, pre7, pre8]
+    queue = []
     def turn(count=1):
         for _ in range(count):
             if queue: queue.pop(0)()
+    small_steps = [pre1, pre2(1), pre2(2), pre4, pre5, pre6, pre7]
+    def tick():
+        if small_steps: small_steps.pop(0)()
     first_send(0)
-    turn()
+    tick()
     for i in range(pairs):
         if i + 1 < pairs:
             first_send(i + 1)
         feed_send(i)
-        if i == 1:
-            adapter_send()
+        third(i, 0)
+        tick()
         turn()
-        third(i, 0)
+        if i:
+            finish(i - 1, 2)
+            turn()
+        mid(i, 1)
+        tick()
         turn()
-        for j in range(1, A):
-            mid(i, j)
-            turn(1)
         if i:
-            fin_wait(i - 1)
-            feed_pass(i - 1)
+            finish(i - 1, 3)
             turn()
-        for j in range(1, A):
-            third(i, j)
-            turn(1)
+        mid(i, 2)
+        tick()
+        turn()
+        if i: feed_pass(i - 1)
+        mid(i, 3)
+        tick()
+        turn()
+        third(i, 1)
         if i:
             arrive(i - 1)
+            if i == 2: pre8()
             queue += comp[i - 1]
-        turn(3)
-    feed_pass(3); feed_pass("a")
-    turn(6)
-    fin_wait(3)
+        turn()
+        finish(i, 0)
+        turn(2)
+        third(i, 2)
+        turn(2)
+        finish(i, 1)
+        turn(2)
+        third(i, 3)
+        turn(2)
+    feed_pass(3)
+    finish(3, 2)
+    turn(2)
+    finish(3, 3)
     turn(100)
     arrive(3)
     queue += comp[3]
@@ -1002,8 +1109,8 @@
     own_ids = None
     cp.close()
 
-def front(A, r, inputs, memory, seg_col, seg_row, mem_row, embed, inner, outer2, norms, ws, fin, fout, down, up):
-    T, D = inputs.shape; M = memory.shape[0]; H = fin.shape[1]; AD = down.shape[1]
+def front(A, r, inputs, memory, seg_row, mem_row, embed, inner, outer, norms, ws, fin, fout):
+    T, D = inputs.shape; M = memory.shape[0]; H = fin.shape[1]
     vm = pl.BlockSpec(memory_space=pltpu.VMEM)
     any_ = pl.BlockSpec(memory_space=pl.ANY)
     sds = jax.ShapeDtypeStruct
@@ -1013,36 +1120,41 @@
     S = (PADDED, inner.shape[1])
     probs, cprobs = (16, T, T + PADDED), (16, T, M)
     return pl.pallas_call(functools.partial(front_kernel, A, r),
-        out_shape=(sds((8, D, D), bf16), sds((D, 2 * H), bf16), sds((2 * H, D), bf16), sds((D, 4 * AD), bf16), sds((4 * AD, D), bf16),
+        out_shape=(sds((8, D, D), bf16), sds((D, H), bf16), sds((H, D), bf16),
             sds(S, f32), sds((PADDED, 2 * D), bf16), sds((8, D), f32), row, row, row, sds(probs, bf16), row, row, full, one, row, mrow, mrow, sds(cprobs, bf16), row,
             full, row, full, one),
-        in_specs=[vm] * 9 + [any_] * 12, out_specs=(any_,) * 25,
+        in_specs=[vm] * 8 + [any_] * 10, out_specs=(any_,) * 23,
         scratch_shapes=[v(8, D, D), v(T, D), v(T, D), v(T, D), v(*probs), v(T, D), vf(T, D), v(T, D), vf(T, D), vf(T, 1), v(T, D), v(M, D), v(M, D), v(*cprobs), v(T, D),
             vf(T, D), v(T, D), vf(T, D), vf(T, 1), vf(T, T + PADDED), vf(T, M),
             vf(3, *S), vf(3, *S), vf(A, *S), v(PADDED, 128), v(PADDED, 128), v(PADDED, 2 * D), v(8 * A * norms.shape[0], 128), vf(8, D), vf(*S),
             pltpu.SemaphoreType.DMA((320,)), pltpu.SemaphoreType.DMA((320,))],
         compiler_params=pltpu.CompilerParams(collective_id=1, has_side_effects=True, vmem_limit_bytes=60 << 20), name="front")(
-            inputs, memory, seg_col, seg_row, mem_row, embed, inner, outer2, norms, *ws, fin, fout, down, up)
+            inputs, memory, seg_row, mem_row, embed, inner, outer, norms, *ws, fin, fout)
 
 
 def exact(l, r, dims):
     return lax.dot_general(l, r, (dims, ((), ())), precision=lax.Precision.HIGHEST, preferred_element_type=f32)
 
-def back_kernel(A, r, gsec, n1, i1, n2, i2, vecs, ngrad3, q, k, v, probs, cq, ck, cv, cprobs, prows, inputs, memory, att, flow, crossed, slow, blow, ay,
-                tangent, embed, inner, outer2, weights, fi, fo,
-                igrad, mgrad, out, aout, fi_out, fo_out, outer_o, inner_o, embed_o, nsum,
-                ws, gmid, gfirst, og, mid, dcq, dck, dcv, startl, dq, dk, dv, pg,
-                xb, yb, mb, mby, axb, ayb, pb, apb, fib, fob, r1, r2, r3, ra1, ra2, ra3, rfi, rfo, rzi, rzo, rxi, rxo, ob, aob, fib2, fob2,
+def back_kernel(A, r, gsec, n2, i2, vecs, ngrad3, tangent, embed, inner, outer, *refs):
+    late, (slow, blow, ay, weights, fi, fo, xp0, xatt, xin, xmem) = refs[:11], refs[11:21]
+    back_body(A, r, gsec, n2, i2, vecs, ngrad3, tangent, embed, inner, outer, late, slow, blow, ay, weights, fi, fo, xp0, xatt, xin, xmem, *refs[21:])
+
+def back_body(A, r, gsec, n2, i2, vecs, ngrad3, tangent, embed, inner, outer, late, slow, blow, ay, weights, fi, fo, xp0, xatt, xin, xmem,
+                igrad_o, mgrad_o, out, aout, fi_out, fo_out, outer_o, inner_o, embed_o, nsum,
+                igrad, mgrad, cq, ck, cv, cprobs, n1, i1, q, k, v, probs, prows, ws, gmid, gfirst, og, mid, dcq, dck, dcv, startl, dq, dk, dv, pg,
+                xb, yb, mb, mby, axb, ayb, pb, apb, fib, fob, r1, r2, r3, sb, xs, ra1, ra2, ra3, rfi, rfo, rzi, rzo, rxi, rxo, ob, aob, fib2, fob2,
                 buf, got, zbuf, nbuf, ngot, nz, w0, w1, w2, w3, s0, s1, s2, ssem, rsem):
     a, b, x, c = place()
     o = 1 - c
     core, xp, yp = device(a, b, x, o), device(a, b, 1 - x, c), device(a, 1 - b, x, c)
+    dp = device(a, b, 1 - x, o)
+    place_n = x * 2 + c
     zp = [device((a + j) % A, b, x, c) for j in range(A)]
     za = a + 1 - 2 * (a % 2)
     zq = device(za, b, x, c)
     peers = (core, xp, yp)
     T, D = gsec.shape
-    M = memory.shape[0]
+    M = xmem.shape[0] // 4
     HID = fi.shape[1] // 2
     Q = fi.shape[0] // 4
     half = D // 2
@@ -1050,12 +1162,15 @@
     loads = {}
     def fetch(slot, w):
         loads[slot] = cp.local(weights.at[w], ws.at[slot])
+    loaded = [cp.local(src, dst) for src, dst in zip(late, (cq, ck, cv, cprobs, n1, i1, q, k, v, probs, prows))]
+    def ready(start, stop):
+        for e in loaded[start:stop]: e.wait()
     fetch(0, 7); fetch(1, 5); fetch(2, 3); fetch(3, 4)
     fown = []
     for xx in range(2):
         dq_ = pl.ds(pl.multiple_of((xx * 2 + c) * Q, Q), Q)
         fown += [cp.local(fi.at[dq_, :], fib.at[xx]), cp.local(fo.at[:, dq_], fob.at[xx])]
-    greet([core, xp, yp] + zp[1:])
+    greet([core, xp, yp, dp] + zp[1:])
     def offer(srcs, mine, theirs):
         n = cp.count
         cp.count += 2
@@ -1070,14 +1185,42 @@
     lowT, highT = pl.ds(0, T), pl.ds(T, T)
     waits = {}
     aw = offer((slow, blow), axb.at[lowT], axb.at[highT]) + offer((ay.at[0], ay.at[1]), ayb.at[lowT], ayb.at[highT])
-    waits[0] = offer((crossed, flow), xb.at[0, lowT], xb.at[0, highT])
+    xload = cp.count
+    cp.count += 4
+    def load_x(me):
+        pltpu.make_async_copy(xp0, xb.at[0], ssem.at[xload]).start()
+        pltpu.make_async_copy(xmem, mb, ssem.at[xload + 1]).start()
+        pltpu.make_async_copy(xin if me else xatt, xb.at[1], ssem.at[xload + 2]).start()
+        pltpu.make_async_copy(xin, xb.at[2], ssem.at[xload + 3]).start()
+    pl.when(c == 0)(functools.partial(load_x, 0))
+    pl.when(c == 1)(functools.partial(load_x, 1))
+    waits[0] = (pltpu.make_async_copy(xp0, xb.at[0], ssem.at[xload]).wait,)
+    waits[1] = (pltpu.make_async_copy(xmem, mb, ssem.at[xload + 1]).wait,)
+    waits[2] = (pltpu.make_async_copy(xin, xb.at[1], ssem.at[xload + 2]).wait,)
+    waits[3] = (pltpu.make_async_copy(xin, xb.at[2], ssem.at[xload + 3]).wait,)
+    def share(srcs, dst, t):
+        m = srcs[0].shape[0]
+        k = cp.count
+        cp.count += 4
+        wide = half // 2
+        here = pl.ds(pl.multiple_of(x * half + t * wide, wide), wide)
+        there = pl.ds(pl.multiple_of((1 - x) * half + t * wide, wide), wide)
+        spot = dst.at[pl.ds(pl.multiple_of(place_n * m, m), m), pl.ds(t * wide, wide)]
+        def start(me):
+            own, other = srcs[me], srcs[1 - me]
+            remote(own.at[:, there], spot, ssem.at[k + 1], rsem.at[k + 1], xp).start()
+            remote(other.at[:, there], spot, ssem.at[k + 3], rsem.at[k + 3], dp).start()
+            remote(other.at[:, here], spot, ssem.at[k + 2], rsem.at[k + 2], core).start()
+            pltpu.make_async_copy(own.at[:, here], spot, ssem.at[k]).start()
+        pl.when(c == 0)(functools.partial(start, 0))
+        pl.when(c == 1)(functools.partial(start, 1))
+        ways = [remote(srcs[0].at[:, here], spot, ssem.at[k + i], rsem.at[k + i], d) for i, d in ((1, xp), (2, core), (3, dp))]
+        cp.all.extend(ways)
+        return (pltpu.make_async_copy(srcs[0].at[:, here], spot, ssem.at[k]).wait,) + tuple(e.wait_recv for e in ways)
     fcopies = []
     for xx in range(2):
         dq_ = pl.ds(pl.multiple_of((xx * 2 + o) * Q, Q), Q)
         fcopies += [cp(fi.at[dq_, :], rfi.at[xx], core), cp(fo.at[:, dq_], rfo.at[xx], core)]
-    waits[1] = offer((memory, memory), mb.at[pl.ds(0, M)], mb.at[pl.ds(M, M)])
-    waits[2] = offer((att, inputs), xb.at[1, lowT], xb.at[1, highT])
-    waits[3] = offer((inputs, inputs), xb.at[2, lowT], xb.at[2, highT])
 
     zf, xf, outs = [], [], []
     def feed0():
@@ -1117,73 +1260,57 @@
         loop(0, HID // 64, rows_fo)
         outs.extend([cp.local(fib2, fi_out).wait, cp.local(fob2, fo_out).wait])
 
-    first, second, third = {}, {}, {}
+    first, second, third, fourth = {}, {}, {}, {}
+    wide = half // 2
     numbers = {}
     for i in range(4):
-        for h in range(2):
-            numbers[i, h] = cp.count
+        for t in range(2):
+            numbers[i, t] = cp.count
             cp.count += 1
-    def level1(i, h):
-        cols = pl.ds(h * half, half)
-        n = numbers[i, h]
-        if h == 0:
-            return remote(pb.at[i, :, :, 1 - x, :, cols], r1.at[i, h], ssem.at[n], rsem.at[n], xp)
-        return remote(pb.at[i, :, 1 - b, :, :, cols], r1.at[i, h], ssem.at[n], rsem.at[n], yp)
-    def product(i):
-        for h in range(2):
-            def tile(t):
-                cols = pl.ds(pl.multiple_of(h * half + t * 256, 256), 256)
-                if i == 1:
-                    p = dot_left(mb[...], mby[:, cols])
-                else:
-                    n = (0, None, 1, 2)[i]
-                    p = dot_left(xb[n], yb[n, :, cols])
-                pb[i, :, :, :, :, cols] = p.astype(bf16).reshape(A, 2, 2, 2 * r, 256)
-            loop(0, half // 256, tile)
-            level1(i, h).start()
+    def level1(i, t):
+        n = numbers[i, t]
+        return remote(pb.at[i, t, :, 1 - b], r1.at[i, t], ssem.at[n], rsem.at[n], yp)
     for i in range(4):
-        for h in range(2):
-            first[i, h] = level1(i, h)
-            cp.all.append(first[i, h])
-    def compute(i):
-        for e in waits[i]: e()
-        product(i)
-    def one(i, h):
+        for t in range(2):
+            first[i, t] = level1(i, t)
+            cp.all.append(first[i, t])
+    def compute(i, t):
+        if t == 0:
+            for e in waits[i]: e()
+        for e in shared[i, t]: e()
+        cols = pl.ds(t * wide, wide)
+        n = (0, None, 1, 2)[i]
+        def rows(u):
+            d = columns(u)
+            p = dot_left(mb[:, d], mby[:, cols]) if i == 1 else dot_left(xb[n, :, d], yb[n, :, cols])
+            pb[i, t, u] = p.astype(bf16).reshape(2, 2, 2 * r, wide)
+        loop(0, A, rows)
+        level1(i, t).start()
+    def one(i, t):
         def go():
-            cols = pl.ds(h * half, half)
-            first[i, h].wait_recv()
-            def add(side):
-                def row(z):
-                    if h == 0:
-                        pb[i, z, side, x, :, cols] = pb[i, z, side, x, :, cols] + r1[i, h, z, side]
-                    else:
-                        pb[i, z, b, side, :, cols] = pb[i, z, b, side, :, cols] + r1[i, h, z, side]
-                loop(0, A, row)
-            add(1 - b if h == 0 else 1 - x)
-            if h == 0:
-                second[i, h] = cp(pb.at[i, :, 1 - b, x, :, cols], r2.at[i, h], yp)
-            else:
-                second[i, h] = cp(pb.at[i, :, b, 1 - x, :, cols], r2.at[i, h], xp)
-            add(b if h == 0 else x)
-        return go
-    def two(i, h):
-        def go():
-            cols = pl.ds(h * half, half)
-            second[i, h].wait_recv()
+            first[i, t].wait_recv()
             for j in range(1, A):
                 aj = (a + j) % A
-                pb[i, aj, b, x, :, cols] = pb[i, aj, b, x, :, cols] + r2[i, h, aj]
-                third[i, h, j] = cp(pb.at[i, aj, b, x, :, cols], r3.at[i, h, j - 1], zp[j])
-            pb[i, a, b, x, :, cols] = pb[i, a, b, x, :, cols] + r2[i, h, a]
+                pb[i, t, aj, b] = pb[i, t, aj, b] + r1[i, t, aj]
+                third[i, t, j] = cp(pb.at[i, t, aj, b], r2.at[i, t, j - 1], zp[j])
+            pb[i, t, a, b] = pb[i, t, a, b] + r1[i, t, a]
         return go
-    def three(i, h):
+    def two(i, t):
         def go():
-            cols = pl.ds(h * half, half)
-            for j in range(1, A): third[i, h, j].wait_recv()
-            t = pb[i, a, b, x, :, cols].astype(f32)
-            for j in range(1, A): t = t + r3[i, h, j - 1].astype(f32)
-            ob[i, :, cols] = t
-            if h == 1:
+            for j in range(1, A): third[i, t, j].wait_recv()
+            for s in (1 - x, x):
+                e = pb[i, t, a, b, s].astype(f32)
+                for j in range(1, A): e = e + r2[i, t, j - 1, s].astype(f32)
+                sb[i, t, s] = e
+            xs[i, t] = sb[i, t, 1 - x].astype(bf16)
+            fourth[i, t] = cp(xs.at[i, t], r3.at[i, t], xp)
+        return go
+    def three(i, t):
+        def go():
+            fourth[i, t].wait_recv()
+            ob[i, :, pl.ds(pl.multiple_of(x * half + t * wide, wide), wide)] = sb[i, t, x]
+            ob[i, :, pl.ds(pl.multiple_of((1 - x) * half + t * wide, wide), wide)] = r3[i, t].astype(f32)
+            if t == 1:
                 outs.append(cp.local(ob.at[i, pl.ds(pl.multiple_of(c * r, r), r)], out.at[2 * i + c]).wait)
                 outs.append(cp(ob.at[i, pl.ds(pl.multiple_of(o * r, r), r)], out.at[2 * i + c], core).wait_recv)
         return go
@@ -1216,9 +1343,10 @@
         outs.append(cp(aob.at[o], aout.at[c], core).wait_recv)
     small = {}
     def lanes(start, count): return pl.ds(pl.multiple_of(start * 128, 128), count * 128)
+    def tail_norm0():
+        small["n"] = [cp(nbuf.at[0], ngot.at[0], core)]
     def tail0():
         small["w"] = [cp(pg.at[:, lanes((a + j) % A * 4, 4)], w0.at[j - 1], zp[j]) for j in range(1, A)]
-        small["n"] = [cp(nbuf.at[0], ngot.at[0], core)]
     def tail_norm(n):
         def go():
             for e in small["n"]: e.wait_recv()
@@ -1252,12 +1380,10 @@
     def tail4():
         small["w"][0].wait_recv()
         t = s2[...] + w3[...]
-        lane = lax.broadcasted_iota(jnp.int32, t.shape, 1)
-        mine = jnp.where((lane // 64) == c, t, 0.0)
-        buf[0] = exact(mine, outer2[...].astype(f32), ((1,), (1,)))
+        mine = jnp.where(c == 0, t[:, :64], t[:, 64:])
+        buf[0] = exact(mine, outer[...].astype(f32), ((1,), (0,)))
         small["w"] = [cp(buf.at[0], got.at[0], core)]
-        grad = exact(tangent[...].astype(bf16).astype(f32), t, ((0,), (0,)))
-        outer_o[...] = jnp.where(c == 0, grad[:, :64], grad[:, 64:])
+        outer_o[...] = exact(mine, tangent[...].astype(bf16).astype(f32), ((0,), (0,)))
     def tail5(n):
         def go():
             small["w"][0].wait_recv()
@@ -1274,8 +1400,8 @@
         for n in range(1, A): t = t + zbuf[n]
         tan = tangent[...]
         t = t * (1.0 - tan * tan)
-        inner_o[...] = exact(embed[...].astype(f32), t, ((0,), (0,)))
-        embed_o[...] = exact(t, inner[...].astype(f32), ((1,), (1,)))
+        inner_o[...] = exact(embed[...].astype(f32), t[:PREFIX], ((0,), (0,)))
+        embed_o[...] = exact(t[:PREFIX], inner[...].astype(f32), ((1,), (1,)))
     def norm_two():
         norm_back_into(gsec, n2, i2, vecs[2:3, :], gmid, nbuf.at[0], 2)
         mid[...] = gmid[...].astype(bf16)
@@ -1307,7 +1433,7 @@
                 dcq[:, cols] = m1.astype(bf16)
                 dck[:, cols] = m2.astype(bf16)
                 dcv[:, cols] = m3.astype(bf16)
-            loop(2 * n, 2 * n + 2, step)
+            for p in range(2 * n, 2 * n + 2): step(p)
         return go
     def self_back(n):
         def go():
@@ -1322,7 +1448,7 @@
                 dv[:, cols] = m3[:T].astype(bf16)
                 pg[:, cols] = m2[T:]
                 pg[:, cv_] = m3[T:]
-            loop(2 * n, 2 * n + 2, step)
+            for p in range(2 * n, 2 * n + 2): step(p)
         return go
     def first_grad():
         s = dcq[...]
@@ -1347,81 +1473,93 @@
                 igrad[:, columns(t)] = s.astype(bf16)
             loop(2 * n, 2 * n + 2, step)
         return go
+    shared = {}
+    def spread(i, srcs, dst):
+        for t in range(2): shared[i, t] = share(srcs, dst, t)
     norm_two()
     wait_slot(0)()
     back_project(mid, 0, 0)(); back_project(mid, 0, 1)()
     fetch(0, 6)
     adapt0()
+    ready(0, 4)
+    cross_back(0)()
     feed0()
-    cross_back(0)(); cross_back(1)()
-    adapt1()
-    cross_back(2)(); cross_back(3)()
-    waits[0] += offer((mid, dcq), yb.at[0, lowT], yb.at[0, highT])
-    waits[1] += offer((dck, dcv), mby.at[pl.ds(0, M)], mby.at[pl.ds(M, M)])
+    cross_back(1)(); cross_back(2)(); cross_back(3)()
+    spread(0, (mid, dcq), yb.at[0])
+    spread(1, (dck, dcv), mby)
     wait_slot(1)()
     first_grad()
-    compute(0)
     fetch(1, 0)
+    ready(4, 6)
     norm_one()
-    adapt2()
-    compute(1)
+    tail_norm0()
     wait_slot(2)()
     back_project(startl, 2, 0)(); back_project(startl, 2, 1)()
     fetch(2, 1)
+    ready(6, 11)
+    self_back(0)()
+    compute(0, 0)
+    tail_norm(1)()
+    self_back(1)()
+    compute(0, 1)
+    adapt1()
+    self_back(2)()
+    compute(1, 0)
+    tail_norm(2)()
+    self_back(3)()
+    tail0()
+    spread(2, (startl, dq), yb.at[1])
+    spread(3, (dk, dv), yb.at[2])
+    compute(1, 1)
+    one(0, 0)(); one(0, 1)()
+    tail_norm3()
+    compute(2, 0); compute(2, 1)
+    tail1()
+    one(1, 0)()
+    compute(3, 0); compute(3, 1)
+    adapt2()
+    one(1, 1)()
+    tail2()
+    tail_norm4()
+    two(0, 0)(); two(0, 1)()
+    wait_slot(3)(); wait_slot(0)()
+    memory_part(0)()
     feed1()
-    self_back(0)()
-    one(0, 0)(); one(0, 1)()
-    self_back(1)()
-    one(1, 0)()
-    self_back(2)()
-    one(1, 1)()
-    self_back(3)()
-    waits[2] += offer((startl, dq), yb.at[1, lowT], yb.at[1, highT])
-    waits[3] += offer((dk, dv), yb.at[2, lowT], yb.at[2, highT])
-    tail0()
-    compute(2)
-    two(0, 0)(); two(0, 1)()
-    tail_norm(1)()
-    compute(3)
-    tail1()
-    two(1, 0)(); two(1, 1)()
-    tail_norm(2)()
-    feed2()
-    wait_slot(3)(); wait_slot(0)()
-    tail2()
-    memory_part(0)()
-    one(2, 0)()
-    tail_norm3()
-    one(2, 1)()
     tail3()
     memory_part(1)()
+    outs.append(cp.local(mgrad, mgrad_o).wait)
     fetch(3, 2)
+    one(2, 0)()
+    two(1, 0)()
+    tail4()
+    one(2, 1)()
+    two(1, 1)()
+    tail5(1)()
     three(0, 0)(); three(0, 1)()
-    tail_norm4()
-    tail4()
-    one(3, 0)()
-    adapt3()
-    one(3, 1)()
-    tail5(1)()
     wait_slot(1)(); wait_slot(2)(); wait_slot(3)()
-    two(2, 0)()
     input_part(0)()
     tail5(2)()
-    two(2, 1)()
+    one(3, 0)()
     input_part(1)()
+    outs.append(cp.local(igrad, igrad_o).wait)
     tail6()
+    two(2, 0)()
+    one(3, 1)()
+    feed2()
+    adapt3()
     three(1, 0)(); three(1, 1)()
+    two(2, 1)(); two(3, 0)()
     tail7()
-    two(3, 0)(); two(3, 1)()
     three(2, 0)(); three(2, 1)()
+    two(3, 1)()
     three(3, 0)(); three(3, 1)()
     for e in outs: e()
     cp.close()
 
-def back(A, r, small, fi_fo):
-    gsec, memory = small[0], small[17]
-    T, D = gsec.shape; M = memory.shape[0]
-    fi, fo = fi_fo[1:]
+def back(A, r, first, late, rest):
+    gsec = first[0]
+    T, D = gsec.shape; M = rest[-1].shape[0] // 4
+    fi, fo = rest[4:6]
     Q, H2 = fi.shape[0] // 4, fi.shape[1]
     H = H2 // 2
     half = D // 2
@@ -1431,43 +1569,62 @@
     vm = pl.BlockSpec(memory_space=pltpu.VMEM)
     sds = jax.ShapeDtypeStruct
     P_, N = PADDED, (8, D)
-    hid = small[-2].shape[1]
+    hid = first[-2].shape[1]
     S = (P_, hid)
     return pl.pallas_call(functools.partial(back_kernel, A, r),
         out_shape=(sds((T, D), bf16), sds((M, D), bf16), sds((8, r, D), f32), sds((2, D // (2 * A), 128), f32), sds((Q, H), f32), sds((H, Q), f32),
-            sds((hid, 64), f32), sds((r, hid), f32), sds((P_, r), f32), sds(N, f32)),
-        in_specs=[vm] * len(small) + [any_] * 3, out_specs=(vm, vm) + (any_,) * 4 + (vm,) * 4,
-        scratch_shapes=[v(4, D, D), vf(T, D), vf(T, D), v(T, D), v(T, D), v(T, D), v(M, D), v(M, D), v(T, D), v(T, D), v(T, D), v(T, D), vf(P_, 2 * D),
-            v(3, 2 * T, D), v(3, 2 * T, D), v(2 * M, D), v(2 * M, D), v(2 * T, D), v(2 * T, 512),
-            v(4, A, 2, 2, 2 * r, D), v(2, A, 2, D // (2 * A), 256), v(2, Q, H2), v(2, H2, Q),
-            v(4, 2, A, 2, 2 * r, half), v(4, 2, A, 2 * r, half), v(4, 2, A - 1, 2 * r, half),
+            sds((64, hid), f32), sds((r, hid), f32), sds((PREFIX, r), f32), sds(N, f32)),
+        in_specs=[vm] * len(first) + [any_] * (len(late) + len(rest)), out_specs=(any_,) * 6 + (vm,) * 4,
+        scratch_shapes=[v(T, D), v(M, D)] + [pltpu.VMEM(e.shape, e.dtype) for e in late] + [v(4, D, D), vf(T, D), vf(T, D), v(T, D), v(T, D), v(T, D), v(M, D), v(M, D), v(T, D), v(T, D), v(T, D), v(T, D), vf(P_, 2 * D),
+            v(3, 4 * T, D), v(3, 4 * T, half), v(4 * M, D), v(4 * M, half), v(2 * T, D), v(2 * T, 512),
+            v(4, 2, A, 2, 2, 2 * r, half // 2), v(2, A, 2, D // (2 * A), 256), v(2, Q, H2), v(2, H2, Q),
+            v(4, 2, A, 2, 2 * r, half // 2), v(4, 2, A - 1, 2, 2 * r, half // 2), v(4, 2, 2 * r, half // 2), vf(4, 2, 2, 2 * r, half // 2), v(4, 2, 2 * r, half // 2),
             v(A, 2, D // (2 * A), 256), v(A, D // (2 * A), 256), v(A - 1, D // (2 * A), 256),
             v(2, Q, H2), v(2, H2, Q), v(2, Q, H), v(2, H, Q), v(Q, H), v(H, Q),
             vf(4, 2 * r, D), vf(2, D // (2 * A), 128), vf(Q, H), vf(H, Q),
             vf(3, *S), vf(3, *S), vf(A, *S), vf(3, *N), vf(3, *N), vf(A, *N), vf(A - 1, P_, 512), vf(P_, 256), vf(P_, 128), vf(P_, 128), vf(P_, 512), vf(P_, 256), vf(P_, 128),
             pltpu.SemaphoreType.DMA((224,)), pltpu.SemaphoreType.DMA((224,))],
         compiler_params=pltpu.CompilerParams(collective_id=2, has_side_effects=True, vmem_limit_bytes=63 << 20),
-        name="back")(*small, *fi_fo)
+        name="back")(*first, *late, *rest)
 
 def fast_body(A, inputs, memory, cotangent, segments, memory_segments, query_self, key_self, value_self, output_self,
               query_cross, key_cross, value_cross, output_cross, self_gain, self_shift, cross_gain, cross_shift,
               final_gain, final_shift, feed_in, feed_out, adapter_down, adapter_up, prefix_embed, prefix_inner, prefix_outer):
     r = query_self.shape[0]
     w, n = lax.axis_index(WIDE), lax.axis_index(NARROW)
-    norms = jnp.pad(jnp.stack([self_gain, self_shift, cross_gain, cross_shift, final_gain, final_shift]), ((0, 10), (0, 0)))
-    norms = jnp.concatenate([norms] * 4, axis=1)
-    outer2 = jnp.concatenate([prefix_outer, prefix_outer], axis=1)
-    embed = jnp.pad(prefix_embed, ((0, PADDED - PREFIX), (0, 0)))
-    (weights, fin2, fout2, down4, up4, tangent, prows, vecs, q, k, v, probs, attended, first_low, n1, i1, cq, ck, cv, cprobs, crossed, second, second_low, n2, i2) = front(
-        A, r, inputs, memory, segments.reshape(-1, 1), segments.reshape(1, -1), memory_segments.reshape(1, -1), embed, prefix_inner, outer2, norms,
-        [query_self, key_self, value_self, output_self, key_cross, query_cross, value_cross, output_cross], feed_in, feed_out, adapter_down, adapter_up)
-    result, grad_second, fi, fo, ay, branch_low, ngrad3 = feed(A, second, cotangent, fin2, fout2, down4, up4, vecs[4:5], vecs[5:6])
-    inputs_grad, memory_grad, sums, adapt, fi_sum, fo_sum, outer_grad, inner_grad, embed_grad, nsum = back(A, r,
-        (grad_second, n1, i1, n2, i2, vecs, ngrad3, q, k, v, probs, cq, ck, cv, cprobs, prows, inputs, memory, attended, first_low, crossed, second_low, branch_low, ay,
-         tangent, embed, prefix_inner, outer2), (weights, fi, fo))
+    blank = jnp.zeros_like(self_gain)
+    norms = jnp.stack([self_gain, self_shift, cross_gain, cross_shift, final_gain, final_shift] + [blank] * 10)
+    (weights, fin2, fout2, tangent, prows, vecs, q, k, v, probs, attended, first_low, n1, i1, cq, ck, cv, cprobs, crossed, second, second_low, n2, i2) = front(
+        A, r, inputs, memory, segments.reshape(1, -1), memory_segments.reshape(1, -1), prefix_embed, prefix_inner, prefix_outer.T, norms,
+        [query_self, key_self, value_self, output_self, key_cross, query_cross, value_cross, output_cross], feed_in, feed_out)
+    result, grad_second, fi, fo, ay, branch_low, ngrad3, xp0, xatt, xin, xmem = feed(
+        A, second, cotangent, feed_in, feed_out, fin2, fout2, adapter_down, adapter_up, vecs[4:5], vecs[5:6], inputs, memory, attended, first_low, crossed)
+    igrad, mgrad, sums, adapt, fi_sum, fo_sum, outer_grad, inner_grad, embed_grad, nsum = back(A, r,
+        (grad_second, n2, i2, vecs, ngrad3, tangent, prefix_embed, prefix_inner, prefix_outer.T), (cq, ck, cv, cprobs, n1, i1, q, k, v, probs, prows),
+        (second_low, branch_low, ay, weights, fi, fo, xp0, xatt, xin, xmem))
     ng = lax.dynamic_slice_in_dim(nsum, (w * 4 + n) * r, r, 1)
-    return (result, inputs_grad, memory_grad, sums[5], sums[6], sums[7], sums[4], sums[1], sums[2], sums[3], sums[0],
-            ng[0], ng[1], ng[2], ng[3], ng[4], ng[5], fi_sum, fo_sum, adapt[0], adapt[1].T, embed_grad[:PREFIX], inner_grad, outer_grad)
+    whole = deliver(result, igrad, mgrad, sums, fi_sum, fo_sum, outer_grad, inner_grad, embed_grad, adapt)
+    return whole[:11] + tuple(ng[k] for k in range(6)) + whole[11:17] + (whole[17].T,)
+
+
+def deliver_kernel(result, igrad, mgrad, sums, fi, fo, outer, inner, embed, adapt, *outs):
+    order = (5, 6, 7, 4, 1, 2, 3, 0)
+    for dst, src in zip(outs[:3], (result, igrad, mgrad)): dst[...] = src[...]
+    for dst, k in zip(outs[3:11], order): dst[...] = sums[k]
+    for dst, src in zip(outs[11:13] + outs[15:], (fi, fo, embed, inner, outer)): dst[...] = src[...]
+    outs[13][...] = adapt[0]
+    outs[14][...] = adapt[1].T
+
+
+def deliver(result, igrad, mgrad, sums, fi, fo, outer, inner, embed, adapt):
+    like = lambda e: jax.ShapeDtypeStruct(e.shape, e.dtype)
+    row = jax.ShapeDtypeStruct(sums.shape[1:], f32)
+    square = jax.ShapeDtypeStruct(adapt.shape[1:], f32)
+    vm = pl.BlockSpec(memory_space=pltpu.VMEM)
+    return pl.pallas_call(deliver_kernel,
+        out_shape=(like(result), like(igrad), like(mgrad)) + (row,) * 8 + (like(fi), like(fo), square, square, like(embed), like(inner), like(outer)),
+        in_specs=[vm] * 10, out_specs=(vm,) * 18, compiler_params=pltpu.CompilerParams(vmem_limit_bytes=60 << 20),
+        name="deliver")(result, igrad, mgrad, sums, fi, fo, outer, inner, embed, adapt)
 
 
 def solution(mesh):

time: 358 us -> 303 us (0.85)
  Pallas kernels: 338 us -> 298 us
  local copies, waits for them, and re-layouts: 16.7 us -> 4.65 us
    pallas_call x1, Pallas kernels: 139 us -> 111 us  [back(): pl.pallas_call(functools.partial(back_kernel, A, r), out_shape=(sds((T, D...]
    pallas_call x1, Pallas kernels: 125 us -> 101 us  [front(): pl.pallas_call(functools.partial(front_kernel, A, r), out_shape=(sds((8,...]
    pallas_call x1, Pallas kernels: 74.3 us -> 82.6 us  [feed(): pl.pallas_call(functools.partial(feed_kernel, A), out_shape=(sds((T, D),...]
    unnamed x28 -> x0, local copies, waits for them, and re-layouts: 7.51 us -> none
    pallas_call x0 -> x1, Pallas kernels: none -> 3.73 us  [deliver(): pl.pallas_call(deliver_kernel, out_shape=(like(result), like(igrad), like...]
where the time goes in v3:
time: 303 us
  Pallas kernels  298 us (98%)
  local copies, waits for them, and re-layouts  4.65 us (2%)
    pallas_call x1, Pallas kernels, back(): pl.pallas_call(functools.partial(back_kernel, A, r), out_shape=(sds((T, D...  111 us
    pallas_call x1, Pallas kernels, front(): pl.pallas_call(functools.partial(front_kernel, A, r), out_shape=(sds((8,...  101 us
    pallas_call x1, Pallas kernels, feed(): pl.pallas_call(functools.partial(feed_kernel, A), out_shape=(sds((T, D),...  82.6 us

profile of v3, /device:TPU:0, one launch (start us, length us, event | category | flops | bytes accessed | tf_op | source)
XLA Modules:
  0.0 303.0 jit_solution(3449057673512443828)
XLA Ops:
  0.7 1.9 stack.35.norms
  2.6 100.8 %front.1 = (bf16[8,1024,1024]{2,1,0:T(8,128)(2,1)}, bf16[1024,512]{1,0:T(8,128)(2,1)}, bf16[512,1024]{1,0:T(8,128)(2,1)}, f32[32,512]{1,0:T(8,128)}, bf16[32,204...) custom-call(bf16[128,1024]{1,0:T(8,128)(2,1)} %inputs_h.1, ...), custom_call_target="tpu_custom_call" | custom-call | tf_op jit(solution)/shard_map/front/pallas_call | solution.py:1122
  103.4 1.4 fusion
  104.9 82.6 %feed_forward.1 = (bf16[128,1024]{1,0:T(8,128)(2,1)}, f32[128,1024]{1,0:T(8,128)}, bf16[1024,1024]{1,0:T(8,128)(2,1)}, bf16[1024,1024]{1,0:T(8,128)(2,1)}, bf16[...) custom-call(f32[128,1024]{1,0:T(8,128)} %get-tuple-element.86.second, ...), custom_call_target="tpu_custom_call" | custom-call | tf_op jit(solution)/shard_map/feed_forward/pallas_call | solution.py:705
  187.5 110.5 %back.1 = (bf16[128,1024]{1,0:T(8,128)(2,1)}, bf16[256,1024]{1,0:T(8,128)(2,1)}, f32[8,32,1024]{2,1,0:T(8,128)}, f32[2,128,128]{2,1,0:T(8,128)}, f32[256,512]{1,...) custom-call(f32[128,1024]{1,0:T(8,128)} %get-tuple-element.94.gsec, ...), custom_call_target="tpu_custom_call" | custom-call | tf_op jit(solution)/shard_map/back/pallas_call | solution.py:1574
  298.0 3.7 %deliver.1 = (bf16[128,1024]{1,0:T(8,128)(2,1)}, bf16[128,1024]{1,0:T(8,128)(2,1)}, bf16[256,1024]{1,0:T(8,128)(2,1)}, f32[32,1024]{1,0:T(8,128)}, f32[32,1024]{...) custom-call(bf16[128,1024]{1,0:T(8,128)(2,1)} %get-tuple-element.93., ...), custom_call_target="tpu_custom_call" | custom-call | tf_op jit(solution)/shard_map/deliver/pallas_call | solution.py:1624
  301.7 0.7 constant_dynamic-slice_fusion
  302.5 0.5 slice_bitcast_fusion
  (2 shorter events, 0.0 us)

commit v4 on v3

--- a/solution.py
+++ b/solution.py
@@ -496,46 +496,48 @@
     staged = [cp.local(src, dst) for src, dst in ((inputs_h, inputs), (memory_h, memory), (att_h, att), (flow_h, flow), (crossed_h, crossed))]
     greet([yp, zp, core, xp, dp])
     T, D = second.shape
-    NC = 4
-    R = T // NC
+    NC, R = 2, T // 2
+    C = R // NC
     HID = fin.shape[1]; TW = 256
     NT = D // TW
-
-    def spread(buf):
-        zs, ys = [], []
-        for q in range(NC):
-            s = pl.ds(q * R, R)
-            zs.append(cp(buf.at[0, s], buf.at[2, s], zp))
-            ys.append(cp(buf.at[0, s], buf.at[1, s], yp))
-        passed = []
-        def forward(q):
-            s = pl.ds(q * R, R)
-            zs[q].wait_recv()
-            passed.append(cp(buf.at[2, s], buf.at[3, s], yp))
-        return ys, forward, passed
-
-    sums = {}
-    def collect(level, between):
-        between()
-        p2 = []
+    def span(h): return pl.ds(h * R, R)
+
+    def spread(buf, h):
+        zs, ys, passed = [], [], []
+        for u in range(NC):
+            s = pl.ds(u * C, C)
+            zs.append(cp(buf.at[h, 0, s], buf.at[h, 2, s], zp))
+        for u in range(NC):
+            s = pl.ds(u * C, C)
+            ys.append(cp(buf.at[h, 0, s], buf.at[h, 1, s], yp))
+        def beside():
+            for e in ys: e.wait_recv()
+        def forward():
+            for u in range(NC):
+                s = pl.ds(u * C, C)
+                zs[u].wait_recv()
+                passed.append(cp(buf.at[h, 2, s], buf.at[h, 3, s], yp))
+        def across():
+            for e in passed: e.wait_recv()
+        return beside, forward, across
+
+    sums, onward = {}, {}
+    def send_part(level, h, j, t):
+        sums[level, h, j, t] = cp(part.at[h, j, t], (q3 if j == 3 else q1).at[level, h, t], yp)
+    def collect(level, h):
         for t in range(NT):
-            sums[level, 3, t].wait_recv()
-            part[2, t] = part[2, t] + q3[level, t]
-            p2.append(cp(part.at[2, t], q2.at[level, t], zp))
-        return p2
-
-    def send_part(level, j, t):
-        sums[level, j, t] = cp(part.at[j, t], (q3 if j == 3 else q1).at[level, t], yp)
-
-    def gather_up(level, p2):
+            sums[level, h, 3, t].wait_recv()
+            part[h, 2, t] = part[h, 2, t] + q3[level, h, t]
+            onward[level, h, t] = cp(part.at[h, 2, t], q2.at[level, h, t], zp)
+    def gather_up(level, h):
         for t in range(NT):
             cols = pl.ds(t * TW, TW)
-            sums[level, 1, t].wait_recv(); p2[t].wait_recv()
-            acc[:, cols] = acc[:, cols] + q1[level, t].astype(f32) + q2[level, t].astype(f32)
-        cp.sent(p2 + [sums[level, j, t] for j in (1, 3) for t in range(NT)])
-
-    rows[0] = second[...].astype(bf16)
-    ys, forward, fw = spread(rows)
+            sums[level, h, 1, t].wait_recv(); onward[level, h, t].wait_recv()
+            acc[h, :, cols] = acc[h, :, cols] + q1[level, h, t].astype(f32) + q2[level, h, t].astype(f32)
+        cp.sent([onward[level, h, t] for t in range(NT)] + [sums[level, h, j, t] for j in (1, 3) for t in range(NT)])
+
+    for h in range(2): rows[h, 0] = second[span(h), :].astype(bf16)
+    ways = [spread(rows, h) for h in range(2)]
     AD = down_ref.shape[1]
     n = x * 2 + c
     nd = pl.ds(pl.multiple_of(n * AD, AD), AD)
@@ -591,104 +593,125 @@
             e.wait_recv()
             late.append(cp(ref, ref, core))
     def adapter_forward():
+        own = rows[:, 0].reshape(T, D)
         for t in range(2):
             cols = pl.ds(t * 256, 256)
-            g, s = gelu_both(dot(rows[0], down[:, cols]))
+            g, s = gelu_both(dot(own, down[:, cols]))
             ay[1, :, cols] = (ADAPT_SCALE * g.astype(bf16).astype(f32)).astype(bf16)
             bslope[:, cols] = s
         def tile(t, _):
             cols = pl.ds(pl.multiple_of(t * 256, 256), 256)
-            acc[:, cols] = acc[:, cols] + dot(ay[1], up[:, cols])
+            acc[:, :, cols] = acc[:, :, cols] + dot(ay[1], up[:, cols]).reshape(2, R, 256)
             return 0
         lax.fori_loop(0, D // 256, tile, 0)
     def adapter_back():
         def tile(t, _):
             cols = pl.ds(pl.multiple_of(t * 256, 256), 256)
-            gbot = bslope[:, cols] * (ADAPT_SCALE * dot_right(brow[0], up[cols, :]))
+            gbot = bslope[:, cols] * (ADAPT_SCALE * dot_right(brow[:, 0].reshape(T, D), up[cols, :]))
             ay[0, :, cols] = gbot.astype(bf16)
             return 0
         lax.fori_loop(0, down.shape[1] // 256, tile, 0)
         def tile2(t, _):
             cols = pl.ds(pl.multiple_of(t * 256, 256), 256)
-            acc[:, cols] = acc[:, cols] + dot_right(ay[0], down[cols, :])
+            acc[:, :, cols] = acc[:, :, cols] + dot_right(ay[0], down[cols, :]).reshape(2, R, 256)
             return 0
         lax.fori_loop(0, D // 256, tile2, 0)
-    def enter(j):
+    def both(buf, h, g): return buf[h, 2 * g:2 * g + 2].reshape(2 * R, buf.shape[3])
+    def put_out(level, h, g, t, p):
+        cols = pl.ds(t * TW, TW)
+        if g == 0:
+            acc[h, :, cols] = p[:R] if level == 0 else acc[h, :, cols] + p[:R]
+            part[h, 1, t] = p[R:].astype(bf16)
+            send_part(level, h, 1, t)
+        else:
+            part[h, 3, t] = p[R:].astype(bf16)
+            send_part(level, h, 3, t)
+            part[h, 2, t] = p[:R].astype(bf16)
+    def enter(h, g):
+        xv = both(rows, h, g)
         def tile(t, _):
             cols = pl.ds(pl.multiple_of(t * TW, TW), TW)
-            g, s = gelu_both(dot(rows[j], fin[:, cols]))
-            hid[j, :, cols] = g.astype(bf16)
-            slope[j, :, cols] = s
+            e, s = gelu_both(dot(xv, fin[:, cols]))
+            hid[h, 2 * g:2 * g + 2, :, cols] = e.astype(bf16).reshape(2, R, TW)
+            slope[h, 2 * g:2 * g + 2, :, cols] = s.reshape(2, R, TW)
             return 0
         lax.fori_loop(0, HID // TW, tile, 0)
+        hv = both(hid, h, g)
         for t in range(NT):
-            cols = pl.ds(t * TW, TW)
-            p = dot(hid[j], fout[:, cols])
-            if j == 0:
-                acc[:, cols] = p
-            else:
-                part[j, t] = p.astype(bf16)
-                if j != 2: send_part(0, j, t)
-    for e in loads: e.wait()
-    enter(0)
-    for q in ys: q.wait_recv()
-    forward(0); forward(1)
-    enter(1)
-    forward(2); forward(3)
-    enter(2)
-    for q in fw: q.wait_recv()
-    enter(3)
-    def between():
-        adapter_weights()
-        adapter_forward()
-    p2 = collect(0, between)
-    gather_up(0, p2)
-    n3, inv3 = norm(second[...] + acc[...])
-    fac = gain[...].astype(f32)
-    result[...] = (n3 * fac + shift[...].astype(f32)).astype(bf16)
-    e = cot[...].astype(f32)
-    gb = norm_back(e, n3, inv3, fac)
-    gbl = gb.astype(bf16)
-    brow[0] = gbl
-    ys, forward, fw = spread(brow)
-    blow[...] = gbl
-    acc[...] = gb
-    ngrad[0:1, :] = jnp.sum(e * n3, axis=0, keepdims=True)
-    ngrad[1:2, :] = jnp.sum(e, axis=0, keepdims=True)
-    def leave(j):
+            put_out(0, h, g, t, dot(hv, fout[:, pl.ds(t * TW, TW)]))
+    def leave(h, g):
+        xv = both(brow, h, g)
         def tile(t, _):
             cols = pl.ds(pl.multiple_of(t * TW, TW), TW)
-            gh = dot_right(brow[j], fout[cols, :])
-            gpre[j, :, cols] = (slope[j, :, cols] * gh).astype(bf16)
+            gh = dot_right(xv, fout[cols, :])
+            gpre[h, 2 * g:2 * g + 2, :, cols] = (slope[h, 2 * g:2 * g + 2, :, cols].reshape(2 * R, TW) * gh).astype(bf16).reshape(2, R, TW)
             return 0
         lax.fori_loop(0, HID // TW, tile, 0)
+        hv = both(gpre, h, g)
         for t in range(NT):
-            cols = pl.ds(t * TW, TW)
-            p = dot_right(gpre[j], fin[cols, :])
-            if j == 0:
-                acc[:, cols] = acc[:, cols] + p
-            else:
-                part[j, t] = p.astype(bf16)
-                if j != 2: send_part(1, j, t)
-    leave(0)
-    for q in ys: q.wait_recv()
-    forward(0); forward(1)
-    leave(1)
-    forward(2); forward(3)
-    leave(2)
-    for q in fw: q.wait_recv()
-    leave(3)
-    p2 = collect(1, adapter_back)
+            put_out(1, h, g, t, dot_right(hv, fin[pl.ds(t * TW, TW), :]))
+    fac = gain[...].astype(f32)
+    off = shift[...].astype(f32)
+    back = []
+    def turn(h):
+        n3, inv3 = norm(second[span(h), :] + acc[h])
+        result[span(h), :] = (n3 * fac + off).astype(bf16)
+        e = cot[span(h), :].astype(f32)
+        gb = norm_back(e, n3, inv3, fac)
+        gbl = gb.astype(bf16)
+        brow[h, 0] = gbl
+        back.append(spread(brow, h))
+        blow[span(h), :] = gbl
+        acc[h] = gb
+        gg, gs = jnp.sum(e * n3, axis=0, keepdims=True), jnp.sum(e, axis=0, keepdims=True)
+        ngrad[0:1, :] = gg if h == 0 else ngrad[0:1, :] + gg
+        ngrad[1:2, :] = gs if h == 0 else ngrad[1:2, :] + gs
+    (beside0, forward0, across0), (beside1, forward1, across1) = ways
+    for e in loads: e.wait()
+    beside0()
+    enter(0, 0)
+    forward0()
+    across0()
+    enter(0, 1)
+    forward1()
+    beside1()
+    enter(1, 0)
+    collect(0, 0)
+    across1()
+    enter(1, 1)
+    adapter_weights()
+    adapter_forward()
+    collect(0, 1)
+    gather_up(0, 0)
+    turn(0)
+    gather_up(0, 1)
+    turn(1)
+    (beside0, forward0, across0), (beside1, forward1, across1) = back
+    beside0()
+    leave(0, 0)
+    forward0()
+    adapter_back()
+    across0()
+    leave(0, 1)
+    forward1()
+    beside1()
+    leave(1, 0)
+    collect(1, 0)
+    across1()
+    leave(1, 1)
     def wtile(t, _):
         cols = pl.ds(pl.multiple_of(t * TW, TW), TW)
-        fi[:, cols] = dot_left(rows[...].reshape(4 * T, D), gpre[:, :, cols].reshape(4 * T, TW)).astype(bf16)
-        fo[:, cols] = dot_left(hid[...].reshape(4 * T, HID), brow[:, :, cols].reshape(4 * T, TW)).astype(bf16)
+        fi[:, cols] = dot_left(rows[...].reshape(4 * T, D), gpre[:, :, :, cols].reshape(4 * T, TW)).astype(bf16)
+        fo[:, cols] = dot_left(hid[...].reshape(4 * T, HID), brow[:, :, :, cols].reshape(4 * T, TW)).astype(bf16)
         return 0
-    lax.fori_loop(0, HID // TW, wtile, 0)
+    lax.fori_loop(0, 1, wtile, 0)
+    collect(1, 1)
+    lax.fori_loop(1, HID // TW, wtile, 0)
     kept += [cp.local(fi, fi_out), cp.local(fo, fo_out)]
     share_on()
-    gather_up(1, p2)
-    gsec[...] = acc[...]
+    for h in range(2):
+        gather_up(1, h)
+        gsec[span(h), :] = acc[h]
     for e in kept[2:]: e.wait()
     for e in near[2:] + late[2:]: e.wait_recv()
     for e in fans: e()
@@ -707,8 +730,8 @@
         out_shape=(sds((T, D), bf16), sds((T, D), f32), sds((D, HID), bf16), sds((HID, D), bf16), sds((2, T, AD), bf16), sds((T, D), bf16), sds((2, D), f32),
             four, four, four, sds((4 * M, D), bf16)),
         in_specs=[vm] * 2 + [any_] * 6 + [vm] * 2 + [any_] * 5, out_specs=(vm,) * 2 + (any_,) * 2 + (vm,) * 3 + (any_,) * 4,
-        scratch_shapes=[v(T, D), v(M, D), v(T, D), v(T, D), v(T, D), v(D, HID), v(HID, D), v(D, HID), v(HID, D), v(D, AD), v(AD, D), v(4, T, D), v(4, T, D), v(4, T, HID), vf(4, T, HID), v(4, T, HID), v(4, D // 256, T, 256),
-            v(2, D // 256, T, 256), v(2, D // 256, T, 256), v(2, D // 256, T, 256), vf(T, AD), vf(T, D),
+        scratch_shapes=[v(T, D), v(M, D), v(T, D), v(T, D), v(T, D), v(D, HID), v(HID, D), v(D, HID), v(HID, D), v(D, AD), v(AD, D), v(2, 4, T // 2, D), v(2, 4, T // 2, D), v(2, 4, T // 2, HID), vf(2, 4, T // 2, HID), v(2, 4, T // 2, HID), v(2, 4, D // 256, T // 2, 256),
+            v(2, 2, D // 256, T // 2, 256), v(2, 2, D // 256, T // 2, 256), v(2, 2, D // 256, T // 2, 256), vf(T, AD), vf(2, T // 2, D),
             pltpu.SemaphoreType.DMA((128,)), pltpu.SemaphoreType.DMA((128,))],
         compiler_params=pltpu.CompilerParams(collective_id=3, has_side_effects=True, vmem_limit_bytes=60 << 20),
         name="feed_forward")(second, cot, fin, fout, fin2, fout2, down, up, gain, shift, inputs, memory, att, flow, crossed)
@@ -716,6 +739,7 @@
 
 NEGATIVE = -1000000000.0
 PADDED = 32
+PREFIX = 30
 
 def project(x, weight, out, tile=256):
     def step(t, _):
@@ -1274,18 +1298,54 @@
         for t in range(2):
             first[i, t] = level1(i, t)
             cp.all.append(first[i, t])
-    def compute(i, t):
-        if t == 0:
-            for e in waits[i]: e()
-        for e in shared[i, t]: e()
-        cols = pl.ds(t * wide, wide)
-        n = (0, None, 1, 2)[i]
-        def rows(u):
-            d = columns(u)
-            p = dot_left(mb[:, d], mby[:, cols]) if i == 1 else dot_left(xb[n, :, d], yb[n, :, cols])
-            pb[i, t, u] = p.astype(bf16).reshape(2, 2, 2 * r, wide)
-        loop(0, A, rows)
-        level1(i, t).start()
+    def share_one(src, dst, t, owner):
+        m = src.shape[0]
+        k = cp.count
+        cp.count += 4
+        wide = half // 2
+        here = pl.ds(pl.multiple_of(x * half + t * wide, wide), wide)
+        there = pl.ds(pl.multiple_of((1 - x) * half + t * wide, wide), wide)
+        spot = dst.at[pl.ds(pl.multiple_of(place_n * m, m), m), pl.ds(t * wide, wide)]
+        kept = pltpu.make_async_copy(src.at[:, here], spot, ssem.at[k])
+        ways = [remote(src.at[:, there], spot, ssem.at[k + 1], rsem.at[k + 1], xp), remote(src.at[:, here], spot, ssem.at[k + 2], rsem.at[k + 2], core),
+                remote(src.at[:, there], spot, ssem.at[k + 3], rsem.at[k + 3], dp)]
+        def mine():
+            ways[0].start()
+            kept.start()
+        def other():
+            ways[2].start()
+            ways[1].start()
+        pl.when(c == owner)(mine)
+        pl.when(c != owner)(other)
+        def arrived():
+            kept.wait()
+            for e in ways: e.wait_recv()
+        def sent():
+            pl.when(c == owner)(ways[0].wait_send)
+            def both():
+                ways[1].wait_send()
+                ways[2].wait_send()
+            pl.when(c != owner)(both)
+        ending.append(sent)
+        return (arrived,)
+    ending = []
+    used, filled = set(), set()
+    def compute(i, t, owner=None):
+        def go():
+            if (i, owner) not in used:
+                used.add((i, owner))
+                for e in waits[i]: e()
+            for e in shared[(i, t) if owner is None else (i, t, owner)]: e()
+            cols = pl.ds(t * wide, wide)
+            n = (0, None, 1, 2)[i]
+            def rows(u):
+                d = columns(u)
+                p = dot_left(mb[:, d], mby[:, cols]) if i == 1 else dot_left(xb[n, :, d], yb[n, :, cols])
+                pb[i, t, u] = p.astype(bf16).reshape(2, 2, 2 * r, wide)
+            loop(0, A, rows)
+            level1(i, t).start()
+        if owner is None: go()
+        else: pl.when(c == owner)(go)
     def one(i, t):
         def go():
             first[i, t].wait_recv()
@@ -1310,7 +1370,8 @@
             fourth[i, t].wait_recv()
             ob[i, :, pl.ds(pl.multiple_of(x * half + t * wide, wide), wide)] = sb[i, t, x]
             ob[i, :, pl.ds(pl.multiple_of((1 - x) * half + t * wide, wide), wide)] = r3[i, t].astype(f32)
-            if t == 1:
+            filled.add((i, t))
+            if (i, 1 - t) in filled:
                 outs.append(cp.local(ob.at[i, pl.ds(pl.multiple_of(c * r, r), r)], out.at[2 * i + c]).wait)
                 outs.append(cp(ob.at[i, pl.ds(pl.multiple_of(o * r, r), r)], out.at[2 * i + c], core).wait_recv)
         return go
@@ -1476,83 +1537,108 @@
     shared = {}
     def spread(i, srcs, dst):
         for t in range(2): shared[i, t] = share(srcs, dst, t)
+    def spread_one(i, src, dst, owner):
+        for t in range(2): shared[i, t, owner] = share_one(src, dst, t, owner)
     norm_two()
+    spread_one(0, mid, yb.at[0], 0)
     wait_slot(0)()
-    back_project(mid, 0, 0)(); back_project(mid, 0, 1)()
+    back_project(mid, 0, 0)()
+    back_project(mid, 0, 1)()
     fetch(0, 6)
-    adapt0()
     ready(0, 4)
     cross_back(0)()
+    cross_back(1)()
+    cross_back(2)()
+    cross_back(3)()
+    compute(0, 1, 0)
+    spread_one(0, dcq, yb.at[0], 1)
     feed0()
-    cross_back(1)(); cross_back(2)(); cross_back(3)()
-    spread(0, (mid, dcq), yb.at[0])
-    spread(1, (dck, dcv), mby)
     wait_slot(1)()
     first_grad()
     fetch(1, 0)
     ready(4, 6)
     norm_one()
-    tail_norm0()
+    spread(1, (dck, dcv), mby)
+    compute(0, 1, 1)
+    compute(0, 0, 0)
     wait_slot(2)()
-    back_project(startl, 2, 0)(); back_project(startl, 2, 1)()
+    back_project(startl, 2, 0)()
+    back_project(startl, 2, 1)()
     fetch(2, 1)
     ready(6, 11)
     self_back(0)()
-    compute(0, 0)
+    wait_slot(3)()
+    wait_slot(0)()
+    memory_part(0)()
+    one(0, 1)()
+    compute(0, 0, 1)
+    self_back(1)()
+    compute(1, 0)
+    self_back(2)()
+    tail_norm0()
+    spread_one(2, startl, yb.at[1], 0)
+    one(0, 0)()
     tail_norm(1)()
-    self_back(1)()
-    compute(0, 1)
+    self_back(3)()
+    compute(1, 1)
+    tail0()
+    spread_one(2, dq, yb.at[1], 1)
+    spread(3, (dk, dv), yb.at[2])
+    compute(2, 0, 0)
+    compute(2, 1, 0)
+    compute(2, 0, 1)
+    one(1, 0)()
+    adapt0()
+    compute(3, 1)
+    feed1()
+    one(1, 1)()
+    one(2, 0)()
+    tail1()
+    compute(2, 1, 1)
+    one(3, 1)()
+    tail2()
+    compute(3, 0)
+    one(2, 1)()
     adapt1()
-    self_back(2)()
-    compute(1, 0)
-    tail_norm(2)()
-    self_back(3)()
-    tail0()
-    spread(2, (startl, dq), yb.at[1])
-    spread(3, (dk, dv), yb.at[2])
-    compute(1, 1)
-    one(0, 0)(); one(0, 1)()
-    tail_norm3()
-    compute(2, 0); compute(2, 1)
-    tail1()
-    one(1, 0)()
-    compute(3, 0); compute(3, 1)
+    one(3, 0)()
+    two(0, 1)()
+    tail3()
+    tail4()
+    two(1, 1)()
     adapt2()
-    one(1, 1)()
-    tail2()
-    tail_norm4()
-    two(0, 0)(); two(0, 1)()
-    wait_slot(3)(); wait_slot(0)()
-    memory_part(0)()
-    feed1()
-    tail3()
+    tail5(1)()
+    two(0, 0)()
+    two(1, 0)()
+    tail5(2)()
+    three(1, 1)()
     memory_part(1)()
     outs.append(cp.local(mgrad, mgrad_o).wait)
     fetch(3, 2)
-    one(2, 0)()
-    two(1, 0)()
-    tail4()
-    one(2, 1)()
-    two(1, 1)()
-    tail5(1)()
-    three(0, 0)(); three(0, 1)()
-    wait_slot(1)(); wait_slot(2)(); wait_slot(3)()
+    wait_slot(1)()
+    wait_slot(2)()
+    wait_slot(3)()
     input_part(0)()
-    tail5(2)()
-    one(3, 0)()
+    two(3, 1)()
+    three(1, 0)()
+    tail6()
+    three(0, 0)()
+    two(3, 0)()
+    tail_norm(2)()
+    three(0, 1)()
+    three(3, 1)()
     input_part(1)()
     outs.append(cp.local(igrad, igrad_o).wait)
-    tail6()
+    adapt3()
+    three(3, 0)()
     two(2, 0)()
-    one(3, 1)()
+    tail_norm3()
     feed2()
-    adapt3()
-    three(1, 0)(); three(1, 1)()
-    two(2, 1)(); two(3, 0)()
+    two(2, 1)()
+    three(2, 1)()
+    three(2, 0)()
     tail7()
-    three(2, 0)(); three(2, 1)()
-    two(3, 1)()
-    three(3, 0)(); three(3, 1)()
+    tail_norm4()
+    for e in ending: e()
     for e in outs: e()
     cp.close()
 

time: 303 us -> 285 us (0.941)
  Pallas kernels: 298 us -> 279 us
    pallas_call x1, Pallas kernels: 82.6 us -> 72.5 us  [feed(): pl.pallas_call(functools.partial(feed_kernel, A), out_shape=(sds((T, D),...]
    pallas_call x1, Pallas kernels: 111 us -> 102 us  [back(): pl.pallas_call(functools.partial(back_kernel, A, r), out_shape=(sds((T, D...]
where the time goes in v4:
time: 285 us
  Pallas kernels  279 us (98%)
  local copies, waits for them, and re-layouts  4.65 us (2%)
    pallas_call x1, Pallas kernels, back(): pl.pallas_call(functools.partial(back_kernel, A, r), out_shape=(sds((T, D...  102 us
    pallas_call x1, Pallas kernels, front(): pl.pallas_call(functools.partial(front_kernel, A, r), out_shape=(sds((8,...  101 us
    pallas_call x1, Pallas kernels, feed(): pl.pallas_call(functools.partial(feed_kernel, A), out_shape=(sds((T, D),...  72.5 us

profile of v4, /device:TPU:0, one launch (start us, length us, event | category | flops | bytes accessed | tf_op | source)
XLA Modules:
  0.0 284.7 jit_solution(5473697503662602417)
XLA Ops:
  0.7 1.9 stack.35.norms
  2.6 100.8 %front.1 = (bf16[8,1024,1024]{2,1,0:T(8,128)(2,1)}, bf16[1024,512]{1,0:T(8,128)(2,1)}, bf16[512,1024]{1,0:T(8,128)(2,1)}, f32[32,512]{1,0:T(8,128)}, bf16[32,204...) custom-call(bf16[128,1024]{1,0:T(8,128)(2,1)} %inputs_h.1, ...), custom_call_target="tpu_custom_call" | custom-call | tf_op jit(solution)/shard_map/front/pallas_call | solution.py:1146
  103.4 1.4 fusion
  104.9 72.5 %feed_forward.1 = (bf16[128,1024]{1,0:T(8,128)(2,1)}, f32[128,1024]{1,0:T(8,128)}, bf16[1024,1024]{1,0:T(8,128)(2,1)}, bf16[1024,1024]{1,0:T(8,128)(2,1)}, bf16[...) custom-call(f32[128,1024]{1,0:T(8,128)} %get-tuple-element.86.second, ...), custom_call_target="tpu_custom_call" | custom-call | tf_op jit(solution)/shard_map/feed_forward/pallas_call | solution.py:728
  177.3 102.4 %back.1 = (bf16[128,1024]{1,0:T(8,128)(2,1)}, bf16[256,1024]{1,0:T(8,128)(2,1)}, f32[8,32,1024]{2,1,0:T(8,128)}, f32[2,128,128]{2,1,0:T(8,128)}, f32[256,512]{1,...) custom-call(f32[128,1024]{1,0:T(8,128)} %get-tuple-element.94.gsec, ...), custom_call_target="tpu_custom_call" | custom-call | tf_op jit(solution)/shard_map/back/pallas_call | solution.py:1660
  279.7 3.7 %deliver.1 = (bf16[128,1024]{1,0:T(8,128)(2,1)}, bf16[128,1024]{1,0:T(8,128)(2,1)}, bf16[256,1024]{1,0:T(8,128)(2,1)}, f32[32,1024]{1,0:T(8,128)}, f32[32,1024]{...) custom-call(bf16[128,1024]{1,0:T(8,128)(2,1)} %get-tuple-element.93., ...), custom_call_target="tpu_custom_call" | custom-call | tf_op jit(solution)/shard_map/deliver/pallas_call | solution.py:1710
  283.4 0.7 constant_dynamic-slice_fusion
  284.2 0.5 slice_bitcast_fusion
  (2 shorter events, 0.0 us)

commit v5 on v4

--- a/solution.py
+++ b/solution.py
@@ -482,8 +482,9 @@
     s = e * factor
     return inverse * (s - jnp.mean(s, axis=-1, keepdims=True) - n * jnp.mean(s * n, axis=-1, keepdims=True))
 
-def feed_kernel(A, second, cot, fin_own, fout_own, fin_two, fout_two, down_ref, up_ref, gain, shift, inputs_h, memory_h, att_h, flow_h, crossed_h,
-                result, gsec, fi_out, fo_out, ay, blow, ngrad, xp0, xatt, xin, xmem, inputs, memory, att, flow, crossed, fin, fout, fi, fo, down, up, rows, brow, hid, slope, gpre, part, q1, q2, q3, bslope, acc, ssem, rsem):
+def feed_part(A, second, vecs, cot, fin_own, fout_own, down_ref, up_ref, inputs, memory, att, flow, crossed, partner, outs, scratch):
+    result, gsec, fi_out, fo_out, ay, blow, ngrad, xp0, xatt, xin, xmem = outs
+    fin, fout, fi, fo, down, up, rows, brow, hid, slope, gpre, part, q1, q2, q3, bslope, acc, ssem, rsem = scratch
     a, b, x, c = place()
     o = 1 - c
     yp = device(a, 1 - b, x, c)
@@ -491,10 +492,7 @@
     core, xp, dp = device(a, b, x, o), device(a, b, 1 - x, c), device(a, b, 1 - x, o)
     cp = Copies(ssem, rsem)
     half = fin_own.shape[1]
-    lo, hi = pl.ds(0, half), pl.ds(half, half)
-    loads = [cp.local(fin_own, fin.at[:, lo]), cp.local(fin_two, fin.at[:, hi]), cp.local(fout_own, fout.at[lo]), cp.local(fout_two, fout.at[hi])]
-    staged = [cp.local(src, dst) for src, dst in ((inputs_h, inputs), (memory_h, memory), (att_h, att), (flow_h, flow), (crossed_h, crossed))]
-    greet([yp, zp, core, xp, dp])
+    loads = [cp.local(fin_own, fin.at[:, pl.ds(0, half)]), cp.local(fout_own, fout.at[pl.ds(0, half)])]
     T, D = second.shape
     NC, R = 2, T // 2
     C = R // NC
@@ -573,7 +571,6 @@
             pl.when(c == 0)(functools.partial(finish, 0))
             pl.when(c == 1)(functools.partial(finish, 1))
         return done
-    for e in staged: e.wait()
     fans = [fan((crossed, flow), xp0), fan((att, None), xatt)]
     M = memory.shape[0]
     share = []
@@ -650,8 +647,7 @@
         hv = both(gpre, h, g)
         for t in range(NT):
             put_out(1, h, g, t, dot_right(hv, fin[pl.ds(t * TW, TW), :]))
-    fac = gain[...].astype(f32)
-    off = shift[...].astype(f32)
+    fac, off = vecs[4:5, :], vecs[5:6, :]
     back = []
     def turn(h):
         n3, inv3 = norm(second[span(h), :] + acc[h])
@@ -668,6 +664,7 @@
         ngrad[1:2, :] = gs if h == 0 else ngrad[1:2, :] + gs
     (beside0, forward0, across0), (beside1, forward1, across1) = ways
     for e in loads: e.wait()
+    partner()
     beside0()
     enter(0, 0)
     forward0()
@@ -717,36 +714,10 @@
     for e in fans: e()
     cp.close()
 
-def feed(A, second, cot, fin, fout, fin2, fout2, down, up, gain, shift, inputs, memory, att, flow, crossed):
-    T, D = second.shape; HID = 2 * fin.shape[1]; AD = down.shape[1] * 4; M = memory.shape[0]
-    v = lambda *s: pltpu.VMEM(s, bf16)
-    vf = lambda *s: pltpu.VMEM(s, f32)
-    vm = pl.BlockSpec(memory_space=pltpu.VMEM)
-    any_ = pl.BlockSpec(memory_space=pl.ANY)
-    sds = jax.ShapeDtypeStruct
-    four = sds((4 * T, D), bf16)
-    return pl.pallas_call(
-        functools.partial(feed_kernel, A),
-        out_shape=(sds((T, D), bf16), sds((T, D), f32), sds((D, HID), bf16), sds((HID, D), bf16), sds((2, T, AD), bf16), sds((T, D), bf16), sds((2, D), f32),
-            four, four, four, sds((4 * M, D), bf16)),
-        in_specs=[vm] * 2 + [any_] * 6 + [vm] * 2 + [any_] * 5, out_specs=(vm,) * 2 + (any_,) * 2 + (vm,) * 3 + (any_,) * 4,
-        scratch_shapes=[v(T, D), v(M, D), v(T, D), v(T, D), v(T, D), v(D, HID), v(HID, D), v(D, HID), v(HID, D), v(D, AD), v(AD, D), v(2, 4, T // 2, D), v(2, 4, T // 2, D), v(2, 4, T // 2, HID), vf(2, 4, T // 2, HID), v(2, 4, T // 2, HID), v(2, 4, D // 256, T // 2, 256),
-            v(2, 2, D // 256, T // 2, 256), v(2, 2, D // 256, T // 2, 256), v(2, 2, D // 256, T // 2, 256), vf(T, AD), vf(2, T // 2, D),
-            pltpu.SemaphoreType.DMA((128,)), pltpu.SemaphoreType.DMA((128,))],
-        compiler_params=pltpu.CompilerParams(collective_id=3, has_side_effects=True, vmem_limit_bytes=60 << 20),
-        name="feed_forward")(second, cot, fin, fout, fin2, fout2, down, up, gain, shift, inputs, memory, att, flow, crossed)
-
 
 NEGATIVE = -1000000000.0
 PADDED = 32
 PREFIX = 30
-
-def project(x, weight, out, tile=256):
-    def step(t, _):
-        cols = pl.ds(pl.multiple_of(t * tile, tile), tile)
-        out[:, cols] = dot(x[...], weight[:, cols]).astype(out.dtype)
-        return 0
-    lax.fori_loop(0, out.shape[1] // tile, step, 0)
 
 
 def lane_half(rows):
@@ -757,82 +728,10 @@
     zero = jnp.zeros_like(v)
     return jnp.where(low, v, zero), jnp.where(low, zero, v)
 
-def self_mask(seg_col, seg_row):
-    T = seg_col.shape[0]
-    row = lax.broadcasted_iota(jnp.int32, (T, T), 0)
-    col = lax.broadcasted_iota(jnp.int32, (T, T), 1)
-    own = jnp.where((row >= col) & (seg_col[...] == seg_row[...]), 0.0, NEGATIVE)
-    lane = lax.broadcasted_iota(jnp.int32, (T, PADDED), 1)
-    return jnp.concatenate([own, jnp.where(lane < 30, 0.0, NEGATIVE)], axis=1)
-
-def attend(q, keys, values, penalty, probs, out, pairs=8):
-    def step(p, _):
-        cols = pl.ds(pl.multiple_of(p * 128, 128), 128)
-        kk, vv = keys(cols), values(cols)
-        qs = split_heads(q[:, cols])
-        vs = split_heads(vv)
-        total = None
-        for s in range(2):
-            score = jnp.where(penalty[...] < -1.0, NEGATIVE, dot_right(qs[s], kk) * 0.125)
-            e = jnp.exp(score - jnp.max(score, axis=-1, keepdims=True))
-            prob = (e * (1.0 / jnp.sum(e, axis=-1, keepdims=True))).astype(bf16)
-            probs[2 * p + s] = prob
-            mixed = dot(prob, vs[s])
-            total = mixed if total is None else total + mixed
-        out[:, cols] = total.astype(bf16)
-        return 0
-    lax.fori_loop(0, pairs, step, 0)
-
-
-def both_keys(own, prows, offset):
-    def get(cols):
-        shifted = pl.ds(pl.multiple_of(cols.start + offset, 128), 128)
-        return jnp.concatenate([own[:, cols], prows[:, shifted]], axis=0)
-    return get
 
 def whole(ref):
     return lambda cols: ref[:, cols]
 
-def add_norm(base, low, weight, gain, shift, out, normed, inverse, tile=256):
-    def step(t, _):
-        cols = pl.ds(pl.multiple_of(t * tile, tile), tile)
-        out[:, cols] = base[:, cols].astype(f32) + dot(low[...], weight[:, cols])
-        return 0
-    lax.fori_loop(0, out.shape[1] // tile, step, 0)
-    n, i = norm(out[...])
-    normed[...] = n
-    inverse[...] = i
-    out[...] = n * gain + shift
-
-def forward_kernel(inputs, memory, seg_col, seg_row, mem_row, weights, prows, vecs,
-                   q, k, v, probs, attended, first, n1, i1, cq, ck, cv, cprobs, crossed, second, n2, i2, pen, cpen):
-    width = inputs.shape[1]
-    pen[...] = self_mask(seg_col, seg_row)
-    cpen[...] = jnp.where(seg_col[...] == mem_row[...], 0.0, NEGATIVE)
-    project(inputs, weights.at[0], q); project(inputs, weights.at[1], k); project(inputs, weights.at[2], v)
-    project(memory, weights.at[6], ck); project(memory, weights.at[7], cv)
-    attend(q, both_keys(k, prows, 0), both_keys(v, prows, width), pen, probs, attended)
-    add_norm(inputs, attended, weights.at[3], vecs[0:1, :], vecs[1:2, :], first, n1, i1)
-    q[...] = q[...]
-    def step(t, _):
-        cols = pl.ds(pl.multiple_of(t * 256, 256), 256)
-        cq[:, cols] = dot(first[...].astype(bf16), weights[4, :, cols]).astype(bf16)
-        return 0
-    lax.fori_loop(0, width // 256, step, 0)
-    attend(cq, whole(ck), whole(cv), cpen, cprobs, crossed)
-    add_norm(first, crossed, weights.at[5], vecs[2:3, :], vecs[3:4, :], second, n2, i2)
-
-def forward(inputs, memory, seg_col, seg_row, mem_row, weights, prows, vecs):
-    T, D = inputs.shape; M = memory.shape[0]
-    vm = pl.BlockSpec(memory_space=pltpu.VMEM)
-    sds = jax.ShapeDtypeStruct
-    row, mrow, full, one = sds((T, D), bf16), sds((M, D), bf16), sds((T, D), f32), sds((T, 1), f32)
-    return pl.pallas_call(forward_kernel,
-        out_shape=(row, row, row, sds((16, T, T + PADDED), bf16), row, full, full, one, row, mrow, mrow, sds((16, T, M), bf16), row, full, full, one),
-        in_specs=[vm] * 8, out_specs=(vm,) * 16,
-        scratch_shapes=[pltpu.VMEM((T, T + PADDED), f32), pltpu.VMEM((T, M), f32)],
-        compiler_params=pltpu.CompilerParams(vmem_limit_bytes=60 << 20), name="attention_forward")(
-            inputs, memory, seg_col, seg_row, mem_row, weights, prows, vecs)
 
 def norm_back_into(e, n, i, gain, out, ngrad, at):
     ee = e[...]
@@ -853,18 +752,16 @@
 def loop(start, stop, step):
     lax.fori_loop(start, stop, lambda t, z: (step(t), z)[1], 0)
 
-def front_kernel(A, r, inputs, memory, seg_row, mem_row, embed, inner, outer, norms, *refs):
-    ws, (fin, fout) = refs[:8], refs[8:10]
-    (wout, fin2, fout2, tangent, prows_o, vecs_o, q_o, k_o, v_o, probs_o, att_o, first_o, n1_o, i1_o, cq_o, ck_o, cv_o, cprobs_o, crossed_o,
-     second_o, slow_o, n2_o, i2_o) = refs[10:33]
+def front_part(A, r, inputs, memory, seg_row, mem_row, embed, inner, outer, norms, ws, fin, fout, fin2, fout2, outs, scratch):
+    (wout, tangent, prows_o, vecs_o, q_o, k_o, v_o, probs_o, att_o, first_o, n1_o, i1_o, cq_o, ck_o, cv_o, cprobs_o, crossed_o, slow_o, n2_o, i2_o) = outs
     (g, q, k, v, probs, att, first, flow, n1, i1, cq, ck, cv, cprobs, crossed, second, slow, n2, i2, pen, cpen,
-     buf, got, zbuf, r0, r1, prows, nout, vecs, tan, ssem, rsem) = refs[33:]
+     buf, got, zbuf, r0, r1, prows, nout, vecs, tan, ssem, rsem) = scratch
     a, b, x, c = place()
     core, xp, yp = device(a, b, x, 1 - c), device(a, b, 1 - x, c), device(a, 1 - b, x, c)
     zp = [device((a + j) % A, b, x, c) for j in range(A)]
     za = a + 1 - 2 * (a % 2)
     zq = device(za, b, x, c)
-    greet([core, xp, yp] + zp[1:])
+    greet([core, xp, yp, device(a, b, 1 - x, 1 - c)] + zp[1:])
     cp = Copies(ssem, rsem)
     T, D = inputs.shape
     pairs = 4
@@ -949,36 +846,35 @@
         ri = pl.ds(pl.multiple_of(c * (D // 2) + i * n, n), n)
         m = H // 8
         ro = pl.ds(pl.multiple_of(c * (H // 2) + i * m, m), m)
-        feeds[i] = [(cp(fin.at[ri], fin2.at[ri], zq), fin2.at[ri]),
-                    (cp(fout.at[ro], fout2.at[ro], zq), fout2.at[ro])]
+        ro2 = pl.ds(pl.multiple_of(H + c * (H // 2) + i * m, m), m)
+        feeds[i] = [(cp(fin.at[ri], fin2.at[ri, pl.ds(H, H)], zq), fin2.at[ri, pl.ds(H, H)]),
+                    (cp(fout.at[ro], fout2.at[ro2], zq), fout2.at[ro2])]
     def feed_pass(i):
         for e, ref in feeds[i]:
             e.wait_recv()
             passed.append(cp(ref, ref, core))
     zc, mc, lc, dc = {}, {}, {}, {}
     two, three = (yp, xp), (xp, yp)
-    def first_send(i):
-        own[i].wait(); cross[i].wait()
-        for h in range(2):
-            mc[i, h, 0] = cp(block(i, h, a, b, x), block(i, h, a, b, x), two[h])
-        for h in range(2):
-            lc[i, h, 0, 0] = cp(block(i, h, a, b, x), block(i, h, a, b, x), three[h])
+    begun = set()
+    def fs(i, h):
+        if i not in begun:
+            begun.add(i)
+            own[i].wait(); cross[i].wait()
+        mc[i, h, 0] = cp(block(i, h, a, b, x), block(i, h, a, b, x), two[h])
+        lc[i, h, 0, 0] = cp(block(i, h, a, b, x), block(i, h, a, b, x), three[h])
+    def fz(i, h):
         for j in range(1, A):
-            for h in range(2):
-                zc[i, h, j] = cp(block(i, h, a, b, x), block(i, h, a, b, x), zp[j])
-    def mid(i, j):
+            zc[i, h, j] = cp(block(i, h, a, b, x), block(i, h, a, b, x), zp[j])
+    def mid(i, h, j):
         aj = (a + A - j) % A
-        for h in range(2):
-            zc[i, h, j].wait_recv()
-            mc[i, h, j] = cp(block(i, h, aj, b, x), block(i, h, aj, b, x), two[h])
-        for h in range(2):
-            lc[i, h, j, 0] = cp(block(i, h, aj, b, x), block(i, h, aj, b, x), three[h])
-    def third(i, j):
+        zc[i, h, j].wait_recv()
+        mc[i, h, j] = cp(block(i, h, aj, b, x), block(i, h, aj, b, x), two[h])
+        lc[i, h, j, 0] = cp(block(i, h, aj, b, x), block(i, h, aj, b, x), three[h])
+    def third(i, h, j):
         aj = (a + A - j) % A
-        for h in range(2):
-            w = (aj, 1 - b, x) if h == 0 else (aj, b, 1 - x)
-            mc[i, h, j].wait_recv()
-            lc[i, h, j, 1] = cp(block(i, h, *w), block(i, h, *w), three[h])
+        w = (aj, 1 - b, x) if h == 0 else (aj, b, 1 - x)
+        mc[i, h, j].wait_recv()
+        lc[i, h, j, 1] = cp(block(i, h, *w), block(i, h, *w), three[h])
     per = D // A
     def finish(i, j):
         aj = (a + A - j) % A
@@ -999,9 +895,6 @@
                 loop(2 * n, 2 * n + 2, step)
             return go
         return [part(0), part(1)]
-    def keep(src, dst):
-        def go(): kept.append(cp.local(src, dst))
-        return go
     def masks():
         row = lax.broadcasted_iota(jnp.int32, (T, T), 0)
         col = lax.broadcasted_iota(jnp.int32, (T, T), 1)
@@ -1066,75 +959,179 @@
             out[...] = s
             olow[...] = s.astype(bf16)
         return [part(0), part(1), last]
-    comp = {
-        0: halves(inputs, 0, q) + halves(inputs, 1, k) + [keep(q, q_o), keep(k, k_o), masks],
-        1: halves(inputs, 2, v) + [keep(v, v_o)] + [own_attend(n) for n in range(4)] + [keep(probs, probs_o), keep(att, att_o)]
-           + normed(inputs, att, 3, 0, first, n1, i1, flow) + [keep(flow, first_o), keep(n1, n1_o), keep(i1, i1_o)],
-        2: halves(memory, 4, ck) + [keep(ck, ck_o)] + halves(flow, 5, cq) + [keep(cq, cq_o)] + [cross_scores(n) for n in range(4)] + [keep(cprobs, cprobs_o)],
-        3: halves(memory, 6, cv) + [keep(cv, cv_o)] + [cross_mix(n) for n in range(2)] + [keep(crossed, crossed_o)]
-           + normed(first, crossed, 7, 2, second, n2, i2, slow) + [keep(second, second_o), keep(slow, slow_o), keep(n2, n2_o), keep(i2, i2_o)],
-    }
-    queue = []
-    def turn(count=1):
-        for _ in range(count):
-            if queue: queue.pop(0)()
-    small_steps = [pre1, pre2(1), pre2(2), pre4, pre5, pre6, pre7]
-    def tick():
-        if small_steps: small_steps.pop(0)()
-    first_send(0)
-    tick()
-    for i in range(pairs):
-        if i + 1 < pairs:
-            first_send(i + 1)
-        feed_send(i)
-        third(i, 0)
-        tick()
-        turn()
-        if i:
-            finish(i - 1, 2)
-            turn()
-        mid(i, 1)
-        tick()
-        turn()
-        if i:
-            finish(i - 1, 3)
-            turn()
-        mid(i, 2)
-        tick()
-        turn()
-        if i: feed_pass(i - 1)
-        mid(i, 3)
-        tick()
-        turn()
-        third(i, 1)
-        if i:
-            arrive(i - 1)
-            if i == 2: pre8()
-            queue += comp[i - 1]
-        turn()
-        finish(i, 0)
-        turn(2)
-        third(i, 2)
-        turn(2)
-        finish(i, 1)
-        turn(2)
-        third(i, 3)
-        turn(2)
+    make_q, make_k, make_v = halves(inputs, 0, q), halves(inputs, 1, k), halves(inputs, 2, v)
+    make_ck, make_cq, make_cv = halves(memory, 4, ck), halves(flow, 5, cq), halves(memory, 6, cv)
+    norm_one, norm_two = normed(inputs, att, 3, 0, first, n1, i1, flow), normed(first, crossed, 7, 2, second, n2, i2, slow)
+    fs(0, 0)
+    fs(0, 1)
+    fz(0, 0)
+    fs(1, 1)
+    fs(1, 0)
+    fz(0, 1)
+    fs(3, 0)
+    fs(2, 0)
+    fz(1, 0)
+    fs(2, 1)
+    third(0, 1, 0)
+    third(1, 1, 0)
+    pre1()
+    fs(3, 1)
+    pre2(1)()
+    mid(0, 0, 3)
+    mid(0, 1, 1)
+    third(0, 0, 0)
+    mid(0, 0, 2)
+    pre2(2)()
+    fz(1, 1)
+    mid(0, 1, 3)
+    mid(0, 0, 1)
+    mid(1, 0, 2)
+    finish(0, 0)
+    third(0, 0, 2)
+    mid(1, 0, 1)
+    fz(2, 0)
+    pre4()
+    pre5()
+    third(0, 0, 1)
+    mid(1, 1, 1)
+    mid(0, 1, 2)
+    feed_send(2)
+    third(1, 0, 0)
+    mid(1, 1, 2)
+    third(0, 1, 1)
+    mid(1, 1, 3)
+    third(0, 1, 2)
+    pre6()
+    fz(2, 1)
+    third(0, 1, 3)
+    third(2, 0, 0)
+    third(0, 0, 3)
+    mid(1, 0, 3)
+    mid(2, 1, 1)
+    finish(0, 2)
+    pre7()
+    finish(0, 1)
+    fz(3, 0)
+    third(1, 0, 1)
+    third(1, 1, 2)
+    third(1, 0, 2)
+    mid(2, 1, 2)
+    third(1, 0, 3)
+    mid(2, 0, 2)
+    fz(3, 1)
+    third(1, 1, 1)
+    third(1, 1, 3)
+    mid(2, 1, 3)
+    finish(0, 3)
+    finish(1, 0)
+    finish(1, 1)
+    feed_send(3)
+    arrive(0)
+    third(2, 1, 0)
+    make_q[0]()
+    finish(1, 3)
+    mid(2, 0, 1)
+    mid(2, 0, 3)
+    finish(1, 2)
+    pre8()
+    third(2, 1, 2)
+    feed_send(0)
+    feed_send(1)
+    make_q[1]()
+    kept.append(cp.local(q, q_o))
+    mid(3, 0, 2)
+    third(2, 1, 3)
+    arrive(1)
+    make_k[0]()
+    make_k[1]()
+    kept.append(cp.local(k, k_o))
+    third(2, 0, 2)
+    third(2, 1, 1)
+    masks()
+    make_v[0]()
+    mid(3, 1, 1)
+    mid(3, 0, 1)
+    third(2, 0, 3)
+    third(2, 0, 1)
+    feed_pass(2)
+    mid(3, 0, 3)
+    make_v[1]()
+    kept.append(cp.local(v, v_o))
+    own_attend(0)()
+    mid(3, 1, 2)
+    finish(2, 2)
+    finish(2, 0)
+    own_attend(1)()
+    mid(3, 1, 3)
     feed_pass(3)
+    own_attend(2)()
+    own_attend(3)()
+    kept.append(cp.local(probs, probs_o))
+    kept.append(cp.local(att, att_o))
+    third(3, 1, 1)
+    finish(2, 3)
+    norm_one[0]()
+    finish(2, 1)
+    third(3, 0, 1)
+    third(3, 0, 0)
+    third(3, 1, 0)
+    norm_one[1]()
+    norm_one[2]()
+    kept.append(cp.local(flow, first_o))
+    kept.append(cp.local(n1, n1_o))
+    kept.append(cp.local(i1, i1_o))
+    feed_pass(0)
+    arrive(2)
+    make_ck[0]()
+    third(3, 0, 2)
+    third(3, 1, 2)
+    make_cq[0]()
+    make_cq[1]()
+    kept.append(cp.local(cq, cq_o))
+    make_ck[1]()
+    kept.append(cp.local(ck, ck_o))
+    third(3, 1, 3)
+    third(3, 0, 3)
+    cross_scores(0)()
+    finish(3, 1)
+    finish(3, 0)
+    cross_scores(1)()
     finish(3, 2)
-    turn(2)
+    cross_scores(2)()
     finish(3, 3)
-    turn(100)
+    cross_scores(3)()
+    kept.append(cp.local(cprobs, cprobs_o))
+    feed_pass(1)
     arrive(3)
-    queue += comp[3]
-    turn(100)
-    for e in kept: e.wait()
-    for e in passed: e.wait_recv()
-    own_ids = None
-    cp.close()
-
-def front(A, r, inputs, memory, seg_row, mem_row, embed, inner, outer, norms, ws, fin, fout):
-    T, D = inputs.shape; M = memory.shape[0]; H = fin.shape[1]
+    make_cv[0]()
+    make_cv[1]()
+    kept.append(cp.local(cv, cv_o))
+    cross_mix(0)()
+    cross_mix(1)()
+    kept.append(cp.local(crossed, crossed_o))
+    norm_two[0]()
+    norm_two[1]()
+    norm_two[2]()
+    kept.append(cp.local(slow, slow_o))
+    kept.append(cp.local(n2, n2_o))
+    kept.append(cp.local(i2, i2_o))
+    def partner():
+        for e in passed: e.wait_recv()
+    def finish():
+        for e in kept: e.wait()
+        cp.close()
+    return (second, vecs, att, flow, crossed), partner, finish
+
+def forward_kernel(A, r, inputs, memory, seg_row, mem_row, embed, inner, outer, norms, cot, *refs):
+    ws, (fin, fout, down, up), outs, scratch = refs[:8], refs[8:12], refs[12:43], refs[43:]
+    fin2, fout2 = scratch[32:34]
+    (second, vecs, att, flow, crossed), partner, finish = front_part(A, r, inputs, memory, seg_row, mem_row, embed, inner, outer, norms, ws, fin, fout, fin2, fout2, outs[:20], scratch[:32])
+    feed_part(A, second, vecs, cot, fin, fout, down, up, inputs, memory, att, flow, crossed, partner, outs[20:], scratch[32:])
+    finish()
+
+def forward(A, r, inputs, memory, seg_row, mem_row, embed, inner, outer, norms, cot, ws, fin, fout, down, up):
+    T, D = inputs.shape; M = memory.shape[0]; H = fin.shape[1]; AD = down.shape[1] * 4
+    HID = 2 * H
     vm = pl.BlockSpec(memory_space=pltpu.VMEM)
     any_ = pl.BlockSpec(memory_space=pl.ANY)
     sds = jax.ShapeDtypeStruct
@@ -1143,17 +1140,22 @@
     row, mrow, full, one = sds((T, D), bf16), sds((M, D), bf16), sds((T, D), f32), sds((T, 1), f32)
     S = (PADDED, inner.shape[1])
     probs, cprobs = (16, T, T + PADDED), (16, T, M)
-    return pl.pallas_call(functools.partial(front_kernel, A, r),
-        out_shape=(sds((8, D, D), bf16), sds((D, H), bf16), sds((H, D), bf16),
-            sds(S, f32), sds((PADDED, 2 * D), bf16), sds((8, D), f32), row, row, row, sds(probs, bf16), row, row, full, one, row, mrow, mrow, sds(cprobs, bf16), row,
-            full, row, full, one),
-        in_specs=[vm] * 8 + [any_] * 10, out_specs=(any_,) * 23,
+    R = T // 2
+    sums = (2, 2, D // 256, R, 256)
+    four = sds((4 * T, D), bf16)
+    sem = pltpu.SemaphoreType.DMA
+    return pl.pallas_call(functools.partial(forward_kernel, A, r),
+        out_shape=(sds((8, D, D), bf16), sds(S, f32), sds((PADDED, 2 * D), bf16), sds((8, D), f32), row, row, row, sds(probs, bf16), row, row, full, one, row, mrow, mrow,
+            sds(cprobs, bf16), row, row, full, one,
+            row, full, sds((D, HID), bf16), sds((HID, D), bf16), sds((2, T, AD), bf16), row, sds((2, D), f32), four, four, four, sds((4 * M, D), bf16)),
+        in_specs=[vm] * 9 + [any_] * 12, out_specs=(any_,) * 20 + (vm,) * 2 + (any_,) * 2 + (vm,) * 3 + (any_,) * 4,
         scratch_shapes=[v(8, D, D), v(T, D), v(T, D), v(T, D), v(*probs), v(T, D), vf(T, D), v(T, D), vf(T, D), vf(T, 1), v(T, D), v(M, D), v(M, D), v(*cprobs), v(T, D),
             vf(T, D), v(T, D), vf(T, D), vf(T, 1), vf(T, T + PADDED), vf(T, M),
-            vf(3, *S), vf(3, *S), vf(A, *S), v(PADDED, 128), v(PADDED, 128), v(PADDED, 2 * D), v(8 * A * norms.shape[0], 128), vf(8, D), vf(*S),
-            pltpu.SemaphoreType.DMA((320,)), pltpu.SemaphoreType.DMA((320,))],
-        compiler_params=pltpu.CompilerParams(collective_id=1, has_side_effects=True, vmem_limit_bytes=60 << 20), name="front")(
-            inputs, memory, seg_row, mem_row, embed, inner, outer, norms, *ws, fin, fout)
+            vf(3, *S), vf(3, *S), vf(A, *S), v(PADDED, 128), v(PADDED, 128), v(PADDED, 2 * D), v(8 * A * norms.shape[0], 128), vf(8, D), vf(*S), sem((320,)), sem((320,)),
+            v(D, HID), v(HID, D), v(D, HID), v(HID, D), v(D, AD), v(AD, D), v(2, 4, R, D), v(2, 4, R, D), v(2, 4, R, HID), vf(2, 4, R, HID), v(2, 4, R, HID), v(2, 4, D // 256, R, 256),
+            v(*sums), v(*sums), v(*sums), vf(T, AD), vf(2, R, D), sem((128,)), sem((128,))],
+        compiler_params=pltpu.CompilerParams(collective_id=1, has_side_effects=True, vmem_limit_bytes=60 << 20), name="forward")(
+            inputs, memory, seg_row, mem_row, embed, inner, outer, norms, cot, *ws, fin, fout, down, up)
 
 
 def exact(l, r, dims):
@@ -1680,11 +1682,10 @@
     w, n = lax.axis_index(WIDE), lax.axis_index(NARROW)
     blank = jnp.zeros_like(self_gain)
     norms = jnp.stack([self_gain, self_shift, cross_gain, cross_shift, final_gain, final_shift] + [blank] * 10)
-    (weights, fin2, fout2, tangent, prows, vecs, q, k, v, probs, attended, first_low, n1, i1, cq, ck, cv, cprobs, crossed, second, second_low, n2, i2) = front(
-        A, r, inputs, memory, segments.reshape(1, -1), memory_segments.reshape(1, -1), prefix_embed, prefix_inner, prefix_outer.T, norms,
-        [query_self, key_self, value_self, output_self, key_cross, query_cross, value_cross, output_cross], feed_in, feed_out)
-    result, grad_second, fi, fo, ay, branch_low, ngrad3, xp0, xatt, xin, xmem = feed(
-        A, second, cotangent, feed_in, feed_out, fin2, fout2, adapter_down, adapter_up, vecs[4:5], vecs[5:6], inputs, memory, attended, first_low, crossed)
+    (weights, tangent, prows, vecs, q, k, v, probs, attended, first_low, n1, i1, cq, ck, cv, cprobs, crossed, second_low, n2, i2,
+     result, grad_second, fi, fo, ay, branch_low, ngrad3, xp0, xatt, xin, xmem) = forward(
+        A, r, inputs, memory, segments.reshape(1, -1), memory_segments.reshape(1, -1), prefix_embed, prefix_inner, prefix_outer.T, norms, cotangent,
+        [query_self, key_self, value_self, output_self, key_cross, query_cross, value_cross, output_cross], feed_in, feed_out, adapter_down, adapter_up)
     igrad, mgrad, sums, adapt, fi_sum, fo_sum, outer_grad, inner_grad, embed_grad, nsum = back(A, r,
         (grad_second, n2, i2, vecs, ngrad3, tangent, prefix_embed, prefix_inner, prefix_outer.T), (cq, ck, cv, cprobs, n1, i1, q, k, v, probs, prows),
         (second_low, branch_low, ay, weights, fi, fo, xp0, xatt, xin, xmem))

time: 285 us -> 274 us (0.961)
  Pallas kernels: 279 us -> 269 us
    pallas_call x1, Pallas kernels: 102 us -> 95.7 us  [back(): pl.pallas_call(functools.partial(back_kernel, A, r), out_shape=(sds((T, D...]
    pallas_call x2 -> x1, Pallas kernels: 173 us -> 170 us  [forward(): pl.pallas_call(functools.partial(forward_kernel, A, r), out_shape=(sds((8...]
where the time goes in v5:
time: 274 us; the launch traced here: 273 us
  Pallas kernels  269 us (98%)
  local copies, waits for them, and re-layouts  3.22 us (1%)
    pallas_call x1, Pallas kernels, forward(): pl.pallas_call(functools.partial(forward_kernel, A, r), out_shape=(sds((8...  170 us
    pallas_call x1, Pallas kernels, back(): pl.pallas_call(functools.partial(back_kernel, A, r), out_shape=(sds((T, D...  95.7 us

profile of v5, /device:TPU:0, one launch (start us, length us, event | category | flops | bytes accessed | tf_op | source)
XLA Modules:
  0.0 273.2 jit_solution(6006342304472609558)
XLA Ops:
  0.7 1.9 stack.35.norms
  2.6 169.8 %forward.1 = (bf16[8,1024,1024]{2,1,0:T(8,128)(2,1)}, f32[32,512]{1,0:T(8,128)}, bf16[32,2048]{1,0:T(8,128)(2,1)}, f32[8,1024]{1,0:T(8,128)}, bf16[128,1024]{1,0...) custom-call(bf16[128,1024]{1,0:T(8,128)(2,1)} %inputs.1, ...), custom_call_target="tpu_custom_call" | custom-call | tf_op jit(solution)/shard_map/forward/pallas_call | solution.py:1147
  172.4 95.7 %back.1 = (bf16[128,1024]{1,0:T(8,128)(2,1)}, bf16[256,1024]{1,0:T(8,128)(2,1)}, f32[8,32,1024]{2,1,0:T(8,128)}, f32[2,128,128]{2,1,0:T(8,128)}, f32[256,512]{1,...) custom-call(f32[128,1024]{1,0:T(8,128)} %get-tuple-element.81.gsec, ...), custom_call_target="tpu_custom_call" | custom-call | tf_op jit(solution)/shard_map/back/pallas_call | solution.py:1662
  268.2 3.7 %deliver.1 = (bf16[128,1024]{1,0:T(8,128)(2,1)}, bf16[128,1024]{1,0:T(8,128)(2,1)}, bf16[256,1024]{1,0:T(8,128)(2,1)}, f32[32,1024]{1,0:T(8,128)}, f32[32,1024]{...) custom-call(bf16[128,1024]{1,0:T(8,128)(2,1)} %get-tuple-element.80., ...), custom_call_target="tpu_custom_call" | custom-call | tf_op jit(solution)/shard_map/deliver/pallas_call | solution.py:1711
  271.9 0.8 constant_dynamic-slice_fusion
  272.7 0.5 slice_bitcast_fusion
  (2 shorter events, 0.0 us)

commit v6 on v5

--- a/solution.py
+++ b/solution.py
@@ -522,11 +522,10 @@
     sums, onward = {}, {}
     def send_part(level, h, j, t):
         sums[level, h, j, t] = cp(part.at[h, j, t], (q3 if j == 3 else q1).at[level, h, t], yp)
-    def collect(level, h):
-        for t in range(NT):
-            sums[level, h, 3, t].wait_recv()
-            part[h, 2, t] = part[h, 2, t] + q3[level, h, t]
-            onward[level, h, t] = cp(part.at[h, 2, t], q2.at[level, h, t], zp)
+    def collect(level, h, t):
+        sums[level, h, 3, t].wait_recv()
+        part[h, 2, t] = part[h, 2, t] + q3[level, h, t]
+        onward[level, h, t] = cp(part.at[h, 2, t], q2.at[level, h, t], zp)
     def gather_up(level, h):
         for t in range(NT):
             cols = pl.ds(t * TW, TW)
@@ -535,7 +534,7 @@
         cp.sent([onward[level, h, t] for t in range(NT)] + [sums[level, h, j, t] for j in (1, 3) for t in range(NT)])
 
     for h in range(2): rows[h, 0] = second[span(h), :].astype(bf16)
-    ways = [spread(rows, h) for h in range(2)]
+    moves = {(0, h): spread(rows, h) for h in range(2)}
     AD = down_ref.shape[1]
     n = x * 2 + c
     nd = pl.ds(pl.multiple_of(n * AD, AD), AD)
@@ -583,8 +582,11 @@
         for e, ref in zip(over, (down.at[:, md], up.at[md])):
             e.wait_recv()
             late.append(cp(ref, ref, core))
+        ready.extend(late[:2])
+    ready = []
+    def adapter_ready():
         near[0].wait_recv(); near[1].wait_recv()
-        for e in late[:2]: e.wait_recv()
+        for e in ready: e.wait_recv()
     def share_on():
         for e, ref in share:
             e.wait_recv()
@@ -625,6 +627,7 @@
             send_part(level, h, 3, t)
             part[h, 2, t] = p[:R].astype(bf16)
     def enter(h, g):
+        moves[0, h][2 * g]()
         xv = both(rows, h, g)
         def tile(t, _):
             cols = pl.ds(pl.multiple_of(t * TW, TW), TW)
@@ -633,10 +636,8 @@
             slope[h, 2 * g:2 * g + 2, :, cols] = s.reshape(2, R, TW)
             return 0
         lax.fori_loop(0, HID // TW, tile, 0)
-        hv = both(hid, h, g)
-        for t in range(NT):
-            put_out(0, h, g, t, dot(hv, fout[:, pl.ds(t * TW, TW)]))
     def leave(h, g):
+        moves[1, h][2 * g]()
         xv = both(brow, h, g)
         def tile(t, _):
             cols = pl.ds(pl.multiple_of(t * TW, TW), TW)
@@ -644,11 +645,10 @@
             gpre[h, 2 * g:2 * g + 2, :, cols] = (slope[h, 2 * g:2 * g + 2, :, cols].reshape(2 * R, TW) * gh).astype(bf16).reshape(2, R, TW)
             return 0
         lax.fori_loop(0, HID // TW, tile, 0)
-        hv = both(gpre, h, g)
-        for t in range(NT):
-            put_out(1, h, g, t, dot_right(hv, fin[pl.ds(t * TW, TW), :]))
+    def out_tile(level, h, g, t):
+        cols = pl.ds(t * TW, TW)
+        put_out(level, h, g, t, dot_right(both(gpre, h, g), fin[cols, :]) if level else dot(both(hid, h, g), fout[:, cols]))
     fac, off = vecs[4:5, :], vecs[5:6, :]
-    back = []
     def turn(h):
         n3, inv3 = norm(second[span(h), :] + acc[h])
         result[span(h), :] = (n3 * fac + off).astype(bf16)
@@ -656,61 +656,100 @@
         gb = norm_back(e, n3, inv3, fac)
         gbl = gb.astype(bf16)
         brow[h, 0] = gbl
-        back.append(spread(brow, h))
+        moves[1, h] = spread(brow, h)
         blow[span(h), :] = gbl
         acc[h] = gb
         gg, gs = jnp.sum(e * n3, axis=0, keepdims=True), jnp.sum(e, axis=0, keepdims=True)
         ngrad[0:1, :] = gg if h == 0 else ngrad[0:1, :] + gg
         ngrad[1:2, :] = gs if h == 0 else ngrad[1:2, :] + gs
-    (beside0, forward0, across0), (beside1, forward1, across1) = ways
+    def wtile(t):
+        cols = pl.ds(t * TW, TW)
+        fi[:, cols] = dot_left(rows[...].reshape(4 * T, D), gpre[:, :, :, cols].reshape(4 * T, TW)).astype(bf16)
+        fo[:, cols] = dot_left(hid[...].reshape(4 * T, HID), brow[:, :, :, cols].reshape(4 * T, TW)).astype(bf16)
     for e in loads: e.wait()
     partner()
-    beside0()
+    enter(1, 0)
+    moves[0, 0][1]()
     enter(0, 0)
-    forward0()
-    across0()
+    moves[0, 1][1]()
     enter(0, 1)
-    forward1()
-    beside1()
-    enter(1, 0)
-    collect(0, 0)
-    across1()
+    out_tile(0, 0, 1, 0)
+    out_tile(0, 0, 1, 1)
+    out_tile(0, 0, 0, 0)
+    out_tile(0, 0, 1, 2)
+    out_tile(0, 0, 0, 1)
+    out_tile(0, 1, 0, 0)
+    out_tile(0, 0, 1, 3)
+    out_tile(0, 0, 0, 2)
+    adapter_weights()
+    collect(0, 0, 0)
+    collect(0, 0, 1)
     enter(1, 1)
-    adapter_weights()
+    collect(0, 0, 2)
+    adapter_ready()
+    out_tile(0, 1, 1, 0)
+    out_tile(0, 1, 1, 1)
+    out_tile(0, 1, 1, 2)
+    collect(0, 0, 3)
+    out_tile(0, 1, 0, 1)
+    out_tile(0, 0, 0, 3)
+    collect(0, 1, 0)
+    out_tile(0, 1, 1, 3)
+    out_tile(0, 1, 0, 2)
+    out_tile(0, 1, 0, 3)
+    collect(0, 1, 1)
     adapter_forward()
-    collect(0, 1)
+    collect(0, 1, 2)
     gather_up(0, 0)
+    collect(0, 1, 3)
     turn(0)
     gather_up(0, 1)
     turn(1)
-    (beside0, forward0, across0), (beside1, forward1, across1) = back
-    beside0()
+    moves[1, 0][1]()
     leave(0, 0)
-    forward0()
+    leave(1, 0)
+    out_tile(1, 0, 0, 0)
+    out_tile(1, 0, 0, 1)
+    moves[1, 1][1]()
+    leave(0, 1)
+    out_tile(1, 0, 1, 0)
+    share_on()
+    out_tile(1, 0, 1, 1)
+    out_tile(1, 0, 1, 2)
+    out_tile(1, 0, 1, 3)
+    out_tile(1, 1, 0, 0)
+    out_tile(1, 1, 0, 1)
+    out_tile(1, 1, 0, 2)
+    collect(1, 0, 0)
+    leave(1, 1)
+    collect(1, 0, 2)
+    out_tile(1, 1, 1, 0)
+    collect(1, 0, 1)
+    out_tile(1, 1, 1, 1)
+    collect(1, 0, 3)
+    out_tile(1, 1, 1, 2)
+    out_tile(1, 1, 1, 3)
+    wtile(0)
+    collect(1, 1, 0)
+    out_tile(1, 0, 0, 2)
+    out_tile(1, 0, 0, 3)
+    collect(1, 1, 1)
+    collect(1, 1, 2)
+    wtile(1)
+    out_tile(1, 1, 0, 3)
+    collect(1, 1, 3)
     adapter_back()
-    across0()
-    leave(0, 1)
-    forward1()
-    beside1()
-    leave(1, 0)
-    collect(1, 0)
-    across1()
-    leave(1, 1)
-    def wtile(t, _):
-        cols = pl.ds(pl.multiple_of(t * TW, TW), TW)
-        fi[:, cols] = dot_left(rows[...].reshape(4 * T, D), gpre[:, :, :, cols].reshape(4 * T, TW)).astype(bf16)
-        fo[:, cols] = dot_left(hid[...].reshape(4 * T, HID), brow[:, :, :, cols].reshape(4 * T, TW)).astype(bf16)
-        return 0
-    lax.fori_loop(0, 1, wtile, 0)
-    collect(1, 1)
-    lax.fori_loop(1, HID // TW, wtile, 0)
+    gather_up(1, 0)
+    gsec[span(0), :] = acc[0]
+    wtile(2)
+    wtile(3)
     kept += [cp.local(fi, fi_out), cp.local(fo, fo_out)]
-    share_on()
-    for h in range(2):
-        gather_up(1, h)
-        gsec[span(h), :] = acc[h]
+    gather_up(1, 1)
+    gsec[span(1), :] = acc[1]
     for e in kept[2:]: e.wait()
-    for e in near[2:] + late[2:]: e.wait_recv()
+    for e in near[2:]: e.wait_recv()
+    for e in late:
+        if not any(e is o for o in ready): e.wait_recv()
     for e in fans: e()
     cp.close()
 
@@ -1169,7 +1208,7 @@
                 igrad_o, mgrad_o, out, aout, fi_out, fo_out, outer_o, inner_o, embed_o, nsum,
                 igrad, mgrad, cq, ck, cv, cprobs, n1, i1, q, k, v, probs, prows, ws, gmid, gfirst, og, mid, dcq, dck, dcv, startl, dq, dk, dv, pg,
                 xb, yb, mb, mby, axb, ayb, pb, apb, fib, fob, r1, r2, r3, sb, xs, ra1, ra2, ra3, rfi, rfo, rzi, rzo, rxi, rxo, ob, aob, fib2, fob2,
-                buf, got, zbuf, nbuf, ngot, nz, w0, w1, w2, w3, s0, s1, s2, ssem, rsem):
+                buf, got, zbuf, nbuf, ngot, nz, w0, w1, w2, w3, s0, s1, s2, nfull, ssem, rsem):
     a, b, x, c = place()
     o = 1 - c
     core, xp, yp = device(a, b, x, o), device(a, b, 1 - x, c), device(a, 1 - b, x, c)
@@ -1424,7 +1463,11 @@
         for e in small["n"]: e.wait_recv()
         t = nz[0]
         for n in range(1, A): t = t + nz[n]
-        nsum[...] = t
+        nfull[...] = t
+        quad = nfull[:, pl.ds(pl.multiple_of((a * 2 + b) * 128, 128), 128)]
+        piece = quad[:, :r]
+        for e in range(1, 4): piece = jnp.where(place_n == e, quad[:, e * r:(e + 1) * r], piece)
+        nsum[...] = piece
     def tail1():
         t = pg[:, lanes(a * 4, 4)]
         for j, e in enumerate(small["w"]):
@@ -1552,93 +1595,93 @@
     cross_back(1)()
     cross_back(2)()
     cross_back(3)()
-    compute(0, 1, 0)
     spread_one(0, dcq, yb.at[0], 1)
+    compute(0, 0, 0)
     feed0()
+    spread(1, (dck, dcv), mby)
+    compute(0, 0, 1)
     wait_slot(1)()
     first_grad()
     fetch(1, 0)
     ready(4, 6)
     norm_one()
-    spread(1, (dck, dcv), mby)
-    compute(0, 1, 1)
-    compute(0, 0, 0)
     wait_slot(2)()
     back_project(startl, 2, 0)()
     back_project(startl, 2, 1)()
     fetch(2, 1)
     ready(6, 11)
     self_back(0)()
+    one(0, 0)()
+    compute(0, 1, 0)
+    self_back(1)()
+    compute(0, 1, 1)
+    self_back(2)()
+    spread_one(2, startl, yb.at[1], 0)
+    self_back(3)()
+    tail0()
+    compute(1, 0)
+    spread_one(2, dq, yb.at[1], 1)
+    compute(1, 1)
+    adapt0()
+    compute(2, 1, 0)
+    one(0, 1)()
+    spread(3, (dk, dv), yb.at[2])
+    tail_norm0()
+    one(1, 0)()
+    compute(2, 1, 1)
+    one(1, 1)()
+    adapt1()
+    tail_norm(1)()
+    tail1()
+    one(2, 1)()
+    compute(3, 0)
     wait_slot(3)()
     wait_slot(0)()
     memory_part(0)()
-    one(0, 1)()
-    compute(0, 0, 1)
-    self_back(1)()
-    compute(1, 0)
-    self_back(2)()
-    tail_norm0()
-    spread_one(2, startl, yb.at[1], 0)
-    one(0, 0)()
-    tail_norm(1)()
-    self_back(3)()
-    compute(1, 1)
-    tail0()
-    spread_one(2, dq, yb.at[1], 1)
-    spread(3, (dk, dv), yb.at[2])
-    compute(2, 0, 0)
-    compute(2, 1, 0)
-    compute(2, 0, 1)
-    one(1, 0)()
-    adapt0()
     compute(3, 1)
-    feed1()
-    one(1, 1)()
-    one(2, 0)()
-    tail1()
-    compute(2, 1, 1)
-    one(3, 1)()
+    adapt2()
     tail2()
-    compute(3, 0)
-    one(2, 1)()
-    adapt1()
-    one(3, 0)()
-    two(0, 1)()
-    tail3()
-    tail4()
-    two(1, 1)()
-    adapt2()
-    tail5(1)()
     two(0, 0)()
-    two(1, 0)()
-    tail5(2)()
-    three(1, 1)()
     memory_part(1)()
     outs.append(cp.local(mgrad, mgrad_o).wait)
     fetch(3, 2)
+    compute(2, 0, 0)
+    tail3()
+    tail4()
+    one(3, 0)()
+    compute(2, 0, 1)
+    tail5(1)()
+    two(1, 1)()
+    one(3, 1)()
+    three(0, 0)()
     wait_slot(1)()
     wait_slot(2)()
     wait_slot(3)()
     input_part(0)()
-    two(3, 1)()
+    three(1, 1)()
+    two(0, 1)()
+    two(2, 1)()
+    tail5(2)()
+    two(1, 0)()
+    feed1()
+    one(2, 0)()
+    three(0, 1)()
+    input_part(1)()
+    outs.append(cp.local(igrad, igrad_o).wait)
+    two(3, 0)()
+    tail_norm(2)()
     three(1, 0)()
     tail6()
-    three(0, 0)()
-    two(3, 0)()
-    tail_norm(2)()
-    three(0, 1)()
+    two(3, 1)()
+    adapt3()
+    tail_norm3()
+    three(2, 1)()
+    two(2, 0)()
     three(3, 1)()
-    input_part(1)()
-    outs.append(cp.local(igrad, igrad_o).wait)
-    adapt3()
+    three(2, 0)()
     three(3, 0)()
-    two(2, 0)()
-    tail_norm3()
+    tail7()
     feed2()
-    two(2, 1)()
-    three(2, 1)()
-    three(2, 0)()
-    tail7()
     tail_norm4()
     for e in ending: e()
     for e in outs: e()
@@ -1661,7 +1704,7 @@
     S = (P_, hid)
     return pl.pallas_call(functools.partial(back_kernel, A, r),
         out_shape=(sds((T, D), bf16), sds((M, D), bf16), sds((8, r, D), f32), sds((2, D // (2 * A), 128), f32), sds((Q, H), f32), sds((H, Q), f32),
-            sds((64, hid), f32), sds((r, hid), f32), sds((PREFIX, r), f32), sds(N, f32)),
+            sds((64, hid), f32), sds((r, hid), f32), sds((PREFIX, r), f32), sds((8, r), f32)),
         in_specs=[vm] * len(first) + [any_] * (len(late) + len(rest)), out_specs=(any_,) * 6 + (vm,) * 4,
         scratch_shapes=[v(T, D), v(M, D)] + [pltpu.VMEM(e.shape, e.dtype) for e in late] + [v(4, D, D), vf(T, D), vf(T, D), v(T, D), v(T, D), v(T, D), v(M, D), v(M, D), v(T, D), v(T, D), v(T, D), v(T, D), vf(P_, 2 * D),
             v(3, 4 * T, D), v(3, 4 * T, half), v(4 * M, D), v(4 * M, half), v(2 * T, D), v(2 * T, 512),
@@ -1670,7 +1713,7 @@
             v(A, 2, D // (2 * A), 256), v(A, D // (2 * A), 256), v(A - 1, D // (2 * A), 256),
             v(2, Q, H2), v(2, H2, Q), v(2, Q, H), v(2, H, Q), v(Q, H), v(H, Q),
             vf(4, 2 * r, D), vf(2, D // (2 * A), 128), vf(Q, H), vf(H, Q),
-            vf(3, *S), vf(3, *S), vf(A, *S), vf(3, *N), vf(3, *N), vf(A, *N), vf(A - 1, P_, 512), vf(P_, 256), vf(P_, 128), vf(P_, 128), vf(P_, 512), vf(P_, 256), vf(P_, 128),
+            vf(3, *S), vf(3, *S), vf(A, *S), vf(3, *N), vf(3, *N), vf(A, *N), vf(A - 1, P_, 512), vf(P_, 256), vf(P_, 128), vf(P_, 128), vf(P_, 512), vf(P_, 256), vf(P_, 128), vf(8, D),
             pltpu.SemaphoreType.DMA((224,)), pltpu.SemaphoreType.DMA((224,))],
         compiler_params=pltpu.CompilerParams(collective_id=2, has_side_effects=True, vmem_limit_bytes=63 << 20),
         name="back")(*first, *late, *rest)
@@ -1679,39 +1722,49 @@
               query_cross, key_cross, value_cross, output_cross, self_gain, self_shift, cross_gain, cross_shift,
               final_gain, final_shift, feed_in, feed_out, adapter_down, adapter_up, prefix_embed, prefix_inner, prefix_outer):
     r = query_self.shape[0]
-    w, n = lax.axis_index(WIDE), lax.axis_index(NARROW)
     blank = jnp.zeros_like(self_gain)
     norms = jnp.stack([self_gain, self_shift, cross_gain, cross_shift, final_gain, final_shift] + [blank] * 10)
     (weights, tangent, prows, vecs, q, k, v, probs, attended, first_low, n1, i1, cq, ck, cv, cprobs, crossed, second_low, n2, i2,
      result, grad_second, fi, fo, ay, branch_low, ngrad3, xp0, xatt, xin, xmem) = forward(
         A, r, inputs, memory, segments.reshape(1, -1), memory_segments.reshape(1, -1), prefix_embed, prefix_inner, prefix_outer.T, norms, cotangent,
         [query_self, key_self, value_self, output_self, key_cross, query_cross, value_cross, output_cross], feed_in, feed_out, adapter_down, adapter_up)
-    igrad, mgrad, sums, adapt, fi_sum, fo_sum, outer_grad, inner_grad, embed_grad, nsum = back(A, r,
+    igrad, mgrad, sums, adapt, fi_sum, fo_sum, outer_grad, inner_grad, embed_grad, ng = back(A, r,
         (grad_second, n2, i2, vecs, ngrad3, tangent, prefix_embed, prefix_inner, prefix_outer.T), (cq, ck, cv, cprobs, n1, i1, q, k, v, probs, prows),
         (second_low, branch_low, ay, weights, fi, fo, xp0, xatt, xin, xmem))
-    ng = lax.dynamic_slice_in_dim(nsum, (w * 4 + n) * r, r, 1)
     whole = deliver(result, igrad, mgrad, sums, fi_sum, fo_sum, outer_grad, inner_grad, embed_grad, adapt)
     return whole[:11] + tuple(ng[k] for k in range(6)) + whole[11:17] + (whole[17].T,)
 
 
-def deliver_kernel(result, igrad, mgrad, sums, fi, fo, outer, inner, embed, adapt, *outs):
+def deliver_kernel(*refs):
+    ins, outs, held, (turned, into, out_of) = refs[:10], refs[10:28], refs[28:38], refs[38:]
+    loads = [pltpu.make_async_copy(src, dst, into.at[i]) for i, (src, dst) in enumerate(zip(ins, held))]
+    for e in loads: e.start()
     order = (5, 6, 7, 4, 1, 2, 3, 0)
-    for dst, src in zip(outs[:3], (result, igrad, mgrad)): dst[...] = src[...]
-    for dst, k in zip(outs[3:11], order): dst[...] = sums[k]
-    for dst, src in zip(outs[11:13] + outs[15:], (fi, fo, embed, inner, outer)): dst[...] = src[...]
-    outs[13][...] = adapt[0]
-    outs[14][...] = adapt[1].T
+    moves = [(3, held[3].at[k], outs[3 + i]) for i, k in enumerate(order)]
+    moves += [(i, held[i], outs[i]) for i in range(3)] + [(4, held[4], outs[11]), (5, held[5], outs[12]), (9, held[9].at[0], outs[13]), (9, turned, outs[14])]
+    moves += [(8, held[8], outs[15]), (7, held[7], outs[16]), (6, held[6], outs[17])]
+    stores, ready = [], set()
+    for n, (i, src, dst) in enumerate(moves):
+        if i not in ready:
+            ready.add(i)
+            loads[i].wait()
+        if src is turned: turned[...] = held[9][1].T
+        stores.append(pltpu.make_async_copy(src, dst, out_of.at[n]))
+        stores[-1].start()
+    for e in stores: e.wait()
 
 
 def deliver(result, igrad, mgrad, sums, fi, fo, outer, inner, embed, adapt):
+    ins = (result, igrad, mgrad, sums, fi, fo, outer, inner, embed, adapt)
     like = lambda e: jax.ShapeDtypeStruct(e.shape, e.dtype)
     row = jax.ShapeDtypeStruct(sums.shape[1:], f32)
     square = jax.ShapeDtypeStruct(adapt.shape[1:], f32)
-    vm = pl.BlockSpec(memory_space=pltpu.VMEM)
+    any_ = pl.BlockSpec(memory_space=pl.ANY)
     return pl.pallas_call(deliver_kernel,
         out_shape=(like(result), like(igrad), like(mgrad)) + (row,) * 8 + (like(fi), like(fo), square, square, like(embed), like(inner), like(outer)),
-        in_specs=[vm] * 10, out_specs=(vm,) * 18, compiler_params=pltpu.CompilerParams(vmem_limit_bytes=60 << 20),
-        name="deliver")(result, igrad, mgrad, sums, fi, fo, outer, inner, embed, adapt)
+        in_specs=[any_] * 10, out_specs=(any_,) * 18,
+        scratch_shapes=[pltpu.VMEM(e.shape, e.dtype) for e in ins] + [pltpu.VMEM(adapt.shape[1:], f32), pltpu.SemaphoreType.DMA((10,)), pltpu.SemaphoreType.DMA((18,))],
+        compiler_params=pltpu.CompilerParams(vmem_limit_bytes=60 << 20), name="deliver")(*ins)
 
 
 def solution(mesh):

time: 274 us -> 264 us (0.964)
  Pallas kernels: 269 us -> 261 us
    pallas_call x1, Pallas kernels: 170 us -> 164 us  [forward(): pl.pallas_call(functools.partial(forward_kernel, A, r), out_shape=(sds((8...]
where the time goes in v6:
time: 264 us
  Pallas kernels  261 us (99%)
    pallas_call x1, Pallas kernels, forward(): pl.pallas_call(functools.partial(forward_kernel, A, r), out_shape=(sds((8...  164 us
    pallas_call x1, Pallas kernels, back(): pl.pallas_call(functools.partial(back_kernel, A, r), out_shape=(sds((T, D...  93.5 us

profile of v6, /device:TPU:0, one launch (start us, length us, event | category | flops | bytes accessed | tf_op | source)
XLA Modules:
  0.0 264.1 jit_solution(9624067049947937726)
XLA Ops:
  0.7 1.9 stack.35.norms
  2.6 163.9 %forward.1 = (bf16[8,1024,1024]{2,1,0:T(8,128)(2,1)}, f32[32,512]{1,0:T(8,128)}, bf16[32,2048]{1,0:T(8,128)(2,1)}, f32[8,1024]{1,0:T(8,128)}, bf16[128,1024]{1,0...) custom-call(bf16[128,1024]{1,0:T(8,128)(2,1)} %inputs.1, ...), custom_call_target="tpu_custom_call" | custom-call | tf_op jit(solution)/shard_map/forward/pallas_call | solution.py:1186
  166.5 93.5 %back.1 = (bf16[128,1024]{1,0:T(8,128)(2,1)}, bf16[256,1024]{1,0:T(8,128)(2,1)}, f32[8,32,1024]{2,1,0:T(8,128)}, f32[2,128,128]{2,1,0:T(8,128)}, f32[256,512]{1,...) custom-call(f32[128,1024]{1,0:T(8,128)} %get-tuple-element.81.gsec, ...), custom_call_target="tpu_custom_call" | custom-call | tf_op jit(solution)/shard_map/back/pallas_call | solution.py:1705
  260.0 0.0 copy-start
  260.0 3.6 %deliver.1 = (bf16[128,1024]{1,0:T(8,128)(2,1)}, bf16[128,1024]{1,0:T(8,128)(2,1)}, bf16[256,1024]{1,0:T(8,128)(2,1)}, f32[32,1024]{1,0:T(8,128)}, f32[32,1024]{...) custom-call(bf16[128,1024]{1,0:T(8,128)(2,1)} %get-tuple-element.80., ...), custom_call_target="tpu_custom_call" | custom-call | tf_op jit(solution)/shard_map/deliver/pallas_call | solution.py:1763
  263.6 0.0 copy-done
  263.6 0.5 slice_bitcast_fusion
  (2 shorter events, 0.0 us)
Async XLA Ops:
  260.0 3.6 %copy-start = (f32[8,32]{1,0:T(8,128)S(1)}, f32[8,32]{1,0:T(8,128)}, u32[]{:S(2)}) copy-start(f32[8,32]{1,0:T(8,128)} %get-tuple-element.128) | copy-start | bytes 3076

commit v7 on v6

--- a/solution.py
+++ b/solution.py
@@ -482,8 +482,8 @@
     s = e * factor
     return inverse * (s - jnp.mean(s, axis=-1, keepdims=True) - n * jnp.mean(s * n, axis=-1, keepdims=True))
 
-def feed_part(A, second, vecs, cot, fin_own, fout_own, down_ref, up_ref, inputs, memory, att, flow, crossed, partner, outs, scratch):
-    result, gsec, fi_out, fo_out, ay, blow, ngrad, xp0, xatt, xin, xmem = outs
+def feed_part(A, second, vecs, cot, fin_own, fout_own, down_ref, up_ref, inputs, memory, att, flow, crossed, slow, partner, outs, scratch):
+    result, gsec, fi_out, fo_out, ay, blow, ngrad, xp0, xatt, xin, xmem, xad = outs
     fin, fout, fi, fo, down, up, rows, brow, hid, slope, gpre, part, q1, q2, q3, bslope, acc, ssem, rsem = scratch
     a, b, x, c = place()
     o = 1 - c
@@ -577,6 +577,7 @@
         kept.append(cp.local(src, rowsn(dst, m, n)))
         near.append(cp(src, rowsn(dst, m, n), core))
         share.append((cp(src, rowsn(dst, m, n), xp), rowsn(dst, m, 2 - 2 * x + c)))
+    fans.append(fan((slow, None), xad))
     def adapter_weights():
         kept[0].wait(); kept[1].wait()
         for e, ref in zip(over, (down.at[:, md], up.at[md])):
@@ -705,6 +706,7 @@
     turn(0)
     gather_up(0, 1)
     turn(1)
+    fans.append(fan((None, blow), xad))
     moves[1, 0][1]()
     leave(0, 0)
     leave(1, 0)
@@ -1159,13 +1161,13 @@
     def finish():
         for e in kept: e.wait()
         cp.close()
-    return (second, vecs, att, flow, crossed), partner, finish
+    return (second, vecs, att, flow, crossed, slow), partner, finish
 
 def forward_kernel(A, r, inputs, memory, seg_row, mem_row, embed, inner, outer, norms, cot, *refs):
-    ws, (fin, fout, down, up), outs, scratch = refs[:8], refs[8:12], refs[12:43], refs[43:]
+    ws, (fin, fout, down, up), outs, scratch = refs[:8], refs[8:12], refs[12:44], refs[44:]
     fin2, fout2 = scratch[32:34]
-    (second, vecs, att, flow, crossed), partner, finish = front_part(A, r, inputs, memory, seg_row, mem_row, embed, inner, outer, norms, ws, fin, fout, fin2, fout2, outs[:20], scratch[:32])
-    feed_part(A, second, vecs, cot, fin, fout, down, up, inputs, memory, att, flow, crossed, partner, outs[20:], scratch[32:])
+    (second, vecs, att, flow, crossed, slow), partner, finish = front_part(A, r, inputs, memory, seg_row, mem_row, embed, inner, outer, norms, ws, fin, fout, fin2, fout2, outs[:20], scratch[:32])
+    feed_part(A, second, vecs, cot, fin, fout, down, up, inputs, memory, att, flow, crossed, slow, partner, outs[20:], scratch[32:])
     finish()
 
 def forward(A, r, inputs, memory, seg_row, mem_row, embed, inner, outer, norms, cot, ws, fin, fout, down, up):
@@ -1186,8 +1188,8 @@
     return pl.pallas_call(functools.partial(forward_kernel, A, r),
         out_shape=(sds((8, D, D), bf16), sds(S, f32), sds((PADDED, 2 * D), bf16), sds((8, D), f32), row, row, row, sds(probs, bf16), row, row, full, one, row, mrow, mrow,
             sds(cprobs, bf16), row, row, full, one,
-            row, full, sds((D, HID), bf16), sds((HID, D), bf16), sds((2, T, AD), bf16), row, sds((2, D), f32), four, four, four, sds((4 * M, D), bf16)),
-        in_specs=[vm] * 9 + [any_] * 12, out_specs=(any_,) * 20 + (vm,) * 2 + (any_,) * 2 + (vm,) * 3 + (any_,) * 4,
+            row, full, sds((D, HID), bf16), sds((HID, D), bf16), sds((2, T, AD), bf16), row, sds((2, D), f32), four, four, four, sds((4 * M, D), bf16), four),
+        in_specs=[vm] * 9 + [any_] * 12, out_specs=(any_,) * 20 + (vm,) * 2 + (any_,) * 2 + (vm,) * 3 + (any_,) * 5,
         scratch_shapes=[v(8, D, D), v(T, D), v(T, D), v(T, D), v(*probs), v(T, D), vf(T, D), v(T, D), vf(T, D), vf(T, 1), v(T, D), v(M, D), v(M, D), v(*cprobs), v(T, D),
             vf(T, D), v(T, D), vf(T, D), vf(T, 1), vf(T, T + PADDED), vf(T, M),
             vf(3, *S), vf(3, *S), vf(A, *S), v(PADDED, 128), v(PADDED, 128), v(PADDED, 2 * D), v(8 * A * norms.shape[0], 128), vf(8, D), vf(*S), sem((320,)), sem((320,)),
@@ -1201,14 +1203,14 @@
     return lax.dot_general(l, r, (dims, ((), ())), precision=lax.Precision.HIGHEST, preferred_element_type=f32)
 
 def back_kernel(A, r, gsec, n2, i2, vecs, ngrad3, tangent, embed, inner, outer, *refs):
-    late, (slow, blow, ay, weights, fi, fo, xp0, xatt, xin, xmem) = refs[:11], refs[11:21]
-    back_body(A, r, gsec, n2, i2, vecs, ngrad3, tangent, embed, inner, outer, late, slow, blow, ay, weights, fi, fo, xp0, xatt, xin, xmem, *refs[21:])
-
-def back_body(A, r, gsec, n2, i2, vecs, ngrad3, tangent, embed, inner, outer, late, slow, blow, ay, weights, fi, fo, xp0, xatt, xin, xmem,
+    late, (ay, weights, fi, fo, xp0, xatt, xin, xmem, xad) = refs[:11], refs[11:20]
+    back_body(A, r, gsec, n2, i2, vecs, ngrad3, tangent, embed, inner, outer, late, ay, weights, fi, fo, xp0, xatt, xin, xmem, xad, *refs[20:])
+
+def back_body(A, r, gsec, n2, i2, vecs, ngrad3, tangent, embed, inner, outer, late, ay, weights, fi, fo, xp0, xatt, xin, xmem, xad,
                 igrad_o, mgrad_o, out, aout, fi_out, fo_out, outer_o, inner_o, embed_o, nsum,
                 igrad, mgrad, cq, ck, cv, cprobs, n1, i1, q, k, v, probs, prows, ws, gmid, gfirst, og, mid, dcq, dck, dcv, startl, dq, dk, dv, pg,
-                xb, yb, mb, mby, axb, ayb, pb, apb, fib, fob, r1, r2, r3, sb, xs, ra1, ra2, ra3, rfi, rfo, rzi, rzo, rxi, rxo, ob, aob, fib2, fob2,
-                buf, got, zbuf, nbuf, ngot, nz, w0, w1, w2, w3, s0, s1, s2, nfull, ssem, rsem):
+                xb, yb, mb, mby, axb, ayb, pb, apb, fib, fob, r1, r2, r3, sb, xs, ra2, ra3, rfi, rfo, rzi, rzo, rxi, rxo, ob, aob, fib2, fob2,
+                buf, got, zbuf, nbuf, ngot, nz, w0, w1, w2, w3, s0, s1, s2, nfull, pgl, ssem, rsem):
     a, b, x, c = place()
     o = 1 - c
     core, xp, yp = device(a, b, x, o), device(a, b, 1 - x, c), device(a, 1 - b, x, c)
@@ -1236,20 +1238,8 @@
         dq_ = pl.ds(pl.multiple_of((xx * 2 + c) * Q, Q), Q)
         fown += [cp.local(fi.at[dq_, :], fib.at[xx]), cp.local(fo.at[:, dq_], fob.at[xx])]
     greet([core, xp, yp, dp] + zp[1:])
-    def offer(srcs, mine, theirs):
-        n = cp.count
-        cp.count += 2
-        def start(keep, give):
-            pltpu.make_async_copy(srcs[keep], mine, ssem.at[n]).start()
-            remote(srcs[give], theirs, ssem.at[n + 1], rsem.at[n], core).start()
-        pl.when(c == 0)(functools.partial(start, 0, 1))
-        pl.when(c == 1)(functools.partial(start, 1, 0))
-        e = remote(srcs[0], theirs, ssem.at[n + 1], rsem.at[n], core)
-        cp.all.append(e)
-        return pltpu.make_async_copy(srcs[0], mine, ssem.at[n]).wait, e.wait_recv
-    lowT, highT = pl.ds(0, T), pl.ds(T, T)
     waits = {}
-    aw = offer((slow, blow), axb.at[lowT], axb.at[highT]) + offer((ay.at[0], ay.at[1]), ayb.at[lowT], ayb.at[highT])
+    aw = [cp.local(xad, axb).wait]
     xload = cp.count
     cp.count += 4
     def load_x(me):
@@ -1263,6 +1253,20 @@
     waits[1] = (pltpu.make_async_copy(xmem, mb, ssem.at[xload + 1]).wait,)
     waits[2] = (pltpu.make_async_copy(xin, xb.at[1], ssem.at[xload + 2]).wait,)
     waits[3] = (pltpu.make_async_copy(xin, xb.at[2], ssem.at[xload + 3]).wait,)
+    def share_adapter():
+        quarter = ayb.shape[1]
+        k = cp.count
+        cp.count += 4
+        here, there = pl.ds(pl.multiple_of(x * quarter, quarter), quarter), pl.ds(pl.multiple_of((1 - x) * quarter, quarter), quarter)
+        spot = ayb.at[pl.ds(pl.multiple_of(place_n * T, T), T)]
+        kept = pltpu.make_async_copy(ay.at[c, :, here], spot, ssem.at[k])
+        ways = [remote(ay.at[c, :, there], spot, ssem.at[k + 1], rsem.at[k + 1], xp), remote(ay.at[o, :, here], spot, ssem.at[k + 2], rsem.at[k + 2], core),
+                remote(ay.at[o, :, there], spot, ssem.at[k + 3], rsem.at[k + 3], dp)]
+        for e in ways: e.start()
+        kept.start()
+        cp.all.extend(ways)
+        aw.extend([kept.wait] + [e.wait_recv for e in ways])
+    share_adapter()
     def share(srcs, dst, t):
         m = srcs[0].shape[0]
         k = cp.count
@@ -1418,26 +1422,20 @@
         return go
     def adapt0():
         for e in aw: e()
-        for t in range(2):
-            apb[t] = dot_left(axb[...], ayb[:, pl.ds(t * 256, 256)]).astype(bf16).reshape(A, 2, D // (2 * A), 256)
-        first["a"] = cp(apb.at[1 - x], ra1, xp)
-    def adapt1():
-        first["a"].wait_recv()
-        def row(z):
-            for s in range(2):
-                apb[x, z, s] = apb[x, z, s] + ra1[z, s]
-        loop(0, A, row)
-        second["a"] = cp(apb.at[x, :, 1 - b], ra2, yp)
+        def rows(u):
+            apb[u] = dot_left(axb[:, columns(u)], ayb[...]).astype(bf16).reshape(2, D // (2 * A), ayb.shape[1])
+        loop(0, A, rows)
+        second["a"] = cp(apb.at[:, 1 - b], ra2, yp)
     def adapt2():
         second["a"].wait_recv()
         for j in range(1, A):
             aj = (a + j) % A
-            apb[x, aj, b] = apb[x, aj, b] + ra2[aj]
-            third["a", j] = cp(apb.at[x, aj, b], ra3.at[j - 1], zp[j])
-        apb[x, a, b] = apb[x, a, b] + ra2[a]
+            apb[aj, b] = apb[aj, b] + ra2[aj]
+            third["a", j] = cp(apb.at[aj, b], ra3.at[j - 1], zp[j])
+        apb[a, b] = apb[a, b] + ra2[a]
     def adapt3():
         for j in range(1, A): third["a", j].wait_recv()
-        t = apb[x, a, b].astype(f32)
+        t = apb[a, b].astype(f32)
         for j in range(1, A): t = t + ra3[j - 1].astype(f32)
         aob[0] = t[:, :128]
         aob[1] = t[:, 128:]
@@ -1448,7 +1446,8 @@
     def tail_norm0():
         small["n"] = [cp(nbuf.at[0], ngot.at[0], core)]
     def tail0():
-        small["w"] = [cp(pg.at[:, lanes((a + j) % A * 4, 4)], w0.at[j - 1], zp[j]) for j in range(1, A)]
+        pgl[...] = pg[...].astype(bf16)
+        small["w"] = [cp(pgl.at[:, lanes((a + j) % A * 4, 4)], w0.at[j - 1], zp[j]) for j in range(1, A)]
     def tail_norm(n):
         def go():
             for e in small["n"]: e.wait_recv()
@@ -1472,7 +1471,7 @@
         t = pg[:, lanes(a * 4, 4)]
         for j, e in enumerate(small["w"]):
             e.wait_recv()
-            t = t + w0[j]
+            t = t + w0[j].astype(f32)
         s0[...] = t
         small["w"] = [cp(s0.at[:, lanes((1 - b) * 2, 2)], w1, yp)]
     def tail2():
@@ -1498,12 +1497,12 @@
         return go
     def tail6():
         small["w"][0].wait_recv()
-        zbuf[a] = buf[2] + got[2]
+        zbuf[a] = (buf[2] + got[2]).astype(bf16)
         small["w"] = [cp(zbuf.at[a], zbuf.at[a], zp[j]) for j in range(1, A)]
     def tail7():
         for e in small["w"]: e.wait_recv()
-        t = zbuf[0]
-        for n in range(1, A): t = t + zbuf[n]
+        t = zbuf[0].astype(f32)
+        for n in range(1, A): t = t + zbuf[n].astype(f32)
         tan = tangent[...]
         t = t * (1.0 - tan * tan)
         inner_o[...] = exact(embed[...].astype(f32), t[:PREFIX], ((0,), (0,)))
@@ -1592,96 +1591,95 @@
     fetch(0, 6)
     ready(0, 4)
     cross_back(0)()
+    feed0()
+    adapt0()
     cross_back(1)()
     cross_back(2)()
     cross_back(3)()
     spread_one(0, dcq, yb.at[0], 1)
-    compute(0, 0, 0)
-    feed0()
-    spread(1, (dck, dcv), mby)
-    compute(0, 0, 1)
     wait_slot(1)()
     first_grad()
     fetch(1, 0)
+    compute(0, 0, 0)
+    spread(1, (dck, dcv), mby)
     ready(4, 6)
     norm_one()
+    compute(0, 0, 1)
+    adapt2()
+    compute(0, 1, 0)
+    compute(0, 1, 1)
     wait_slot(2)()
     back_project(startl, 2, 0)()
+    spread_one(2, startl, yb.at[1], 0)
     back_project(startl, 2, 1)()
     fetch(2, 1)
     ready(6, 11)
     self_back(0)()
     one(0, 0)()
-    compute(0, 1, 0)
+    compute(1, 0)
     self_back(1)()
-    compute(0, 1, 1)
     self_back(2)()
-    spread_one(2, startl, yb.at[1], 0)
     self_back(3)()
+    tail_norm0()
     tail0()
-    compute(1, 0)
+    spread(3, (dk, dv), yb.at[2])
+    one(0, 1)()
+    compute(1, 1)
+    one(1, 0)()
+    compute(2, 1, 0)
     spread_one(2, dq, yb.at[1], 1)
-    compute(1, 1)
-    adapt0()
-    compute(2, 1, 0)
-    one(0, 1)()
-    spread(3, (dk, dv), yb.at[2])
-    tail_norm0()
-    one(1, 0)()
-    compute(2, 1, 1)
-    one(1, 1)()
-    adapt1()
-    tail_norm(1)()
-    tail1()
-    one(2, 1)()
-    compute(3, 0)
+    feed1()
     wait_slot(3)()
     wait_slot(0)()
     memory_part(0)()
     compute(3, 1)
-    adapt2()
-    tail2()
-    two(0, 0)()
+    tail_norm(1)()
+    one(1, 1)()
+    tail1()
+    compute(2, 1, 1)
     memory_part(1)()
     outs.append(cp.local(mgrad, mgrad_o).wait)
     fetch(3, 2)
-    compute(2, 0, 0)
-    tail3()
-    tail4()
-    one(3, 0)()
-    compute(2, 0, 1)
-    tail5(1)()
-    two(1, 1)()
     one(3, 1)()
-    three(0, 0)()
+    compute(3, 0)
     wait_slot(1)()
     wait_slot(2)()
     wait_slot(3)()
     input_part(0)()
+    tail2()
+    compute(2, 0, 0)
+    one(2, 1)()
+    two(0, 0)()
+    adapt3()
+    tail3()
+    feed2()
+    tail4()
+    two(0, 1)()
+    tail5(1)()
+    one(3, 0)()
+    compute(2, 0, 1)
+    two(1, 0)()
+    one(2, 0)()
+    tail_norm(2)()
+    three(0, 1)()
+    two(1, 1)()
+    two(2, 1)()
+    three(0, 0)()
+    tail5(2)()
     three(1, 1)()
-    two(0, 1)()
-    two(2, 1)()
-    tail5(2)()
-    two(1, 0)()
-    feed1()
-    one(2, 0)()
-    three(0, 1)()
+    two(3, 0)()
+    tail6()
+    tail_norm3()
+    three(2, 1)()
+    two(3, 1)()
+    two(2, 0)()
+    three(3, 0)()
     input_part(1)()
     outs.append(cp.local(igrad, igrad_o).wait)
-    two(3, 0)()
-    tail_norm(2)()
     three(1, 0)()
-    tail6()
-    two(3, 1)()
-    adapt3()
-    tail_norm3()
-    three(2, 1)()
-    two(2, 0)()
+    three(2, 0)()
     three(3, 1)()
-    three(2, 0)()
-    three(3, 0)()
     tail7()
-    feed2()
     tail_norm4()
     for e in ending: e()
     for e in outs: e()
@@ -1689,8 +1687,8 @@
 
 def back(A, r, first, late, rest):
     gsec = first[0]
-    T, D = gsec.shape; M = rest[-1].shape[0] // 4
-    fi, fo = rest[4:6]
+    T, D = gsec.shape; M = rest[7].shape[0] // 4
+    fi, fo = rest[2:4]
     Q, H2 = fi.shape[0] // 4, fi.shape[1]
     H = H2 // 2
     half = D // 2
@@ -1707,13 +1705,13 @@
             sds((64, hid), f32), sds((r, hid), f32), sds((PREFIX, r), f32), sds((8, r), f32)),
         in_specs=[vm] * len(first) + [any_] * (len(late) + len(rest)), out_specs=(any_,) * 6 + (vm,) * 4,
         scratch_shapes=[v(T, D), v(M, D)] + [pltpu.VMEM(e.shape, e.dtype) for e in late] + [v(4, D, D), vf(T, D), vf(T, D), v(T, D), v(T, D), v(T, D), v(M, D), v(M, D), v(T, D), v(T, D), v(T, D), v(T, D), vf(P_, 2 * D),
-            v(3, 4 * T, D), v(3, 4 * T, half), v(4 * M, D), v(4 * M, half), v(2 * T, D), v(2 * T, 512),
-            v(4, 2, A, 2, 2, 2 * r, half // 2), v(2, A, 2, D // (2 * A), 256), v(2, Q, H2), v(2, H2, Q),
+            v(3, 4 * T, D), v(3, 4 * T, half), v(4 * M, D), v(4 * M, half), v(4 * T, D), v(4 * T, 256),
+            v(4, 2, A, 2, 2, 2 * r, half // 2), v(A, 2, D // (2 * A), 256), v(2, Q, H2), v(2, H2, Q),
             v(4, 2, A, 2, 2 * r, half // 2), v(4, 2, A - 1, 2, 2 * r, half // 2), v(4, 2, 2 * r, half // 2), vf(4, 2, 2, 2 * r, half // 2), v(4, 2, 2 * r, half // 2),
-            v(A, 2, D // (2 * A), 256), v(A, D // (2 * A), 256), v(A - 1, D // (2 * A), 256),
+            v(A, D // (2 * A), 256), v(A - 1, D // (2 * A), 256),
             v(2, Q, H2), v(2, H2, Q), v(2, Q, H), v(2, H, Q), v(Q, H), v(H, Q),
             vf(4, 2 * r, D), vf(2, D // (2 * A), 128), vf(Q, H), vf(H, Q),
-            vf(3, *S), vf(3, *S), vf(A, *S), vf(3, *N), vf(3, *N), vf(A, *N), vf(A - 1, P_, 512), vf(P_, 256), vf(P_, 128), vf(P_, 128), vf(P_, 512), vf(P_, 256), vf(P_, 128), vf(8, D),
+            vf(3, *S), vf(3, *S), v(A, *S), vf(3, *N), vf(3, *N), vf(A, *N), v(A - 1, P_, 512), vf(P_, 256), vf(P_, 128), vf(P_, 128), vf(P_, 512), vf(P_, 256), vf(P_, 128), vf(8, D), v(P_, 2 * D),
             pltpu.SemaphoreType.DMA((224,)), pltpu.SemaphoreType.DMA((224,))],
         compiler_params=pltpu.CompilerParams(collective_id=2, has_side_effects=True, vmem_limit_bytes=63 << 20),
         name="back")(*first, *late, *rest)
@@ -1725,12 +1723,12 @@
     blank = jnp.zeros_like(self_gain)
     norms = jnp.stack([self_gain, self_shift, cross_gain, cross_shift, final_gain, final_shift] + [blank] * 10)
     (weights, tangent, prows, vecs, q, k, v, probs, attended, first_low, n1, i1, cq, ck, cv, cprobs, crossed, second_low, n2, i2,
-     result, grad_second, fi, fo, ay, branch_low, ngrad3, xp0, xatt, xin, xmem) = forward(
+     result, grad_second, fi, fo, ay, branch_low, ngrad3, xp0, xatt, xin, xmem, xad) = forward(
         A, r, inputs, memory, segments.reshape(1, -1), memory_segments.reshape(1, -1), prefix_embed, prefix_inner, prefix_outer.T, norms, cotangent,
         [query_self, key_self, value_self, output_self, key_cross, query_cross, value_cross, output_cross], feed_in, feed_out, adapter_down, adapter_up)
     igrad, mgrad, sums, adapt, fi_sum, fo_sum, outer_grad, inner_grad, embed_grad, ng = back(A, r,
         (grad_second, n2, i2, vecs, ngrad3, tangent, prefix_embed, prefix_inner, prefix_outer.T), (cq, ck, cv, cprobs, n1, i1, q, k, v, probs, prows),
-        (second_low, branch_low, ay, weights, fi, fo, xp0, xatt, xin, xmem))
+        (ay, weights, fi, fo, xp0, xatt, xin, xmem, xad))
     whole = deliver(result, igrad, mgrad, sums, fi_sum, fo_sum, outer_grad, inner_grad, embed_grad, adapt)
     return whole[:11] + tuple(ng[k] for k in range(6)) + whole[11:17] + (whole[17].T,)
 

time: 264 us -> 258 us (0.977)
  Pallas kernels: 261 us -> 254 us
    pallas_call x1, Pallas kernels: 93.5 us -> 86.6 us  [back(): pl.pallas_call(functools.partial(back_kernel, A, r), out_shape=(sds((T, D...]
where the time goes in v7:
time: 258 us
  Pallas kernels  254 us (98%)
    pallas_call x1, Pallas kernels, forward(): pl.pallas_call(functools.partial(forward_kernel, A, r), out_shape=(sds((8...  164 us
    pallas_call x1, Pallas kernels, back(): pl.pallas_call(functools.partial(back_kernel, A, r), out_shape=(sds((T, D...  86.6 us

profile of v7, /device:TPU:0, one launch (start us, length us, event | category | flops | bytes accessed | tf_op | source)
XLA Modules:
  0.0 257.5 jit_solution(3078067618234974940)
XLA Ops:
  0.7 1.9 stack.35.norms
  2.6 164.1 %forward.1 = (bf16[8,1024,1024]{2,1,0:T(8,128)(2,1)}, f32[32,512]{1,0:T(8,128)}, bf16[32,2048]{1,0:T(8,128)(2,1)}, f32[8,1024]{1,0:T(8,128)}, bf16[128,1024]{1,0...) custom-call(bf16[128,1024]{1,0:T(8,128)(2,1)} %inputs.1, ...), custom_call_target="tpu_custom_call" | custom-call | tf_op jit(solution)/shard_map/forward/pallas_call | solution.py:1188
  166.7 86.6 %back.1 = (bf16[128,1024]{1,0:T(8,128)(2,1)}, bf16[256,1024]{1,0:T(8,128)(2,1)}, f32[8,32,1024]{2,1,0:T(8,128)}, f32[2,128,128]{2,1,0:T(8,128)}, f32[256,512]{1,...) custom-call(f32[128,1024]{1,0:T(8,128)} %get-tuple-element.80.gsec, ...), custom_call_target="tpu_custom_call" | custom-call | tf_op jit(solution)/shard_map/back/pallas_call | solution.py:1703
  253.4 0.0 copy-start
  253.4 3.6 %deliver.1 = (bf16[128,1024]{1,0:T(8,128)(2,1)}, bf16[128,1024]{1,0:T(8,128)(2,1)}, bf16[256,1024]{1,0:T(8,128)(2,1)}, f32[32,1024]{1,0:T(8,128)}, f32[32,1024]{...) custom-call(bf16[128,1024]{1,0:T(8,128)(2,1)} %get-tuple-element.79., ...), custom_call_target="tpu_custom_call" | custom-call | tf_op jit(solution)/shard_map/deliver/pallas_call | solution.py:1761
  257.0 0.0 copy-done
  257.0 0.5 slice_bitcast_fusion
  (2 shorter events, 0.0 us)
Async XLA Ops:
  253.4 3.6 %copy-start = (f32[8,32]{1,0:T(8,128)S(1)}, f32[8,32]{1,0:T(8,128)}, u32[]{:S(2)}) copy-start(f32[8,32]{1,0:T(8,128)} %get-tuple-element.126) | copy-start | bytes 3076

commit v8 on v7

--- a/solution.py
+++ b/solution.py
@@ -1005,144 +1005,144 @@
     norm_one, norm_two = normed(inputs, att, 3, 0, first, n1, i1, flow), normed(first, crossed, 7, 2, second, n2, i2, slow)
     fs(0, 0)
     fs(0, 1)
+    fs(1, 1)
+    fs(3, 0)
+    fs(1, 0)
+    fz(1, 1)
     fz(0, 0)
-    fs(1, 1)
-    fs(1, 0)
+    fs(2, 0)
+    pre1()
+    third(3, 0, 0)
+    pre2(1)()
+    mid(1, 1, 1)
+    fs(2, 1)
+    mid(1, 1, 2)
+    fz(1, 0)
+    third(0, 1, 0)
+    pre2(2)()
+    feed_send(0)
+    mid(1, 1, 3)
+    third(0, 0, 0)
+    third(1, 1, 1)
+    fs(3, 1)
+    pre4()
+    mid(0, 0, 2)
+    mid(0, 0, 1)
     fz(0, 1)
-    fs(3, 0)
-    fs(2, 0)
-    fz(1, 0)
-    fs(2, 1)
-    third(0, 1, 0)
+    mid(1, 0, 2)
+    mid(1, 0, 3)
+    pre5()
+    mid(1, 0, 1)
+    mid(0, 0, 3)
+    third(1, 0, 0)
+    third(1, 0, 2)
+    mid(0, 1, 1)
+    fz(2, 0)
+    mid(0, 1, 3)
+    mid(0, 1, 2)
+    third(0, 0, 3)
+    feed_send(2)
     third(1, 1, 0)
-    pre1()
-    fs(3, 1)
-    pre2(1)()
-    mid(0, 0, 3)
-    mid(0, 1, 1)
-    third(0, 0, 0)
-    mid(0, 0, 2)
-    pre2(2)()
-    fz(1, 1)
-    mid(0, 1, 3)
-    mid(0, 0, 1)
-    mid(1, 0, 2)
+    pre6()
+    third(1, 1, 2)
+    third(0, 0, 1)
+    third(0, 0, 2)
+    fz(2, 1)
+    third(0, 1, 1)
+    mid(2, 0, 3)
+    fz(3, 1)
+    third(0, 1, 3)
+    mid(2, 0, 2)
+    finish(0, 1)
+    pre7()
+    third(0, 1, 2)
     finish(0, 0)
-    third(0, 0, 2)
-    mid(1, 0, 1)
-    fz(2, 0)
-    pre4()
-    pre5()
-    third(0, 0, 1)
-    mid(1, 1, 1)
-    mid(0, 1, 2)
-    feed_send(2)
-    third(1, 0, 0)
-    mid(1, 1, 2)
-    third(0, 1, 1)
-    mid(1, 1, 3)
-    third(0, 1, 2)
-    pre6()
-    fz(2, 1)
-    third(0, 1, 3)
+    third(1, 1, 3)
+    mid(2, 0, 1)
+    third(1, 0, 3)
+    mid(2, 1, 2)
+    third(1, 0, 1)
+    third(3, 1, 0)
+    finish(1, 2)
+    feed_pass(0)
+    mid(2, 1, 3)
+    mid(2, 1, 1)
+    finish(0, 3)
+    finish(0, 2)
+    finish(1, 3)
+    fz(3, 0)
     third(2, 0, 0)
-    third(0, 0, 3)
-    mid(1, 0, 3)
-    mid(2, 1, 1)
-    finish(0, 2)
-    pre7()
-    finish(0, 1)
-    fz(3, 0)
-    third(1, 0, 1)
-    third(1, 1, 2)
-    third(1, 0, 2)
-    mid(2, 1, 2)
-    third(1, 0, 3)
-    mid(2, 0, 2)
-    fz(3, 1)
-    third(1, 1, 1)
-    third(1, 1, 3)
-    mid(2, 1, 3)
-    finish(0, 3)
-    finish(1, 0)
-    finish(1, 1)
+    mid(3, 1, 1)
+    third(2, 1, 0)
+    arrive(0)
+    third(2, 0, 2)
+    feed_send(1)
+    third(2, 0, 1)
+    make_q[0]()
     feed_send(3)
-    arrive(0)
-    third(2, 1, 0)
-    make_q[0]()
-    finish(1, 3)
-    mid(2, 0, 1)
-    mid(2, 0, 3)
-    finish(1, 2)
-    pre8()
-    third(2, 1, 2)
-    feed_send(0)
-    feed_send(1)
     make_q[1]()
     kept.append(cp.local(q, q_o))
-    mid(3, 0, 2)
-    third(2, 1, 3)
-    arrive(1)
+    finish(1, 1)
     make_k[0]()
+    finish(1, 0)
+    pre8()
     make_k[1]()
     kept.append(cp.local(k, k_o))
-    third(2, 0, 2)
-    third(2, 1, 1)
+    third(2, 1, 2)
+    mid(3, 0, 1)
     masks()
+    arrive(1)
+    third(2, 1, 3)
     make_v[0]()
-    mid(3, 1, 1)
-    mid(3, 0, 1)
-    third(2, 0, 3)
-    third(2, 0, 1)
-    feed_pass(2)
-    mid(3, 0, 3)
     make_v[1]()
     kept.append(cp.local(v, v_o))
+    third(2, 1, 1)
+    third(2, 0, 3)
     own_attend(0)()
-    mid(3, 1, 2)
-    finish(2, 2)
+    feed_pass(2)
     finish(2, 0)
     own_attend(1)()
+    finish(2, 2)
+    mid(3, 0, 2)
     mid(3, 1, 3)
-    feed_pass(3)
     own_attend(2)()
     own_attend(3)()
     kept.append(cp.local(probs, probs_o))
     kept.append(cp.local(att, att_o))
+    mid(3, 1, 2)
+    feed_pass(1)
+    finish(2, 3)
+    mid(3, 0, 3)
+    finish(2, 1)
+    norm_one[0]()
     third(3, 1, 1)
-    finish(2, 3)
-    norm_one[0]()
-    finish(2, 1)
-    third(3, 0, 1)
-    third(3, 0, 0)
-    third(3, 1, 0)
     norm_one[1]()
     norm_one[2]()
     kept.append(cp.local(flow, first_o))
     kept.append(cp.local(n1, n1_o))
     kept.append(cp.local(i1, i1_o))
-    feed_pass(0)
+    third(3, 0, 1)
+    finish(3, 0)
+    third(3, 0, 2)
     arrive(2)
     make_ck[0]()
-    third(3, 0, 2)
     third(3, 1, 2)
     make_cq[0]()
+    feed_pass(3)
     make_cq[1]()
     kept.append(cp.local(cq, cq_o))
+    third(3, 0, 3)
+    third(3, 1, 3)
     make_ck[1]()
     kept.append(cp.local(ck, ck_o))
-    third(3, 1, 3)
-    third(3, 0, 3)
+    finish(3, 1)
     cross_scores(0)()
-    finish(3, 1)
-    finish(3, 0)
+    finish(3, 2)
     cross_scores(1)()
-    finish(3, 2)
+    finish(3, 3)
     cross_scores(2)()
-    finish(3, 3)
     cross_scores(3)()
     kept.append(cp.local(cprobs, cprobs_o))
-    feed_pass(1)
     arrive(3)
     make_cv[0]()
     make_cv[1]()

time: 258 us -> 255 us (0.988)
    pallas_call x1, Pallas kernels: 164 us -> 161 us  [forward(): pl.pallas_call(functools.partial(forward_kernel, A, r), out_shape=(sds((8...]
where the time goes in v8:
time: 255 us
  Pallas kernels  252 us (99%)
    pallas_call x1, Pallas kernels, forward(): pl.pallas_call(functools.partial(forward_kernel, A, r), out_shape=(sds((8...  161 us
    pallas_call x1, Pallas kernels, back(): pl.pallas_call(functools.partial(back_kernel, A, r), out_shape=(sds((T, D...  86.9 us

profile of v8, /device:TPU:0, one launch (start us, length us, event | category | flops | bytes accessed | tf_op | source)
XLA Modules:
  0.0 255.1 jit_solution(17894916282786783299)
XLA Ops:
  0.7 1.9 stack.35.norms
  2.6 161.5 %forward.1 = (bf16[8,1024,1024]{2,1,0:T(8,128)(2,1)}, f32[32,512]{1,0:T(8,128)}, bf16[32,2048]{1,0:T(8,128)(2,1)}, f32[8,1024]{1,0:T(8,128)}, bf16[128,1024]{1,0...) custom-call(bf16[128,1024]{1,0:T(8,128)(2,1)} %inputs.1, ...), custom_call_target="tpu_custom_call" | custom-call | tf_op jit(solution)/shard_map/forward/pallas_call | solution.py:1188
  164.1 86.9 %back.1 = (bf16[128,1024]{1,0:T(8,128)(2,1)}, bf16[256,1024]{1,0:T(8,128)(2,1)}, f32[8,32,1024]{2,1,0:T(8,128)}, f32[2,128,128]{2,1,0:T(8,128)}, f32[256,512]{1,...) custom-call(f32[128,1024]{1,0:T(8,128)} %get-tuple-element.80.gsec, ...), custom_call_target="tpu_custom_call" | custom-call | tf_op jit(solution)/shard_map/back/pallas_call | solution.py:1703
  251.0 0.0 copy-start
  251.0 3.6 %deliver.1 = (bf16[128,1024]{1,0:T(8,128)(2,1)}, bf16[128,1024]{1,0:T(8,128)(2,1)}, bf16[256,1024]{1,0:T(8,128)(2,1)}, f32[32,1024]{1,0:T(8,128)}, f32[32,1024]{...) custom-call(bf16[128,1024]{1,0:T(8,128)(2,1)} %get-tuple-element.79., ...), custom_call_target="tpu_custom_call" | custom-call | tf_op jit(solution)/shard_map/deliver/pallas_call | solution.py:1761
  254.5 0.0 copy-done
  254.6 0.5 slice_bitcast_fusion
  (2 shorter events, 0.0 us)
Async XLA Ops:
  251.0 3.6 %copy-start = (f32[8,32]{1,0:T(8,128)S(1)}, f32[8,32]{1,0:T(8,128)}, u32[]{:S(2)}) copy-start(f32[8,32]{1,0:T(8,128)} %get-tuple-element.126) | copy-start | bytes 3076
